TPU v7x, 32 devices: a whole 2x2x4 slice. The times are simulated.
32 devices in a mesh: lat: 2 (over x), lon: 16 (over z, y, core).
Axes of the slice: x: 2, y: 2, z: 4, core: 2. Of those that a mesh axis runs over, the one named last changes fastest.
Arguments:
- fields: bfloat16 [16, 512, 768], P('lat', 'lon'), may hold values from -60 to 60
- conv_kernel: float32 [3, 3, 768], replicated, may hold values from -1 to 1
- layer_norm_gain: float32 [768], replicated, may hold values from 0.1 to 1.9
- qkv_weight: bfloat16 [768, 2304], replicated, may hold values from -0.21875 to 0.21875
- out_weight: bfloat16 [768, 768], replicated, may hold values from -0.21875 to 0.21875
- score_bias: float32 [24, 64, 64], replicated, may hold values from -4 to 400
- pattern: int32 [2, 16, 256], P('lat', 'lon'), may hold values from 0 to 255, each once within a row
- cotangent: bfloat16 [16, 512, 768], P('lat', 'lon'), may hold values from -6 to 6
Outputs:
- block_out: bfloat16 [16, 512, 768], P('lat', 'lon')
- grad_fields: bfloat16 [16, 512, 768], P('lat', 'lon')
- grad_project: float32 [768, 768], P('lat', 'lon')
- grad_kernel: float32 [3, 3, 768], replicated
- gain_gradient: float32 [768], replicated
Inputs may be any that keep to these rules, and one draw needn't show every extreme that they name: pattern[a, b, :] lists each of the 256 cells of block (a, b) once.
All inputs are finite; a program needn't handle non-finite values.
Results may differ from a plain program's by a relative error of at most 0.028.
Values may be sent and summed in bfloat16 or wider, within the bound.
No kernel may reach another device: no remote copies, remote signals or barrier semaphores. Data moves between devices by JAX's collectives and lax.ppermute only.
A program may use at most 128 MiB of HBM per device.

v0:
```python
import math

import jax
import jax.numpy as jnp
from jax import lax
from jax.sharding import PartitionSpec as P

HEADS = 24
HEAD_DIM = 32
GROUP = 64


epsilon = 1e-05


def extended(array, sides, width, wrap):
    for axis, dim in sides:
        peers, length = (lax.axis_size(axis), array.shape[dim])
        up = [(i, (i + 1) % peers) for i in range(peers if wrap else peers - 1)]
        down = [(j, i) for i, j in up]
        last = lax.slice_in_dim(array, length - width, length, axis=dim)
        first = lax.slice_in_dim(array, 0, width, axis=dim)
        before = lax.ppermute(last, axis, up)
        after = lax.ppermute(first, axis, down)
        array = jnp.concatenate([before, array, after], axis=dim)
    return array


def widened(field):
    beside_all = extended(field, (("lon", 1),), 1, True)
    return extended(beside_all, (("lat", 0),), 1, False)


def apply_taps(padded, conv_kernel, lat_rows, lon_cols):
    summed = jnp.zeros((lat_rows, lon_cols, padded.shape[2]), jnp.float32)
    for lat_tap in range(3):
        for lon_tap in range(3):
            summed = (
                summed
                + conv_kernel[lat_tap, lon_tap]
                * padded[lat_tap : lat_tap + lat_rows, lon_tap : lon_tap + lon_cols]
            )
    return summed


def to_owner(packed):
    arrived = lax.all_to_all(
        lax.all_to_all(packed, "lat", split_axis=0, concat_axis=3, tiled=True),
        "lon",
        split_axis=1,
        concat_axis=4,
        tiled=True,
    )
    return arrived.reshape(-1, arrived.shape[-1])


def to_grid(packed):
    arrived = lax.all_to_all(
        lax.all_to_all(packed, "lat", split_axis=3, concat_axis=0, tiled=True),
        "lon",
        split_axis=4,
        concat_axis=1,
        tiled=True,
    )
    return arrived.reshape(-1, arrived.shape[-1])


def attention_probs(queries, key_rows, score_bias):
    scores = jnp.einsum("gihd,gjhd->ghij", queries, key_rows, preferred_element_type=jnp.float32)
    scores = scores * queries.shape[-1] ** (-0.5) + score_bias[None]
    peak = jnp.max(scores, axis=-1, keepdims=True)
    lifted = jnp.exp(scores - peak)
    return lifted / jnp.sum(lifted, axis=-1, keepdims=True)


def body(
    fields, conv_kernel, layer_norm_gain, qkv_weight, out_weight, score_bias, pattern, cotangent
):
    lat_rows, lon_cols, feature_count = fields.shape
    cell_count = lat_rows * lon_cols
    lat_count = lax.axis_size("lat")
    lon_count = lax.axis_size("lon")
    slot_count = cell_count // (lat_count * lon_count)
    scale_everywhere = 1.0 / math.sqrt(cell_count * lat_count * lon_count)
    head_scale = HEAD_DIM ** (-0.5)
    group_count = cell_count // GROUP
    slot_order = pattern.reshape(cell_count)
    inverse = (
        jnp.zeros((cell_count,), jnp.int32)
        .at[slot_order]
        .set(jnp.arange(cell_count, dtype=jnp.int32))
    )

    def outward(field):
        picked = jnp.take(field.reshape(cell_count, feature_count), slot_order, axis=0)
        return picked.reshape(lat_count, lon_count, slot_count, 1, 1, feature_count)

    def inward(grouped):
        return grouped.reshape(1, 1, slot_count, lat_count, lon_count, grouped.shape[-1])

    def homeward(flat):
        return jnp.take(flat, inverse, axis=0).reshape(lat_rows, lon_cols, feature_count)

    padded_fields = widened(fields)
    state_h = (
        fields.astype(jnp.float32) + apply_taps(padded_fields, conv_kernel, lat_rows, lon_cols)
    ).astype(jnp.bfloat16)
    state_f = state_h.astype(jnp.float32)
    mean_h = jnp.mean(state_f, axis=-1, keepdims=True)
    mean_removed = state_f - mean_h
    var_h = jnp.mean(mean_removed * mean_removed, axis=-1, keepdims=True)
    inverse_deviation = lax.rsqrt(var_h + epsilon)
    standardized_input = mean_removed * inverse_deviation
    normalized_fields = (standardized_input * layer_norm_gain).astype(jnp.bfloat16)
    normed_g = to_owner(outward(normalized_fields))
    cot_g = to_owner(outward(cotangent))
    qkv_rows = jnp.dot(normed_g, qkv_weight, preferred_element_type=jnp.float32).astype(
        jnp.bfloat16
    )
    split_rows = qkv_rows.reshape(group_count, GROUP, 3, HEADS, HEAD_DIM)
    queries = split_rows[:, :, 0]
    key_rows = split_rows[:, :, 1]
    value_rows = split_rows[:, :, 2]
    probs = attention_probs(queries, key_rows, score_bias)
    probs_low = probs.astype(jnp.bfloat16)
    attended = jnp.einsum(
        "ghij,gjhd->gihd", probs_low, value_rows, preferred_element_type=jnp.float32
    )
    attended = attended.astype(jnp.bfloat16).reshape(cell_count, feature_count)
    mixed = jnp.dot(attended, out_weight, preferred_element_type=jnp.float32).astype(jnp.bfloat16)
    mixed_flat = to_grid(inward(mixed))
    rows_summed = lax.psum_scatter(
        lax.dot_general(
            attended, cot_g, (((0,), (0,)), ((), ())), preferred_element_type=jnp.float32
        ).astype(jnp.bfloat16),
        "lat",
        scatter_dimension=0,
        tiled=True,
    )
    grad_project = (
        lax.psum_scatter(rows_summed, "lon", scatter_dimension=1, tiled=True).astype(jnp.float32)
        * scale_everywhere
    )
    grad_att = lax.dot_general(
        cot_g, out_weight, (((1,), (1,)), ((), ())), preferred_element_type=jnp.float32
    ).astype(jnp.bfloat16)
    grad_heads = grad_att.reshape(group_count, GROUP, HEADS, HEAD_DIM)
    held_query, held_key = (queries, key_rows)
    grad_probs = jnp.einsum(
        "gihd,gjhd->ghij", grad_heads, value_rows, preferred_element_type=jnp.float32
    )
    grad_scores = probs * (grad_probs - jnp.sum(probs * grad_probs, axis=-1, keepdims=True))
    grad_scores = grad_scores.astype(jnp.bfloat16)
    grad_query = (
        jnp.einsum("ghij,gjhd->gihd", grad_scores, held_key, preferred_element_type=jnp.float32)
        * head_scale
    )
    grad_key = (
        jnp.einsum("ghij,gihd->gjhd", grad_scores, held_query, preferred_element_type=jnp.float32)
        * head_scale
    )
    grad_value = jnp.einsum(
        "ghij,gihd->gjhd", probs_low, grad_heads, preferred_element_type=jnp.float32
    )
    grad_qkv = jnp.stack([grad_query, grad_key, grad_value], axis=2).astype(jnp.bfloat16)
    grad_qkv = grad_qkv.reshape(cell_count, 3 * feature_count)
    grad_grouped = lax.dot_general(
        grad_qkv, qkv_weight, (((1,), (1,)), ((), ())), preferred_element_type=jnp.float32
    ).astype(jnp.bfloat16)
    grad_flat = to_grid(inward(grad_grouped))
    block_out = (state_f + homeward(mixed_flat).astype(jnp.float32)).astype(jnp.bfloat16)
    normalized_gradient = homeward(grad_flat).astype(jnp.float32)
    gain_on_device = jnp.sum(normalized_gradient * standardized_input, axis=(0, 1))
    gain_scaled = normalized_gradient * layer_norm_gain
    layer_norm_gradient = inverse_deviation * (
        gain_scaled
        - jnp.mean(gain_scaled, axis=-1, keepdims=True)
        - standardized_input * jnp.mean(gain_scaled * standardized_input, axis=-1, keepdims=True)
    )
    grad_h = (cotangent.astype(jnp.float32) + layer_norm_gradient).astype(jnp.bfloat16)
    grad_hf = grad_h.astype(jnp.float32)
    padded_grad = widened(grad_h)
    grad_fields = (
        grad_hf + apply_taps(padded_grad, conv_kernel[::-1, ::-1], lat_rows, lon_cols)
    ).astype(jnp.bfloat16)
    kernel_terms = []
    for lat_tap in range(3):
        for lon_tap in range(3):
            kernel_terms.append(
                jnp.sum(
                    padded_fields[lat_tap : lat_tap + lat_rows, lon_tap : lon_tap + lon_cols]
                    * grad_hf,
                    axis=(0, 1),
                )
            )
    kernel_local = jnp.stack(kernel_terms).reshape(3, 3, feature_count)
    gain_total, kernel_total = lax.psum((gain_on_device, kernel_local), ("lat", "lon"))
    return (
        block_out,
        grad_fields,
        grad_project,
        kernel_total * scale_everywhere,
        gain_total * scale_everywhere,
    )


def solution(mesh):
    placed = (
        P("lat", "lon", None),
        P(),
        P(),
        P(),
        P(),
        P(),
        P("lat", "lon", None),
        P("lat", "lon", None),
    )
    return jax.shard_map(
        body,
        mesh=mesh,
        in_specs=placed,
        out_specs=(P("lat", "lon", None), P("lat", "lon", None), P("lat", "lon"), P(), P()),
        check_vma=False,
    )
```

profile of v0, /device:TPU:0, one launch (start us, length us, event | category | flops | bytes accessed | tf_op | source)
XLA Modules:
  0.0 325.8 jit_solution(15683025207276023643)
XLA Ops:
  8.8 5.1 %collective-permute-start.1 = (bf16[8,1,768]{2,1,0:T(2,128)(2,1)S(1)}, bf16[8,1,768]{2,1,0:T(2,128)(2,1)S(1)}, u32[]{:S(2)}, u32[]{:S(2)}) collective-permute-start(bf16[8,1,768]{2,1,0:T(2,128)(2,1)S(1)} %get-tuple-element.67), channel_id=1, source_target_pairs={{1,0},{2,1},{3,2},{4,3},{5,4},{6,5},{7,6},{8,7},{9,8},{10,9},{11,1... | collective-permute-start | bytes 36872 | tf_op jit(solution)/shard_map/ppermute | solution.py:24
  15.8 1.6 slice_reduce_fusion.8
  19.5 4.4 %collective-permute-start.2 = (bf16[1,34,768]{2,1,0:T(8,128)(2,1)}, bf16[1,34,768]{2,1,0:T(8,128)(2,1)}, u32[]{:S(2)}, u32[]{:S(2)}) collective-permute-start(bf16[1,34,768]{2,1,0:T(8,128)(2,1)} %get-tuple-element.61), channel_id=1, source_target_pairs={{0,16},{1,17},{2,18},{3,19},{4,20},{5,21},{6,22},{7,23},{8,24},{9,... | collective-permute-start | bytes 156680 | tf_op jit(solution)/shard_map/ppermute | solution.py:23
  25.2 3.2 gather_fusion.2
  28.4 1.8 collective-permute-done.3
  30.3 1.6 maximum_maximum_fusion
  34.9 3.3 %gather_fusion = bf16[256,768]{1,0:T(8,128)(2,1)} fusion(bf16[256,768]{1,0:T(8,128)(2,1)} %bitcast.109, s32[1024]{0:T(1024)} %copy-done.39), kind=kCustom, calls=%fused_computation.clone | custom fusion | bytes 787456 | tf_op jit(solution)/shard_map/jit(_take)/gather | solution.py:95
  38.3 2.0 broadcast_select_fusion.1
  41.1 4.1 %all-to-all-start.4 = ((bf16[2,16,8,1,1,768]{5,1,2,4,3,0:T(8,128)(2,1)}), bf16[2,16,8,1,1,768]{5,1,2,4,3,0:T(8,128)(2,1)}, u32[]{:S(2)}, u32[]{:S(2)}) async-start(bf16[2,16,8,1,1,768]{5,1,2,4,3,0:T(8,128)(2,1)} %copy.58), calls=%async_computation.4 | async-start | bytes 786432 | tf_op jit(solution)/shard_map/all_to_all | solution.py:48
  45.2 1.8 copy.45
  47.0 4.2 %all-to-all-done.4 = bf16[2,16,8,1,1,768]{5,1,2,4,3,0:T(8,128)(2,1)} async-done(((bf16[2,16,8,1,1,768]{5,1,2,4,3,0:T(8,128)(2,1)}), bf16[2,16,8,1,1,768]{5,1,2,4,3,0:T(8,128)(2,1)}, u32[]{:S(2)}, u32[]{:S(2)}) %all-to-all-start.4) | async-done | bytes 393248 | tf_op jit(solution)/shard_map/all_to_all | solution.py:48
  51.2 4.1 %all-to-all-start = ((bf16[2,16,8,1,1,768]{5,1,2,4,3,0:T(8,128)(2,1)}), bf16[2,16,8,1,1,768]{5,1,2,4,3,0:T(8,128)(2,1)}, u32[]{:S(2)}, u32[]{:S(2)}) async-start(bf16[2,16,8,1,1,768]{5,1,2,4,3,0:T(8,128)(2,1)} %copy.45), calls=%async_computation | async-start | bytes 786432 | tf_op jit(solution)/shard_map/all_to_all | solution.py:48
  55.4 2.1 copy.59
  57.5 3.8 %all-to-all-done = bf16[2,16,8,1,1,768]{5,1,2,4,3,0:T(8,128)(2,1)} async-done(((bf16[2,16,8,1,1,768]{5,1,2,4,3,0:T(8,128)(2,1)}), bf16[2,16,8,1,1,768]{5,1,2,4,3,0:T(8,128)(2,1)}, u32[]{:S(2)}, u32[]{:S(2)}) %all-to-all-start) | async-done | bytes 393248 | tf_op jit(solution)/shard_map/all_to_all | solution.py:48
  61.3 4.2 %all-to-all-start.5 = ((bf16[1,16,8,2,1,768]{5,3,2,4,0,1:T(2,128)(2,1)}), bf16[1,16,8,2,1,768]{5,3,2,4,0,1:T(2,128)(2,1)}, u32[]{:S(2)}, u32[]{:S(2)}) async-start(bf16[1,16,8,2,1,768]{5,3,2,4,0,1:T(2,128)(2,1)} %copy.59), calls=%async_computation.5 | async-start | bytes 786432 | tf_op jit(solution)/shard_map/all_to_all | solution.py:47
  65.5 2.1 copy.46
  67.7 10.1 %all-to-all-done.5 = bf16[1,16,8,2,1,768]{5,3,2,4,0,1:T(2,128)(2,1)} async-done(((bf16[1,16,8,2,1,768]{5,3,2,4,0,1:T(2,128)(2,1)}), bf16[1,16,8,2,1,768]{5,3,2,4,0,1:T(2,128)(2,1)}, u32[]{:S(2)}, u32[]{:S(2)}) %all-to-all-start.5) | async-done | bytes 393248 | tf_op jit(solution)/shard_map/all_to_all | solution.py:47
  77.7 4.4 %all-to-all-start.1 = ((bf16[1,16,8,2,1,768]{5,3,2,4,0,1:T(2,128)(2,1)}), bf16[1,16,8,2,1,768]{5,3,2,4,0,1:T(2,128)(2,1)}, u32[]{:S(2)}, u32[]{:S(2)}) async-start(bf16[1,16,8,2,1,768]{5,3,2,4,0,1:T(2,128)(2,1)} %copy.46), calls=%async_computation.1 | async-start | bytes 786432 | tf_op jit(solution)/shard_map/all_to_all | solution.py:47
  82.1 2.3 copy.52
  86.3 2.5 convolution_convert_fusion.5
  88.8 1.9 copy.61
  90.7 2.6 reshape.146
  95.3 2.1 convolution_convert_fusion
  97.4 2.4 copy.48
  99.8 4.6 %reshape.138 = bf16[4,64,3,24,32]{1,0,4,3,2:T(4,128)(2,1)} reshape(bf16[256,2304]{0,1:T(8,128)(2,1)} %copy.48) | data formatting | bytes 2359296 | tf_op jit(solution)/shard_map/reshape | solution.py:120
  104.4 2.6 fusion.58
  108.1 1.7 fusion.61
  109.8 1.8 fusion.5
  114.1 1.8 fusion.7
  118.9 2.5 reshape.139
  121.4 1.9 convolution_convert_fusion.6
  124.1 4.4 %all-to-all-start.2 = ((bf16[1,1,8,2,16,768]{5,4,2,1,0,3:T(8,128)(2,1)}), bf16[1,1,8,2,16,768]{5,4,2,1,0,3:T(8,128)(2,1)}, u32[]{:S(2)}, u32[]{:S(2)}) async-start(bf16[1,1,8,2,16,768]{5,4,2,1,0,3:T(8,128)(2,1)} %copy.55), calls=%async_computation.2 | async-start | bytes 786432 | tf_op jit(solution)/shard_map/all_to_all | solution.py:59
  128.4 2.2 pad_maximum_fusion
  130.6 4.5 %copy.67 = bf16[4,64,3,24,32]{1,0,4,3,2:T(4,128)(2,1)} copy(bf16[4,64,3,24,32]{1,4,3,0,2:T(8,128)(2,1)S(1)} %pad_maximum_fusion) | data formatting | bytes 2359296 | tf_op jit(solution)/shard_map/stack | solution.py:165
  135.1 4.5 %convert_element_type.159 = bf16[256,2304]{0,1:T(8,128)(2,1)} reshape(bf16[4,64,3,24,32]{1,0,4,3,2:T(4,128)(2,1)} %copy.67) | data formatting | bytes 2359296 | tf_op jit(solution)/shard_map/convert_element_type | solution.py:165
  139.6 2.4 convolution_convert_fusion.4
  142.8 4.2 %all-to-all-start.6 = ((bf16[1,1,8,2,16,768]{5,4,2,1,0,3:T(8,128)(2,1)}), bf16[1,1,8,2,16,768]{5,4,2,1,0,3:T(8,128)(2,1)}, u32[]{:S(2)}, u32[]{:S(2)}) async-start(bf16[1,1,8,2,16,768]{5,4,2,1,0,3:T(8,128)(2,1)} %copy.68), calls=%async_computation.6 | async-start | bytes 786432 | tf_op jit(solution)/shard_map/all_to_all | solution.py:59
  147.0 2.2 copy.56
  149.1 5.0 %all-to-all-done.6 = bf16[1,1,8,2,16,768]{5,4,2,1,0,3:T(8,128)(2,1)} async-done(((bf16[1,1,8,2,16,768]{5,4,2,1,0,3:T(8,128)(2,1)}), bf16[1,1,8,2,16,768]{5,4,2,1,0,3:T(8,128)(2,1)}, u32[]{:S(2)}, u32[]{:S(2)}) %all-to-all-start.6) | async-done | bytes 393248 | tf_op jit(solution)/shard_map/all_to_all | solution.py:59
  154.2 4.9 %all-to-all-start.3 = ((bf16[2,1,8,1,16,768]{5,0,2,3,1,4:T(2,128)(2,1)}), bf16[2,1,8,1,16,768]{5,0,2,3,1,4:T(2,128)(2,1)}, u32[]{:S(2)}, u32[]{:S(2)}) async-start(bf16[2,1,8,1,16,768]{5,0,2,3,1,4:T(2,128)(2,1)} %copy.56), calls=%async_computation.3 | async-start | bytes 786432 | tf_op jit(solution)/shard_map/all_to_all | solution.py:58
  159.2 2.6 convolution_convert_fusion.1
  161.8 2.1 copy.69
  163.9 7.4 %all-to-all-done.3 = bf16[2,1,8,1,16,768]{5,0,2,3,1,4:T(2,128)(2,1)} async-done(((bf16[2,1,8,1,16,768]{5,0,2,3,1,4:T(2,128)(2,1)}), bf16[2,1,8,1,16,768]{5,0,2,3,1,4:T(2,128)(2,1)}, u32[]{:S(2)}, u32[]{:S(2)}) %all-to-all-start.3) | async-done | bytes 393248 | tf_op jit(solution)/shard_map/all_to_all | solution.py:58
  171.4 4.2 %all-to-all-start.7 = ((bf16[2,1,8,1,16,768]{5,0,2,3,1,4:T(2,128)(2,1)}), bf16[2,1,8,1,16,768]{5,0,2,3,1,4:T(2,128)(2,1)}, u32[]{:S(2)}, u32[]{:S(2)}) async-start(bf16[2,1,8,1,16,768]{5,0,2,3,1,4:T(2,128)(2,1)} %copy.69), calls=%async_computation.7 | async-start | bytes 786432 | tf_op jit(solution)/shard_map/all_to_all | solution.py:58
  177.5 2.1 scatter_custom_fusion
  182.0 1.8 copy.57
  183.8 4.0 %all-to-all-done.7 = bf16[2,1,8,1,16,768]{5,0,2,3,1,4:T(2,128)(2,1)} async-done(((bf16[2,1,8,1,16,768]{5,0,2,3,1,4:T(2,128)(2,1)}), bf16[2,1,8,1,16,768]{5,0,2,3,1,4:T(2,128)(2,1)}, u32[]{:S(2)}, u32[]{:S(2)}) %all-to-all-start.7) | async-done | bytes 393248 | tf_op jit(solution)/shard_map/all_to_all | solution.py:58
  187.8 1.8 copy.70
  189.6 3.3 %gather_fusion.1 = bf16[256,768]{1,0:T(8,128)(2,1)} fusion(bf16[256,768]{1,0:T(8,128)(2,1)} %bitcast.107, s32[1024]{0:T(1024)} %pad_clamp_fusion), kind=kCustom, calls=%fused_computation.1.clone | custom fusion | bytes 787456 | tf_op jit(solution)/shard_map/jit(_take)/gather | solution.py:102
  192.9 3.3 %gather_fusion.3 = bf16[256,768]{1,0:T(8,128)(2,1)} fusion(bf16[256,768]{1,0:T(8,128)(2,1)} %bitcast.108, s32[1024]{0:T(1024)} %pad_clamp_fusion), kind=kCustom, calls=%fused_computation.3.clone | custom fusion | bytes 787456 | tf_op jit(solution)/shard_map/jit(_take)/gather | solution.py:102
  200.9 1.8 fusion.20
  202.7 3.2 fusion.45
  209.4 2.0 stack.59
  212.8 1.6 fusion.59
  214.5 4.3 %collective-permute-start.5 = (bf16[8,1,768]{2,1,0:T(2,128)(2,1)}, bf16[8,1,768]{2,1,0:T(2,128)(2,1)}, u32[]{:S(2)}, u32[]{:S(2)}) collective-permute-start(bf16[8,1,768]{2,1,0:T(2,128)(2,1)} %get-tuple-element.64), channel_id=1, source_target_pairs={{1,0},{2,1},{3,2},{4,3},{5,4},{6,5},{7,6},{8,7},{9,8},{10,9},{11,1... | collective-permute-start | bytes 36872 | tf_op jit(solution)/shard_map/ppermute | solution.py:24
  218.8 37.9 %all-reduce = (f32[3,3,768]{2,1,0:T(4,128)}, f32[768]{0:T(1024)}) all-reduce(f32[3,3,768]{2,1,0:T(4,128)} %reshape.149, f32[768]{0:T(1024)} %get-tuple-element.30), channel_id=1, replica_groups=mesh['lat'=2,'lon'=16] {'lat','lon'}, use_global_device_ids=true, to_apply=%region_19.21 | all-reduce | flops 7680 | bytes 61440 | tf_op jit(solution)/shard_map/psum | solution.py:197
  256.7 2.1 copy.76
  261.2 4.2 %collective-permute-start.6 = (bf16[1,34,768]{2,1,0:T(8,128)(2,1)S(1)}, bf16[1,34,768]{2,1,0:T(8,128)(2,1)S(1)}, u32[]{:S(2)}, u32[]{:S(2)}) collective-permute-start(bf16[1,34,768]{2,1,0:T(8,128)(2,1)S(1)} %get-tuple-element.57), channel_id=1, source_target_pairs={{0,16},{1,17},{2,18},{3,19},{4,20},{5,21},{6,22},{7,23},{8,24},{9,... | collective-permute-start | bytes 156680 | tf_op jit(solution)/shard_map/ppermute | solution.py:23
  268.0 3.5 %collective-permute-done.7 = bf16[1,34,768]{2,1,0:T(8,128)(2,1)S(1)} collective-permute-done((bf16[1,34,768]{2,1,0:T(8,128)(2,1)S(1)}, bf16[1,34,768]{2,1,0:T(8,128)(2,1)S(1)}, u32[]{:S(2)}, u32[]{:S(2)}) %collective-permute-start.7) | collective-permute-done | bytes 52256 | tf_op jit(solution)/shard_map/ppermute | solution.py:24
  271.5 1.6 maximum_maximum_fusion.1
  273.3 2.4 fusion.36
  275.7 38.5 %reduce-scatter.7.cloned.1.call-done = bf16[48,384]{1,0:T(8,128)(2,1)} async-done(((bf16[768,384]{1,0:T(8,128)(2,1)}), bf16[48,384]{1,0:T(8,128)(2,1)}) %reduce-scatter.7.cloned.1.call-update) | async-done | bytes 36880
  315.7 1.6 convert_multiply_fusion.19
  317.3 1.7 copy.71
  (144 shorter events, 43.1 us)
Async XLA Ops:
  7.2 88.1 %copy-start = (bf16[768,2304]{1,0:T(8,128)(2,1)S(1)}, bf16[768,2304]{1,0:T(8,128)(2,1)}, u32[]{:S(2)}) copy-start(bf16[768,2304]{1,0:T(8,128)(2,1)} %param.13) | copy-start | bytes 10616836
  8.3 9.0 %collective-permute-start = (bf16[8,1,768]{2,1,0:T(2,128)(2,1)S(1)}, bf16[8,1,768]{2,1,0:T(2,128)(2,1)S(1)}, u32[]{:S(2)}, u32[]{:S(2)}) collective-permute-start(bf16[8,1,768]{2,1,0:T(2,128)(2,1)S(1)} %get-tuple-element.66), channel_id=1, source_target_pairs={{0,1},{1,2},{2,3},{3,4},{4,5},{5,6},{6,7},{7,8},{8,9},{9,10},{10,1... | collective-permute-start | bytes 36872 | tf_op jit(solution)/shard_map/ppermute | solution.py:23
  8.8 8.5 %collective-permute-start.1 = (bf16[8,1,768]{2,1,0:T(2,128)(2,1)S(1)}, bf16[8,1,768]{2,1,0:T(2,128)(2,1)S(1)}, u32[]{:S(2)}, u32[]{:S(2)}) collective-permute-start(bf16[8,1,768]{2,1,0:T(2,128)(2,1)S(1)} %get-tuple-element.67), channel_id=1, source_target_pairs={{1,0},{2,1},{3,2},{4,3},{5,4},{6,5},{7,6},{8,7},{9,8},{10,9},{11,1... | collective-permute-start | bytes 36872 | tf_op jit(solution)/shard_map/ppermute | solution.py:24
  17.3 15.9 %copy-start.22 = (f32[768]{0:T(1024)}, f32[768]{0:T(1024)S(1)}, u32[]{:S(2)}) copy-start(f32[768]{0:T(1024)S(1)} %get-tuple-element.39) | copy-start | bytes 9220
  17.3 15.9 %copy-start.24 = (f32[768]{0:T(1024)}, f32[768]{0:T(1024)S(1)}, u32[]{:S(2)}) copy-start(f32[768]{0:T(1024)S(1)} %get-tuple-element.40) | copy-start | bytes 9220
  17.3 0.6 copy-start.15
  17.9 1.5 copy-start.18
  19.5 9.0 %collective-permute-start.2 = (bf16[1,34,768]{2,1,0:T(8,128)(2,1)}, bf16[1,34,768]{2,1,0:T(8,128)(2,1)}, u32[]{:S(2)}, u32[]{:S(2)}) collective-permute-start(bf16[1,34,768]{2,1,0:T(8,128)(2,1)} %get-tuple-element.61), channel_id=1, source_target_pairs={{0,16},{1,17},{2,18},{3,19},{4,20},{5,21},{6,22},{7,23},{8,24},{9,... | collective-permute-start | bytes 156680 | tf_op jit(solution)/shard_map/ppermute | solution.py:23
  23.9 6.4 %collective-permute-start.3 = (bf16[1,34,768]{2,1,0:T(8,128)(2,1)}, bf16[1,34,768]{2,1,0:T(8,128)(2,1)}, u32[]{:S(2)}, u32[]{:S(2)}) collective-permute-start(bf16[1,34,768]{2,1,0:T(8,128)(2,1)} %get-tuple-element.62), channel_id=1, source_target_pairs={{16,0},{17,1},{18,2},{19,3},{20,4},{21,5},{22,6},{23,7},{24,8},{25... | collective-permute-start | bytes 156680 | tf_op jit(solution)/shard_map/ppermute | solution.py:24
  25.2 3.2 copy-start.39
  28.4 3.6 %copy-start.9 = (bf16[8,32,768]{2,1,0:T(8,128)(2,1)S(1)}, bf16[8,32,768]{2,1,0:T(8,128)(2,1)}, u32[]{:S(2)}) copy-start(bf16[8,32,768]{2,1,0:T(8,128)(2,1)} %param.10) | copy-start | bytes 1179652
  28.4 3.6 %copy-start.16 = (bf16[8,1,768]{2,1,0:T(2,128)(2,1)S(1)}, bf16[8,1,768]{2,1,0:T(2,128)(2,1)}, u32[]{:S(2)}) copy-start(bf16[8,1,768]{2,1,0:T(2,128)(2,1)} %copy-done.15) | copy-start | bytes 36868
  28.4 3.6 %copy-start.19 = (bf16[8,1,768]{2,1,0:T(2,128)(2,1)S(1)}, bf16[8,1,768]{2,1,0:T(2,128)(2,1)}, u32[]{:S(2)}) copy-start(bf16[8,1,768]{2,1,0:T(2,128)(2,1)} %copy-done.18) | copy-start | bytes 36868
  28.4 3.6 %copy-start.26 = (f32[768]{0:T(1024)S(1)}, f32[768]{0:T(1024)}, u32[]{:S(2)}) copy-start(f32[768]{0:T(1024)} %get-tuple-element.41) | copy-start | bytes 9220
  28.4 3.6 %copy-start.28 = (f32[768]{0:T(1024)S(1)}, f32[768]{0:T(1024)}, u32[]{:S(2)}) copy-start(f32[768]{0:T(1024)} %get-tuple-element.42) | copy-start | bytes 9220
  28.4 3.6 %copy-start.30 = (f32[768]{0:T(1024)S(1)}, f32[768]{0:T(1024)}, u32[]{:S(2)}) copy-start(f32[768]{0:T(1024)} %get-tuple-element.43) | copy-start | bytes 9220
  28.4 3.6 %copy-start.32 = (f32[768]{0:T(1024)S(1)}, f32[768]{0:T(1024)}, u32[]{:S(2)}) copy-start(f32[768]{0:T(1024)} %get-tuple-element.44) | copy-start | bytes 9220
  28.4 3.6 %copy-start.34 = (f32[768]{0:T(1024)S(1)}, f32[768]{0:T(1024)}, u32[]{:S(2)}) copy-start(f32[768]{0:T(1024)} %get-tuple-element.45) | copy-start | bytes 9220
  28.4 3.6 %copy-start.36 = (f32[768]{0:T(1024)S(1)}, f32[768]{0:T(1024)}, u32[]{:S(2)}) copy-start(f32[768]{0:T(1024)} %get-tuple-element.46) | copy-start | bytes 9220
  31.9 1.3 copy-start.2
  31.9 1.3 copy-start.4
  32.0 1.9 copy-start.21
  33.2 0.7 copy-start.6
  41.1 10.1 %all-to-all-start.4 = ((bf16[2,16,8,1,1,768]{5,1,2,4,3,0:T(8,128)(2,1)}), bf16[2,16,8,1,1,768]{5,1,2,4,3,0:T(8,128)(2,1)}, u32[]{:S(2)}, u32[]{:S(2)}) async-start(bf16[2,16,8,1,1,768]{5,1,2,4,3,0:T(8,128)(2,1)} %copy.58), calls=%async_computation.4 | async-start | bytes 786432 | tf_op jit(solution)/shard_map/all_to_all | solution.py:48
  51.2 10.1 %all-to-all-start = ((bf16[2,16,8,1,1,768]{5,1,2,4,3,0:T(8,128)(2,1)}), bf16[2,16,8,1,1,768]{5,1,2,4,3,0:T(8,128)(2,1)}, u32[]{:S(2)}, u32[]{:S(2)}) async-start(bf16[2,16,8,1,1,768]{5,1,2,4,3,0:T(8,128)(2,1)} %copy.45), calls=%async_computation | async-start | bytes 786432 | tf_op jit(solution)/shard_map/all_to_all | solution.py:48
  61.3 16.4 %all-to-all-start.5 = ((bf16[1,16,8,2,1,768]{5,3,2,4,0,1:T(2,128)(2,1)}), bf16[1,16,8,2,1,768]{5,3,2,4,0,1:T(2,128)(2,1)}, u32[]{:S(2)}, u32[]{:S(2)}) async-start(bf16[1,16,8,2,1,768]{5,3,2,4,0,1:T(2,128)(2,1)} %copy.59), calls=%async_computation.5 | async-start | bytes 786432 | tf_op jit(solution)/shard_map/all_to_all | solution.py:47
  77.7 16.4 %all-to-all-start.1 = ((bf16[1,16,8,2,1,768]{5,3,2,4,0,1:T(2,128)(2,1)}), bf16[1,16,8,2,1,768]{5,3,2,4,0,1:T(2,128)(2,1)}, u32[]{:S(2)}, u32[]{:S(2)}) async-start(bf16[1,16,8,2,1,768]{5,3,2,4,0,1:T(2,128)(2,1)} %copy.46), calls=%async_computation.1 | async-start | bytes 786432 | tf_op jit(solution)/shard_map/all_to_all | solution.py:47
  85.5 0.8 copy-start.12
  106.9 1.1 copy-start.13
  108.1 1.7 copy-start.14
  124.1 18.7 %all-to-all-start.2 = ((bf16[1,1,8,2,16,768]{5,4,2,1,0,3:T(8,128)(2,1)}), bf16[1,1,8,2,16,768]{5,4,2,1,0,3:T(8,128)(2,1)}, u32[]{:S(2)}, u32[]{:S(2)}) async-start(bf16[1,1,8,2,16,768]{5,4,2,1,0,3:T(8,128)(2,1)} %copy.55), calls=%async_computation.2 | async-start | bytes 786432 | tf_op jit(solution)/shard_map/all_to_all | solution.py:59
  142.8 11.4 %all-to-all-start.6 = ((bf16[1,1,8,2,16,768]{5,4,2,1,0,3:T(8,128)(2,1)}), bf16[1,1,8,2,16,768]{5,4,2,1,0,3:T(8,128)(2,1)}, u32[]{:S(2)}, u32[]{:S(2)}) async-start(bf16[1,1,8,2,16,768]{5,4,2,1,0,3:T(8,128)(2,1)} %copy.68), calls=%async_computation.6 | async-start | bytes 786432 | tf_op jit(solution)/shard_map/all_to_all | solution.py:59
  154.2 17.2 %all-to-all-start.3 = ((bf16[2,1,8,1,16,768]{5,0,2,3,1,4:T(2,128)(2,1)}), bf16[2,1,8,1,16,768]{5,0,2,3,1,4:T(2,128)(2,1)}, u32[]{:S(2)}, u32[]{:S(2)}) async-start(bf16[2,1,8,1,16,768]{5,0,2,3,1,4:T(2,128)(2,1)} %copy.56), calls=%async_computation.3 | async-start | bytes 786432 | tf_op jit(solution)/shard_map/all_to_all | solution.py:58
  159.1 97.6 %reduce-scatter.5.cloned.1.call-start = ((), (), s32[]{:S(2)}) async-start(), calls=%async_computation.10 | async-start | bytes 1769472 | tf_op jit(solution)/shard_map/reduce_scatter | solution.py:132
  171.4 16.4 %all-to-all-start.7 = ((bf16[2,1,8,1,16,768]{5,0,2,3,1,4:T(2,128)(2,1)}), bf16[2,1,8,1,16,768]{5,0,2,3,1,4:T(2,128)(2,1)}, u32[]{:S(2)}, u32[]{:S(2)}) async-start(bf16[2,1,8,1,16,768]{5,0,2,3,1,4:T(2,128)(2,1)} %copy.69), calls=%async_computation.7 | async-start | bytes 786432 | tf_op jit(solution)/shard_map/all_to_all | solution.py:58
  175.6 138.6 %reduce-scatter.7.cloned.1.call-start = ((), (), s32[]{:S(2)}) async-start(), calls=%async_computation.11 | async-start | bytes 626688
  199.4 1.4 copy-start.7
  199.4 1.4 copy-start.8
  199.4 1.4 copy-start.40
  200.7 1.9 copy-start.1
  200.8 1.9 copy-start.3
  200.8 1.9 copy-start.5
  200.8 1.8 copy-start.10
  200.8 1.8 copy-start.17
  200.8 1.8 copy-start.20
  200.8 1.8 copy-start.38
  214.4 45.9 %collective-permute-start.4 = (bf16[8,1,768]{2,1,0:T(2,128)(2,1)}, bf16[8,1,768]{2,1,0:T(2,128)(2,1)}, u32[]{:S(2)}, u32[]{:S(2)}) collective-permute-start(bf16[8,1,768]{2,1,0:T(2,128)(2,1)} %get-tuple-element.63), channel_id=1, source_target_pairs={{0,1},{1,2},{2,3},{3,4},{4,5},{5,6},{6,7},{7,8},{8,9},{9,10},{10,1... | collective-permute-start | bytes 36872 | tf_op jit(solution)/shard_map/ppermute | solution.py:23
  214.5 45.8 %collective-permute-start.5 = (bf16[8,1,768]{2,1,0:T(2,128)(2,1)}, bf16[8,1,768]{2,1,0:T(2,128)(2,1)}, u32[]{:S(2)}, u32[]{:S(2)}) collective-permute-start(bf16[8,1,768]{2,1,0:T(2,128)(2,1)} %get-tuple-element.64), channel_id=1, source_target_pairs={{1,0},{2,1},{3,2},{4,3},{5,4},{6,5},{7,6},{8,7},{9,8},{10,9},{11,1... | collective-permute-start | bytes 36872 | tf_op jit(solution)/shard_map/ppermute | solution.py:24
  258.8 14.4 %copy-start.23 = (f32[768]{0:T(1024)S(1)}, f32[768]{0:T(1024)}, u32[]{:S(2)}) copy-start(f32[768]{0:T(1024)} %copy-done.22) | copy-start | bytes 9220
  258.8 14.4 %copy-start.25 = (f32[768]{0:T(1024)S(1)}, f32[768]{0:T(1024)}, u32[]{:S(2)}) copy-start(f32[768]{0:T(1024)} %copy-done.24) | copy-start | bytes 9220
  258.8 14.4 %copy-start.27 = (f32[768]{0:T(1024)S(1)}, f32[768]{0:T(1024)}, u32[]{:S(2)}) copy-start(f32[768]{0:T(1024)} %get-tuple-element.41) | copy-start | bytes 9220
  258.8 14.4 %copy-start.11 = (bf16[8,32,768]{2,1,0:T(8,128)(2,1)S(1)}, bf16[8,32,768]{2,1,0:T(8,128)(2,1)}, u32[]{:S(2)}) copy-start(bf16[8,32,768]{2,1,0:T(8,128)(2,1)} %get-tuple-element.49) | copy-start | bytes 1179652
  258.9 14.4 %copy-start.29 = (f32[768]{0:T(1024)S(1)}, f32[768]{0:T(1024)}, u32[]{:S(2)}) copy-start(f32[768]{0:T(1024)} %get-tuple-element.42) | copy-start | bytes 9220
  258.9 14.4 %copy-start.31 = (f32[768]{0:T(1024)S(1)}, f32[768]{0:T(1024)}, u32[]{:S(2)}) copy-start(f32[768]{0:T(1024)} %get-tuple-element.43) | copy-start | bytes 9220
  258.9 14.4 %copy-start.33 = (f32[768]{0:T(1024)S(1)}, f32[768]{0:T(1024)}, u32[]{:S(2)}) copy-start(f32[768]{0:T(1024)} %get-tuple-element.44) | copy-start | bytes 9220
  258.9 14.4 %copy-start.35 = (f32[768]{0:T(1024)S(1)}, f32[768]{0:T(1024)}, u32[]{:S(2)}) copy-start(f32[768]{0:T(1024)} %get-tuple-element.45) | copy-start | bytes 9220
  258.9 14.4 %copy-start.37 = (f32[768]{0:T(1024)S(1)}, f32[768]{0:T(1024)}, u32[]{:S(2)}) copy-start(f32[768]{0:T(1024)} %get-tuple-element.46) | copy-start | bytes 9220
  261.2 6.8 %collective-permute-start.6 = (bf16[1,34,768]{2,1,0:T(8,128)(2,1)S(1)}, bf16[1,34,768]{2,1,0:T(8,128)(2,1)S(1)}, u32[]{:S(2)}, u32[]{:S(2)}) collective-permute-start(bf16[1,34,768]{2,1,0:T(8,128)(2,1)S(1)} %get-tuple-element.57), channel_id=1, source_target_pairs={{0,16},{1,17},{2,18},{3,19},{4,20},{5,21},{6,22},{7,23},{8,24},{9,... | collective-permute-start | bytes 156680 | tf_op jit(solution)/shard_map/ppermute | solution.py:23
  265.4 6.1 %collective-permute-start.7 = (bf16[1,34,768]{2,1,0:T(8,128)(2,1)S(1)}, bf16[1,34,768]{2,1,0:T(8,128)(2,1)S(1)}, u32[]{:S(2)}, u32[]{:S(2)}) collective-permute-start(bf16[1,34,768]{2,1,0:T(8,128)(2,1)S(1)} %get-tuple-element.58), channel_id=1, source_target_pairs={{16,0},{17,1},{18,2},{19,3},{20,4},{21,5},{22,6},{23,7},{24,8},{25... | collective-permute-start | bytes 156680 | tf_op jit(solution)/shard_map/ppermute | solution.py:24
Sparse Core Ops, SparseCore 0:
  162.2 22.0 reduce-scatter.4
  259.0 55.2 reduce-scatter.6
where the time goes:
time: 329 us; the launch traced here: 326 us
  local copies, waits for them, and re-layouts  84 us (26%)
  waiting for transfers between devices  79.3 us (24%)
  starting transfers between devices  55.8 us (17%)
  blocking collectives  37.9 us (12%)
  other arithmetic  35.4 us (11%)
  matrix products  18.7 us (6%)
  between operations  14.8 us (4%)
    unnamed x3, waiting for transfers between devices  38.5 us
    psum x1, blocking collectives, body(): lax.psum((gain_on_device, kernel_local), ('lat', 'lon'))  37.9 us
    ppermute x4, starting transfers between devices, extended(): after = lax.ppermute(first, axis, down)  12 us
    all_to_all x2, waiting for transfers between devices, to_grid(): lax.all_to_all(lax.all_to_all(packed, 'lat', split_axis=3, concat_axis=0,...  11.5 us
    all_to_all x2, waiting for transfers between devices, to_owner(): lax.all_to_all(lax.all_to_all(packed, 'lat', split_axis=0, concat_axis=3,...  10.9 us
    unnamed x86, local copies, waits for them, and re-layouts  10 us
    ppermute x4, starting transfers between devices, extended(): before = lax.ppermute(last, axis, up)  9.19 us
    all_to_all x2, starting transfers between devices, to_grid(): lax.all_to_all(lax.all_to_all(packed, 'lat', split_axis=3, concat_axis=0,...  9.15 us
  transfers between devices with their start and end apart: 18, of which 10 were waited for; matrix products, arithmetic and copies ran while one was open for 27% of the time, Pallas kernels for 0%

commit v1 on v0

v1 whole, which is shorter than its diff:
```python
import math

import jax
import jax.numpy as jnp
from jax import lax
from jax.experimental import pallas as pl
from jax.experimental.pallas import tpu as pltpu
from jax.sharding import PartitionSpec as P

HEADS = 24
HEAD_DIM = 32
GROUP = 64
PAIR = 2 * GROUP
EDGE = 8

epsilon = 1e-05
f32, bf16 = jnp.float32, jnp.bfloat16
AXES = ("lat", "lon")
NN = (((1,), (0,)), ((), ()))
NT = (((1,), (1,)), ((), ()))
TN = (((0,), (0,)), ((), ()))
VMEM = pl.BlockSpec(memory_space=pltpu.VMEM)


def dot(a, b, dims=NN):
    return lax.dot_general(a, b, dims, preferred_element_type=f32)


def call(kernel, name, out_shape, operands, scratch=(), flops=0):
    size = sum(math.prod(x.shape) * x.dtype.itemsize for x in (*operands, *out_shape))
    return pl.pallas_call(
        kernel,
        name=name,
        out_shape=list(out_shape),
        in_specs=[VMEM] * len(operands),
        out_specs=[VMEM] * len(out_shape),
        scratch_shapes=list(scratch),
        compiler_params=pltpu.CompilerParams(vmem_limit_bytes=40 * 1024 * 1024),
        cost_estimate=pl.CostEstimate(flops=flops, bytes_accessed=size, transcendentals=0),
    )(*operands)


def shape(dims, dtype):
    return jax.ShapeDtypeStruct(dims, dtype)


def by_cell(pattern_row, cells):
    cell = lax.broadcasted_iota(jnp.int32, (cells, cells), 0)
    return jnp.where(pattern_row == cell, 1.0, 0.0).astype(bf16)


def by_slot(pattern_col, cells):
    cell = lax.broadcasted_iota(jnp.int32, (cells, cells), 1)
    return jnp.where(pattern_col == cell, 1.0, 0.0).astype(bf16)


def position_by_row(cells, slots, blocks, row_dim):
    row = lax.broadcasted_iota(jnp.int32, (cells, cells), row_dim)
    position = lax.broadcasted_iota(jnp.int32, (cells, cells), 1 - row_dim)
    place = lax.rem(row, slots) * blocks + lax.div(row, slots)
    return jnp.where(place == position, 1.0, 0.0).astype(bf16)


def pack_kernel(pattern_ref, rows_ref, out_ref):
    cells = rows_ref.shape[0]
    out_ref[...] = dot(by_slot(pattern_ref[...], cells), rows_ref[...]).astype(bf16)


def fill_pad(pad, field_ref, before_ref, after_ref, left_ref, right_ref):
    rows, cols, _ = field_ref.shape
    pad[0, EDGE : EDGE + cols] = before_ref[...].astype(f32)
    pad[rows + 1, EDGE : EDGE + cols] = after_ref[...].astype(f32)
    for row in range(rows):
        pad[row + 1, EDGE : EDGE + cols] = field_ref[row].astype(f32)
    left, right = left_ref[...].astype(f32), right_ref[...].astype(f32)
    for row in range(rows + 2):
        pad[row, EDGE - 1 : EDGE] = left[row : row + 1]
        pad[row, EDGE + cols : EDGE + cols + 1] = right[row : row + 1]


def taps_row(pad, taps, row, cols, flip):
    summed = pad[row + 1, EDGE : EDGE + cols]
    for a in range(3):
        for b in range(3):
            at = 3 * (2 - a) + 2 - b if flip else 3 * a + b
            summed = summed + taps[at : at + 1] * pad[row + a, EDGE - 1 + b : EDGE - 1 + b + cols]
    return summed


def normalized(h):
    mean = jnp.mean(h, axis=-1, keepdims=True)
    centred = h - mean
    var = jnp.mean(centred * centred, axis=-1, keepdims=True)
    deviation = lax.rsqrt(var + epsilon)
    return centred * deviation, deviation


def enter_kernel(
    pattern_ref, field_ref, before_ref, after_ref, left_ref, right_ref, taps_ref, gain_ref,
    h_ref, out_ref, pad, normed,
):
    rows, cols, _ = field_ref.shape
    fill_pad(pad, field_ref, before_ref, after_ref, left_ref, right_ref)
    taps, gain = taps_ref[...], gain_ref[...]
    for row in range(rows):
        h = taps_row(pad, taps, row, cols, False).astype(bf16)
        h_ref[row * cols : (row + 1) * cols] = h
        xhat, _ = normalized(h.astype(f32))
        normed[row * cols : (row + 1) * cols] = (xhat * gain).astype(bf16)
    out_ref[...] = dot(by_slot(pattern_ref[...], rows * cols), normed[...]).astype(bf16)


def cot_kernel(slots, blocks, arrived_ref, out_weight_ref, grad_att_ref, cot_ref):
    cells = arrived_ref.shape[0]
    grouped = dot(position_by_row(cells, slots, blocks, 1), arrived_ref[...]).astype(bf16)
    grad_att_ref[...] = dot(out_weight_ref[...], grouped, NT).astype(bf16)
    cot_ref[...] = grouped.T


def low_lanes(dims):
    return lax.broadcasted_iota(jnp.int32, dims, len(dims) - 1) < GROUP


def pair_scores(left, right):
    both = dot(left, right, TN)
    return jnp.where(low_lanes((GROUP, PAIR)), both[:GROUP], both[GROUP:])


def pair_diagonal(compact):
    low = low_lanes((GROUP, PAIR))
    zero = jnp.zeros_like(compact)
    return jnp.concatenate([jnp.where(low, compact, zero), jnp.where(low, zero, compact)], axis=0)


def forward_kernel(
    slots, blocks, unroll,
    arrived_ref, qkv_weight_t_ref, out_weight_t_ref, bias_ref,
    mixed_ref, qkv_ref, probs_ref, att_ref,
):
    cells, width = arrived_ref.shape
    grouped = dot(position_by_row(cells, slots, blocks, 1), arrived_ref[...]).astype(bf16)
    step = width // 2
    for at in range(0, 3 * width, step):
        qkv_ref[at : at + step] = dot(qkv_weight_t_ref[at : at + step], grouped, NT).astype(bf16)
    scale = HEAD_DIM ** (-0.5)

    def head(e):
        at = pl.multiple_of(e * HEAD_DIM, HEAD_DIM)
        rows = pl.ds(at, HEAD_DIM)
        bias = bias_ref[e]
        for pair in range(cells // PAIR):
            lanes = slice(pair * PAIR, (pair + 1) * PAIR)
            q = qkv_ref[rows, lanes]
            k = qkv_ref[pl.ds(width + at, HEAD_DIM), lanes]
            v = qkv_ref[pl.ds(2 * width + at, HEAD_DIM), lanes]
            scores = pair_scores(k, q) * scale + bias
            lifted = jnp.exp(scores - jnp.max(scores, axis=0, keepdims=True))
            probs = lifted / jnp.sum(lifted, axis=0, keepdims=True)
            probs_ref[e, :, lanes] = probs
            att_ref[rows, lanes] = dot(v, pair_diagonal(probs).astype(bf16)).astype(bf16)

    def heads(step, carry):
        for u in range(unroll):
            head(step * unroll + u)
        return carry

    lax.fori_loop(0, HEADS // unroll, heads, 0)
    mixed = dot(out_weight_t_ref[...], att_ref[...]).astype(bf16)
    mixed_ref[...] = dot(position_by_row(cells, slots, blocks, 0), mixed, NT).astype(bf16)


def backward_kernel(
    slots, blocks, unroll,
    qkv_ref, probs_ref, grad_att_ref, qkv_weight_ref,
    out_ref, grad_qkv,
):
    cells, width = out_ref.shape
    scale = HEAD_DIM ** (-0.5)

    def head(e):
        at = pl.multiple_of(e * HEAD_DIM, HEAD_DIM)
        rows = pl.ds(at, HEAD_DIM)
        key_rows, value_rows = pl.ds(width + at, HEAD_DIM), pl.ds(2 * width + at, HEAD_DIM)
        for pair in range(cells // PAIR):
            lanes = slice(pair * PAIR, (pair + 1) * PAIR)
            q, k, v = qkv_ref[rows, lanes], qkv_ref[key_rows, lanes], qkv_ref[value_rows, lanes]
            grad = grad_att_ref[rows, lanes]
            probs = probs_ref[e, :, lanes]
            grad_probs = pair_scores(v, grad)
            dropped = jnp.sum(probs * grad_probs, axis=0, keepdims=True)
            grad_scores = pair_diagonal(probs * (grad_probs - dropped)).astype(bf16)
            grad_qkv[rows, lanes] = (dot(k, grad_scores) * scale).astype(bf16)
            grad_qkv[key_rows, lanes] = (dot(q, grad_scores, NT) * scale).astype(bf16)
            grad_qkv[value_rows, lanes] = dot(grad, pair_diagonal(probs).astype(bf16), NT).astype(bf16)

    def heads(step, carry):
        for u in range(unroll):
            head(step * unroll + u)
        return carry

    lax.fori_loop(0, HEADS // unroll, heads, 0)
    grad = dot(qkv_weight_ref[...], grad_qkv[...]).astype(bf16)
    out_ref[...] = dot(position_by_row(cells, slots, blocks, 0), grad, NT).astype(bf16)


def project_kernel(cot_ref, att_ref, out_ref):
    if out_ref.ndim == 2:
        out_ref[...] = dot(cot_ref[...], att_ref[...], NT).astype(bf16)
        return
    lats, lons, cols, rows = out_ref.shape
    for a in range(lats):
        part = dot(cot_ref[...], att_ref[a * rows : (a + 1) * rows], NT).astype(bf16)
        for b in range(lons):
            out_ref[a, b] = part[b * cols : (b + 1) * cols]


def leave_kernel(pattern_ref, mixed_ref, h_ref, out_ref):
    mixed = dot(by_cell(pattern_ref[...], h_ref.shape[0]), mixed_ref[...])
    out_ref[...] = (h_ref[...].astype(f32) + mixed).astype(bf16)


def return_kernel(
    pattern_ref, arrived_ref, h_ref, cot_ref, gain_ref,
    field_ref, before_ref, after_ref, left_ref, right_ref,
    grad_ref, sums_ref, pad, normed_grad,
):
    rows, cols, width = field_ref.shape
    fill_pad(pad, field_ref, before_ref, after_ref, left_ref, right_ref)
    normed_grad[...] = dot(by_cell(pattern_ref[...], rows * cols), arrived_ref[...])
    gain = gain_ref[...]

    def fold(x):
        return jnp.sum(x.reshape(cols // 8, 8, width), axis=0)

    sums = [jnp.zeros((8, width), f32) for _ in range(10)]
    for row in range(rows):
        at = slice(row * cols, (row + 1) * cols)
        xhat, deviation = normalized(h_ref[at].astype(f32))
        grad = normed_grad[at]
        sums[9] = sums[9] + fold(grad * xhat)
        u = grad * gain
        inner = u - jnp.mean(u, axis=-1, keepdims=True)
        inner = inner - xhat * jnp.mean(u * xhat, axis=-1, keepdims=True)
        grad_h = (cot_ref[at].astype(f32) + deviation * inner).astype(bf16)
        grad_ref[row] = grad_h
        grad_h = grad_h.astype(f32)
        for a in range(3):
            for b in range(3):
                moved = pad[row + a, EDGE - 1 + b : EDGE - 1 + b + cols]
                sums[3 * a + b] = sums[3 * a + b] + fold(moved * grad_h)
    for i in range(10):
        sums_ref[i : i + 1] = jnp.sum(sums[i], axis=0, keepdims=True)
    sums_ref[10:16] = jnp.zeros((6, width), f32)


def spread_kernel(
    field_ref, before_ref, after_ref, left_ref, right_ref, taps_ref, out_ref, pad
):
    rows, cols, _ = field_ref.shape
    fill_pad(pad, field_ref, before_ref, after_ref, left_ref, right_ref)
    taps = taps_ref[...]
    for row in range(rows):
        out_ref[row] = taps_row(pad, taps, row, cols, True).astype(bf16)


def swap_pairs(size, bit):
    return [(i, i ^ bit) for i in range(size)]


def rims(field):
    lat_count, lon_count = lax.axis_size("lat"), lax.axis_size("lon")
    first, last = field[0], field[-1]
    if lat_count == 2:
        low = lax.axis_index("lat") == 0
        met = lax.ppermute(jnp.where(low, last, first), "lat", [(0, 1), (1, 0)])
        none = jnp.zeros_like(met)
        before, after = jnp.where(low, none, met), jnp.where(low, met, none)
    else:
        up = [(i, i + 1) for i in range(lat_count - 1)]
        before = lax.ppermute(last, "lat", up)
        after = lax.ppermute(first, "lat", [(j, i) for i, j in up])
    right = [(i, (i + 1) % lon_count) for i in range(lon_count)]

    def column(at):
        return jnp.concatenate([before[at : at + 1], field[:, at], after[at : at + 1]], axis=0)

    from_left = lax.ppermute(column(field.shape[1] - 1), "lon", right)
    from_right = lax.ppermute(column(0), "lon", [(j, i) for i, j in right])
    return before, after, from_left, from_right


def exchange(rows):
    blocks = lax.axis_size("lat") * lax.axis_size("lon")
    cells, width = rows.shape
    sent = rows.reshape(blocks, cells // blocks, width)
    return lax.all_to_all(sent, AXES, split_axis=0, concat_axis=0, tiled=True).reshape(cells, width)


def total_over_devices(x):
    for axis in ("lon", "lat"):
        size = lax.axis_size(axis)
        if size & (size - 1):
            x = lax.psum(x, axis)
            continue
        bit = 1
        while bit < size:
            x = x + lax.ppermute(x, axis, swap_pairs(size, bit))
            bit *= 2
    return x


def body(
    fields, conv_kernel, layer_norm_gain, qkv_weight, out_weight, score_bias, pattern, cotangent
):
    rows, cols, width = fields.shape
    cells = rows * cols
    lat_count, lon_count = lax.axis_size("lat"), lax.axis_size("lon")
    blocks = lat_count * lon_count
    slots = cells // blocks
    scale_everywhere = 1.0 / math.sqrt(cells * blocks)
    pattern_row = pattern.reshape(1, cells)
    pattern_col = pattern.reshape(cells, 1)
    gain = layer_norm_gain.reshape(1, width)
    taps = conv_kernel.reshape(9, width)
    cot_rows = cotangent.reshape(cells, width)
    qkv_weight_t = qkv_weight.T
    out_weight_t = out_weight.T
    bias = jnp.swapaxes(score_bias, 1, 2)
    bias = jnp.concatenate([bias, bias], axis=2)
    pad = pltpu.VMEM((rows + 2, cols + 2 * EDGE, width), f32)
    rows_shape = shape((cells, width), bf16)
    cols_shape = shape((width, cells), bf16)
    tall_shape = shape((3 * width, cells), bf16)

    cot_packed = call(pack_kernel, "pack_cotangent", [rows_shape], [pattern_col, cot_rows])[0]
    cot_arrived = exchange(cot_packed)
    grad_att, cot_cols = call(
        lambda *refs: cot_kernel(slots, blocks, *refs),
        "cotangent_products", [cols_shape, cols_shape], [cot_arrived, out_weight],
    )

    beside = rims(fields)
    h, packed = call(
        enter_kernel, "convolve_normalize_pack", [rows_shape, rows_shape],
        [pattern_col, fields, *beside, taps, gain],
        [pad, pltpu.VMEM((cells, width), bf16)],
    )
    arrived = exchange(packed)
    mixed, qkv, probs, att = call(
        lambda *refs: forward_kernel(slots, blocks, 2, *refs),
        "attention_forward",
        [rows_shape, tall_shape, shape((HEADS, GROUP, cells), f32), cols_shape],
        [arrived, qkv_weight_t, out_weight_t, bias],
        flops=5_000_000_000,
    )
    mixed_home = exchange(mixed)
    grad_grouped = call(
        lambda *refs: backward_kernel(slots, blocks, 2, *refs),
        "attention_backward", [rows_shape], [qkv, probs, grad_att, qkv_weight],
        [pltpu.VMEM((3 * width, cells), bf16)],
        flops=10_000_000_000,
    )[0]
    grad_home = exchange(grad_grouped)

    part_rows, part_cols = width // lat_count, width // lon_count
    parts = (lat_count, lon_count, part_cols, part_rows)
    if part_rows % 128 == 0 and part_cols % 16 == 0:
        project = call(project_kernel, "project_gradient", [shape(parts, bf16)], [cot_cols, att])[0]
    else:
        project = call(project_kernel, "project_gradient", [shape((width, width), bf16)], [cot_cols, att])[0]
        project = project.reshape(lon_count, part_cols, lat_count, part_rows).transpose(2, 0, 1, 3)
    project = project.reshape(blocks, part_cols, part_rows)
    project = lax.all_to_all(project, AXES, split_axis=0, concat_axis=0, tiled=True)
    grad_project = jnp.sum(project.astype(f32), axis=0).T * scale_everywhere

    block_out = call(leave_kernel, "block_out", [rows_shape], [pattern_row, mixed_home, h])[0]
    grad_h, sums = call(
        return_kernel, "normalize_back",
        [shape(fields.shape, bf16), shape((16, width), f32)],
        [pattern_row, grad_home, h, cot_rows, gain, fields, *beside],
        [pad, pltpu.VMEM((cells, width), f32)],
    )
    grad_fields = call(
        spread_kernel, "convolve_back", [shape(fields.shape, bf16)],
        [grad_h, *rims(grad_h), taps], [pad],
    )[0]
    sums = total_over_devices(sums) * scale_everywhere
    return (
        block_out.reshape(rows, cols, width),
        grad_fields,
        grad_project,
        sums[:9].reshape(3, 3, width),
        sums[9],
    )


def solution(mesh):
    placed = (
        P("lat", "lon", None),
        P(),
        P(),
        P(),
        P(),
        P(),
        P("lat", "lon", None),
        P("lat", "lon", None),
    )
    return jax.shard_map(
        body,
        mesh=mesh,
        in_specs=placed,
        out_specs=(P("lat", "lon", None), P("lat", "lon", None), P("lat", "lon"), P(), P()),
        check_vma=False,
    )
```

time: 329 us -> 156 us (0.47)
  local copies, waits for them, and re-layouts: 84 us -> 24.4 us
  waiting for transfers between devices: 79.3 us -> 42.4 us
  Pallas kernels: 0 us -> 32.5 us
  other arithmetic: 35.4 us -> 6.05 us
  starting transfers between devices: 55.8 us -> 31.9 us
  blocking collectives: 37.9 us -> 16.3 us
  matrix products: 18.7 us -> 0 us
  between operations: 14.8 us -> 0.97 us
    unnamed x3 -> x0, waiting for transfers between devices: 38.5 us -> none
    psum x1 -> x0, blocking collectives: 37.9 us -> none  [body(): lax.psum((gain_on_device, kernel_local), ('lat', 'lon'))]
    pallas_call x0 -> x9, Pallas kernels: none -> 32.5 us  [call(): pl.pallas_call(kernel, name=name, out_shape=list(out_shape), in_specs=[VM...]
    ppermute x8 -> x11, waiting for transfers between devices: 5.37 us -> 28.7 us  [the longest x5 14.8 us: total_over_devices(): x = x + lax.ppermute(x, axis, swap_pairs(size, bit))]
    all_to_all x8 -> x4, waiting for transfers between devices: 35.4 us -> 13.8 us  [the longest x3 13.8 us: exchange(): lax.all_to_all(sent, AXES, split_axis=0, concat_axis=0, tiled=True)]
    all_to_all x8 -> x4, starting transfers between devices: 34.6 us -> 13.7 us  [the longest x3 10.9 us: exchange(): lax.all_to_all(sent, AXES, split_axis=0, concat_axis=0, tiled=True)]
    dot_general x11 -> x0, matrix products: 18.7 us -> none  [the longest x1 2.6 us: body(): lax.dot_general(attended, cot_g, (((0,), (0,)), ((), ())), preferred_elem...]
    all_to_all x0 -> x1, blocking collectives: none -> 16.3 us  [exchange(): lax.all_to_all(sent, AXES, split_axis=0, concat_axis=0, tiled=True)]
  transfers between devices with their start and end apart: 18 -> 15, of which waited for: 10 -> 7; matrix products, arithmetic and copies ran while one was open for 27% -> 10% of each run, Pallas kernels for 0% -> 7%
where the time goes in v1:
time: 156 us; the launch traced here: 155 us
  waiting for transfers between devices  42.4 us (27%)
  Pallas kernels  32.5 us (21%)
  starting transfers between devices  31.9 us (20%)
  local copies, waits for them, and re-layouts  24.4 us (16%)
  blocking collectives  16.3 us (10%)
  other arithmetic  6.05 us (4%)
    pallas_call x9, Pallas kernels, call(): pl.pallas_call(kernel, name=name, out_shape=list(out_shape), in_specs=[VM...  32.5 us
    unnamed x57, local copies, waits for them, and re-layouts  19.1 us
    all_to_all x1, blocking collectives, exchange(): lax.all_to_all(sent, AXES, split_axis=0, concat_axis=0, tiled=True)  16.3 us
    ppermute x5, waiting for transfers between devices, total_over_devices(): x = x + lax.ppermute(x, axis, swap_pairs(size, bit))  14.8 us
    all_to_all x3, waiting for transfers between devices, exchange(): lax.all_to_all(sent, AXES, split_axis=0, concat_axis=0, tiled=True)  13.8 us
    all_to_all x3, starting transfers between devices, exchange(): lax.all_to_all(sent, AXES, split_axis=0, concat_axis=0, tiled=True)  10.9 us
    ppermute x2, waiting for transfers between devices, rims(): from_left = lax.ppermute(column(field.shape[1] - 1), 'lon', right)  9.77 us
    ppermute x5, starting transfers between devices, total_over_devices(): x = x + lax.ppermute(x, axis, swap_pairs(size, bit))  8.85 us
  transfers between devices with their start and end apart: 15, of which 7 were waited for; matrix products, arithmetic and copies ran while one was open for 10% of the time, Pallas kernels for 7%

profile of v1, /device:TPU:0, one launch (start us, length us, event | category | flops | bytes accessed | tf_op | source)
XLA Modules:
  0.0 154.6 jit_solution(14890757498917849401)
XLA Ops:
  0.6 1.5 select_bitcast_fusion.1
  2.1 2.9 %collective-permute-start = (bf16[32,768]{1,0:T(8,128)(2,1)}, bf16[32,768]{1,0:T(8,128)(2,1)}, u32[]{:S(2)}, u32[]{:S(2)}) collective-permute-start(bf16[32,768]{1,0:T(8,128)(2,1)} %select_bitcast_fusion.1), channel_id=1, source_target_pairs={{0,16},{16,0},{1,17},{17,1},{2,18},{18,2},{3,19},{19,3},{4,20},{20... | collective-permute-start | bytes 147464 | tf_op jit(solution)/shard_map/ppermute | solution.py:275
  5.0 1.5 copy.22.pattern_ref
  6.5 1.0 copy-done.6
  7.5 0.9 copy-done.11
  8.4 0.3 pack_cotangent.1
  8.7 0.7 copy-done.8
  9.5 5.0 %all-to-all-start.2 = ((bf16[32,8,768]{2,1,0:T(8,128)(2,1)}), bf16[32,8,768]{2,1,0:T(8,128)(2,1)}, u32[]{:S(2)}, u32[]{:S(2)}) async-start(bf16[32,8,768]{2,1,0:T(8,128)(2,1)} %bitcast.36), calls=%async_computation.2 | async-start | bytes 786432 | tf_op jit(solution)/shard_map/all_to_all | solution.py:296
  14.5 1.0 fusion
  15.5 0.8 broadcast_select_fusion.2
  16.4 0.6 copy-done.13
  17.0 0.6 copy-done.16
  17.6 0.6 pad_maximum_fusion.2
  18.2 4.2 %collective-permute-start.2 = (bf16[10,768]{1,0:T(8,128)(2,1)}, bf16[10,768]{1,0:T(8,128)(2,1)}, u32[]{:S(2)}, u32[]{:S(2)}) collective-permute-start(bf16[10,768]{1,0:T(8,128)(2,1)} %pad_maximum_fusion.2), channel_id=1, source_target_pairs={{1,0},{2,1},{3,2},{4,3},{5,4},{6,5},{7,6},{8,7},{9,8},{10,9},{11,1... | collective-permute-start | bytes 46088 | tf_op jit(solution)/shard_map/ppermute | solution.py:288
  22.5 0.6 pad_maximum_fusion.1
  23.1 1.4 reshape.64.taps_ref
  24.5 4.9 %collective-permute-done.1.left_ref = bf16[10,768]{1,0:T(8,128)(2,1)} collective-permute-done((bf16[10,768]{1,0:T(8,128)(2,1)}, bf16[10,768]{1,0:T(8,128)(2,1)}, u32[]{:S(2)}, u32[]{:S(2)}) %collective-permute-start.1) | collective-permute-done | bytes 15392 | tf_op jit(solution)/shard_map/ppermute | solution.py:287
  29.4 1.0 copy-done.4
  30.4 0.9 copy-done.12
  31.3 0.8 copy-done.14
  32.1 0.8 copy-done.17
  32.9 0.8 copy-done.19
  33.7 2.3 %convolve_normalize_pack.1 = (bf16[256,768]{1,0:T(8,128)(2,1)S(1)}, bf16[256,768]{1,0:T(8,128)(2,1)S(1)}) custom-call(s32[256,1]{1,0:T(8,128)S(1)} %copy-done.12, bf16[8,32,768]{2,1,0:T(8,128)(2,1)S(1)} %copy-done.4, bf16[32,768]{1,0:T(8,128)(2,1)S(1)} %copy-done.17, bf16[32,768]{1,0:T(8,128)(2,1)S(1)} %copy-done.14, ...), custom_call_target="tpu_custom_call" | custom-call | bytes 1340416 | tf_op jit(solution)/shard_map/convolve_normalize_pack/pallas_call | solution.py:31
  36.0 0.0 copy-start.9
  36.0 0.7 copy-done.9
  36.7 0.7 copy-done.21
  37.5 3.3 %all-to-all-start = ((bf16[32,8,768]{2,1,0:T(8,128)(2,1)}), bf16[32,8,768]{2,1,0:T(8,128)(2,1)}, u32[]{:S(2)}, u32[]{:S(2)}) async-start(bf16[32,8,768]{2,1,0:T(8,128)(2,1)} %bitcast.40), calls=%async_computation | async-start | bytes 786432 | tf_op jit(solution)/shard_map/all_to_all | solution.py:296
  40.8 3.6 %copy.23 = bf16[768,2304]{0,1:T(8,128)(2,1)} copy(bf16[768,2304]{1,0:T(8,128)(2,1)S(1)} %copy-done.1) | data formatting | bytes 7077888 | tf_op args[3]
  44.4 2.4 %copy.25 = f32[24,64,64]{1,2,0:T(8,128)} copy(f32[24,64,64]{2,1,0:T(8,128)} %param.13) | data formatting | bytes 786432 | tf_op args[5]
  46.8 0.6 copy.24
  47.4 1.6 %pad_maximum_fusion.refs_3_ = f32[24,64,128]{2,1,0:T(8,128)S(1)} fusion(f32[24,64,64]{2,1,0:T(8,128)} %bitcast.45), kind=kLoop, calls=%fused_computation.1 | loop fusion | flops 196608 | bytes 1179648 | tf_op jit(solution)/shard_map/concatenate | solution.py:329
  49.1 1.7 %cotangent_products.1 = (bf16[768,256]{1,0:T(8,128)(2,1)S(1)}, bf16[768,256]{1,0:T(8,128)(2,1)S(1)}) custom-call(bf16[256,768]{1,0:T(8,128)(2,1)} %bitcast.15.refs_0_, bf16[768,768]{1,0:T(8,128)(2,1)S(1)} %copy-done), custom_call_target="tpu_custom_call" | custom-call | bytes 2359296 | tf_op jit(solution)/shard_map/cotangent_products/pallas_call | solution.py:31
  50.8 0.7 copy-done.23
  51.5 2.3 %all-to-all-done = bf16[32,8,768]{2,1,0:T(8,128)(2,1)} async-done(((bf16[32,8,768]{2,1,0:T(8,128)(2,1)}), bf16[32,8,768]{2,1,0:T(8,128)(2,1)}, u32[]{:S(2)}, u32[]{:S(2)}) %all-to-all-start) | async-done | bytes 393248 | tf_op jit(solution)/shard_map/all_to_all | solution.py:296
  53.8 2.0 %copy-done.3 = bf16[768,2304]{0,1:T(8,128)(2,1)S(1)} copy-done((bf16[768,2304]{0,1:T(8,128)(2,1)S(1)}, bf16[768,2304]{0,1:T(8,128)(2,1)}, u32[]{:S(2)}) %copy-start.3) | copy-done | bytes 3538968
  55.9 8.9 %attention_forward.1 = (bf16[256,768]{1,0:T(8,128)(2,1)}, bf16[2304,256]{1,0:T(8,128)(2,1)S(1)}, f32[24,64,256]{2,1,0:T(8,128)S(1)}, bf16[768,256]{1,0:T(8,128)(2,1)S(1)}) custom-call(bf16[256,768]{1,0:T(8,128)(2,1)} %bitcast.6.refs_0_, bf16[2304,768]{1,0:T(8,128)(2,1)S(1)} %bitcast.33, bf16[768,768]{1,0:T(8,128)(2,1)S(1)} %bitcast.39, ...), custom_call_target="tpu_custom_call" | custom-call | flops 5000000000 | bytes 9437184 | tf_op jit(solution)/shard_map/attention_forward/pallas_call | solution.py:31
  64.8 12.3 %attention_backward.1 = bf16[256,768]{1,0:T(8,128)(2,1)S(1)} custom-call(bf16[2304,256]{1,0:T(8,128)(2,1)S(1)} %get-tuple-element.18.refs_0_, f32[24,64,256]{2,1,0:T(8,128)S(1)} %get-tuple-element.19.refs_1_, bf16[768,256]{1,0:T(8,128)(2,1)S(1)} %copy-done.24, bf16[768,2304]{1,0:T(8,128)(2,1)S(1)} %copy-done.2), custom_call_target="tpu_custom_call" | custom-call | flops 10000000000 | bytes 7077888 | tf_op jit(solution)/shard_map/attention_backward/pallas_call | solution.py:31
  77.1 16.3 %all_to_all.25 = bf16[32,8,768]{2,1,0:T(8,128)(2,1)S(1)} all-to-all(bf16[32,8,768]{2,1,0:T(8,128)(2,1)S(1)} %bitcast.41), channel_id=1, replica_groups=mesh['lat'=2,'lon'=16] {'lat','lon'}, dimensions={0} | all-to-all | bytes 786432 | tf_op jit(solution)/shard_map/all_to_all | solution.py:296
  93.4 2.6 %all-to-all-start.1 = ((bf16[32,8,768]{2,1,0:T(8,128)(2,1)}), bf16[32,8,768]{2,1,0:T(8,128)(2,1)S(1)}, u32[]{:S(2)}, u32[]{:S(2)}) async-start(bf16[32,8,768]{2,1,0:T(8,128)(2,1)} %bitcast.10), calls=%async_computation.1 | async-start | bytes 786432 | tf_op jit(solution)/shard_map/all_to_all | solution.py:296
  96.0 1.6 %project_gradient.1 = bf16[2,16,48,384]{3,2,1,0:T(8,128)(2,1)} custom-call(bf16[768,256]{1,0:T(8,128)(2,1)S(1)} %get-tuple-element.22.cot_ref, bf16[768,256]{1,0:T(8,128)(2,1)S(1)} %get-tuple-element.23.att_ref), custom_call_target="tpu_custom_call" | custom-call | bytes 1966080 | tf_op jit(solution)/shard_map/project_gradient/pallas_call | solution.py:31
  97.6 11.4 %all-to-all-done.1 = bf16[32,8,768]{2,1,0:T(8,128)(2,1)S(1)} async-done(((bf16[32,8,768]{2,1,0:T(8,128)(2,1)}), bf16[32,8,768]{2,1,0:T(8,128)(2,1)S(1)}, u32[]{:S(2)}, u32[]{:S(2)}) %all-to-all-start.1) | async-done | bytes 393248 | tf_op jit(solution)/shard_map/all_to_all | solution.py:296
  109.1 0.0 copy-start.18
  109.1 0.0 copy-start.22
  109.1 2.8 %all-to-all-start.4 = ((bf16[32,48,384]{2,1,0:T(8,128)(2,1)}), bf16[32,48,384]{2,1,0:T(8,128)(2,1)S(1)}, u32[]{:S(2)}, u32[]{:S(2)}) async-start(bf16[32,48,384]{2,1,0:T(8,128)(2,1)} %bitcast.21), calls=%async_computation.4 | async-start | bytes 2359296 | tf_op jit(solution)/shard_map/all_to_all | solution.py:373
  112.0 2.6 %normalize_back.1 = (bf16[8,32,768]{2,1,0:T(8,128)(2,1)S(1)}, f32[16,768]{1,0:T(8,128)S(1)}) custom-call(s32[1,256]{1,0:T(1,128)S(1)} %bitcast.43, bf16[256,768]{1,0:T(8,128)(2,1)S(1)} %bitcast.38, bf16[256,768]{1,0:T(8,128)(2,1)S(1)} %copy-done.10, bf16[256,768]{1,0:T(8,128)(2,1)S(1)} %bitcast.35, f32[1,768]{1,0:T(1,128)S(1)} %reshape.65.gain_ref, ...), custom_call_target="tpu_custom_call" | custom-call | bytes 2148352 | tf_op jit(solution)/shard_map/normalize_back/pallas_call | solution.py:31
  114.6 0.2 collective-permute-start.6
  114.8 0.2 copy.27
  115.0 1.8 %collective-permute-start.3 = (bf16[32,768]{1,0:T(8,128)(2,1)S(1)}, bf16[32,768]{1,0:T(8,128)(2,1)S(1)}, u32[]{:S(2)}, u32[]{:S(2)}) collective-permute-start(bf16[32,768]{1,0:T(8,128)(2,1)S(1)} %select_bitcast_fusion), channel_id=1, source_target_pairs={{0,16},{16,0},{1,17},{17,1},{2,18},{18,2},{3,19},{19,3},{4,20},{20... | collective-permute-start | bytes 147464 | tf_op jit(solution)/shard_map/ppermute | solution.py:275
  116.8 1.6 %collective-permute-start.7 = (f32[16,768]{1,0:T(8,128)S(1)}, f32[16,768]{1,0:T(8,128)S(1)}, u32[]{:S(2)}, u32[]{:S(2)}) collective-permute-start(f32[16,768]{1,0:T(8,128)S(1)} %add.15), channel_id=1, source_target_pairs={{0,2},{1,3},{2,0},{3,1},{4,6},{5,7},{6,4},{7,5},{8,10},{9,11},{10,... | collective-permute-start | bytes 147464 | tf_op jit(solution)/shard_map/ppermute | solution.py:307
  118.3 4.1 %collective-permute-done.3 = bf16[32,768]{1,0:T(8,128)(2,1)S(1)} collective-permute-done((bf16[32,768]{1,0:T(8,128)(2,1)S(1)}, bf16[32,768]{1,0:T(8,128)(2,1)S(1)}, u32[]{:S(2)}, u32[]{:S(2)}) %collective-permute-start.3) | collective-permute-done | bytes 49184 | tf_op jit(solution)/shard_map/ppermute | solution.py:275
  122.5 0.9 collective-permute-start.8
  123.4 9.4 %collective-permute-done.8 = f32[16,768]{1,0:T(8,128)S(1)} collective-permute-done((f32[16,768]{1,0:T(8,128)S(1)}, f32[16,768]{1,0:T(8,128)S(1)}, u32[]{:S(2)}, u32[]{:S(2)}) %collective-permute-start.8) | collective-permute-done | bytes 49184 | tf_op jit(solution)/shard_map/ppermute | solution.py:307
  132.8 4.7 %collective-permute-start.9 = (f32[16,768]{1,0:T(8,128)S(1)}, f32[16,768]{1,0:T(8,128)S(1)}, u32[]{:S(2)}, u32[]{:S(2)}) collective-permute-start(f32[16,768]{1,0:T(8,128)S(1)} %add.17), channel_id=1, source_target_pairs={{0,8},{1,9},{2,10},{3,11},{4,12},{5,13},{6,14},{7,15},{8,0},{9,1},... | collective-permute-start | bytes 147464 | tf_op jit(solution)/shard_map/ppermute | solution.py:307
  137.5 0.3 collective-permute-start.5
  137.8 5.4 %collective-permute-done.9 = f32[16,768]{1,0:T(8,128)S(1)} collective-permute-done((f32[16,768]{1,0:T(8,128)S(1)}, f32[16,768]{1,0:T(8,128)S(1)}, u32[]{:S(2)}, u32[]{:S(2)}) %collective-permute-start.9) | collective-permute-done | bytes 49184 | tf_op jit(solution)/shard_map/ppermute | solution.py:307
  143.2 1.5 collective-permute-start.10
  144.8 0.1 collective-permute-start.4
  144.8 1.0 block_out.1
  145.9 4.9 %collective-permute-done.4.left_ref = bf16[10,768]{1,0:T(8,128)(2,1)S(1)} collective-permute-done((bf16[10,768]{1,0:T(8,128)(2,1)S(1)}, bf16[10,768]{1,0:T(8,128)(2,1)S(1)}, u32[]{:S(2)}, u32[]{:S(2)}) %collective-permute-start.4) | collective-permute-done | bytes 15392 | tf_op jit(solution)/shard_map/ppermute | solution.py:287
  150.8 1.7 %convolve_back.1 = bf16[8,32,768]{2,1,0:T(8,128)(2,1)} custom-call(bf16[8,32,768]{2,1,0:T(8,128)(2,1)S(1)} %get-tuple-element.21.field_ref, bf16[32,768]{1,0:T(8,128)(2,1)S(1)} %get-tuple-element.34.before_ref, bf16[32,768]{1,0:T(8,128)(2,1)S(1)} %get-tuple-element.33.after_ref, bf16[10,768]{1,0:T(8,128)(2,1)S(1)} %collective-permute-done.4.left_ref, ...), custom_call_target="tpu_custom_call" | custom-call | bytes 943104 | tf_op jit(solution)/shard_map/convolve_back/pallas_call | solution.py:31
  152.5 0.6 reshape.77
  153.1 0.6 slice_reduce_fusion
  153.8 0.2 convert_reduce_fusion
  153.9 0.6 multiply_bitcast_fusion
  (60 shorter events, 0.2 us)
Async XLA Ops:
  2.1 13.4 %collective-permute-start = (bf16[32,768]{1,0:T(8,128)(2,1)}, bf16[32,768]{1,0:T(8,128)(2,1)}, u32[]{:S(2)}, u32[]{:S(2)}) collective-permute-start(bf16[32,768]{1,0:T(8,128)(2,1)} %select_bitcast_fusion.1), channel_id=1, source_target_pairs={{0,16},{16,0},{1,17},{17,1},{2,18},{18,2},{3,19},{19,3},{4,20},{20... | collective-permute-start | bytes 147464 | tf_op jit(solution)/shard_map/ppermute | solution.py:275
  5.0 19.5 %copy-start.25 = (f32[768]{0:T(1024)S(1)}, f32[768]{0:T(1024)}, u32[]{:S(2)}) copy-start(f32[768]{0:T(1024)} %param.10) | copy-start | bytes 9220
  6.5 1.0 copy-start.6
  7.5 0.9 copy-start.11
  8.4 32.4 %copy-start.1 = (bf16[768,2304]{1,0:T(8,128)(2,1)S(1)}, bf16[768,2304]{1,0:T(8,128)(2,1)}, u32[]{:S(2)}) copy-start(bf16[768,2304]{1,0:T(8,128)(2,1)} %refs_3_.1) | copy-start | bytes 10616836
  8.7 0.7 copy-start.8
  9.5 28.0 %all-to-all-start.2 = ((bf16[32,8,768]{2,1,0:T(8,128)(2,1)}), bf16[32,8,768]{2,1,0:T(8,128)(2,1)}, u32[]{:S(2)}, u32[]{:S(2)}) async-start(bf16[32,8,768]{2,1,0:T(8,128)(2,1)} %bitcast.36), calls=%async_computation.2 | async-start | bytes 786432 | tf_op jit(solution)/shard_map/all_to_all | solution.py:296
  16.4 0.6 copy-start.13
  17.0 0.6 copy-start.16
  18.2 6.3 %collective-permute-start.2 = (bf16[10,768]{1,0:T(8,128)(2,1)}, bf16[10,768]{1,0:T(8,128)(2,1)}, u32[]{:S(2)}, u32[]{:S(2)}) collective-permute-start(bf16[10,768]{1,0:T(8,128)(2,1)} %pad_maximum_fusion.2), channel_id=1, source_target_pairs={{1,0},{2,1},{3,2},{4,3},{5,4},{6,5},{7,6},{8,7},{9,8},{10,9},{11,1... | collective-permute-start | bytes 46088 | tf_op jit(solution)/shard_map/ppermute | solution.py:288
  23.1 6.3 %collective-permute-start.1 = (bf16[10,768]{1,0:T(8,128)(2,1)}, bf16[10,768]{1,0:T(8,128)(2,1)}, u32[]{:S(2)}, u32[]{:S(2)}) collective-permute-start(bf16[10,768]{1,0:T(8,128)(2,1)} %pad_maximum_fusion.1), channel_id=1, source_target_pairs={{0,1},{1,2},{2,3},{3,4},{4,5},{5,6},{6,7},{7,8},{8,9},{9,10},{10,1... | collective-permute-start | bytes 46088 | tf_op jit(solution)/shard_map/ppermute | solution.py:287
  29.4 1.0 copy-start.4
  30.4 0.9 copy-start.12
  31.3 0.8 copy-start.14
  32.1 0.8 copy-start.17
  32.9 0.8 copy-start.19
  36.0 0.7 copy-start.9
  36.7 0.7 copy-start.21
  37.5 16.4 %all-to-all-start = ((bf16[32,8,768]{2,1,0:T(8,128)(2,1)}), bf16[32,8,768]{2,1,0:T(8,128)(2,1)}, u32[]{:S(2)}, u32[]{:S(2)}) async-start(bf16[32,8,768]{2,1,0:T(8,128)(2,1)} %bitcast.40), calls=%async_computation | async-start | bytes 786432 | tf_op jit(solution)/shard_map/all_to_all | solution.py:296
  44.4 2.4 %copy-start = (bf16[768,768]{1,0:T(8,128)(2,1)S(1)}, bf16[768,768]{1,0:T(8,128)(2,1)}, u32[]{:S(2)}) copy-start(bf16[768,768]{1,0:T(8,128)(2,1)} %refs_1_.1) | copy-start | bytes 3538948
  50.8 0.8 copy-start.23
  53.8 2.0 %copy-start.3 = (bf16[768,2304]{0,1:T(8,128)(2,1)S(1)}, bf16[768,2304]{0,1:T(8,128)(2,1)}, u32[]{:S(2)}) copy-start(bf16[768,2304]{0,1:T(8,128)(2,1)} %copy.23) | copy-start | bytes 10616836
  55.8 8.9 %copy-start.2 = (bf16[768,2304]{1,0:T(8,128)(2,1)S(1)}, bf16[768,2304]{1,0:T(8,128)(2,1)}, u32[]{:S(2)}) copy-start(bf16[768,2304]{1,0:T(8,128)(2,1)} %refs_3_.1) | copy-start | bytes 10616836
  55.9 8.9 %copy-start.24 = (bf16[768,256]{1,0:T(8,128)(2,1)S(1)}, bf16[768,256]{1,0:T(8,128)(2,1)}, u32[]{:S(2)}) copy-start(bf16[768,256]{1,0:T(8,128)(2,1)} %copy-done.23) | copy-start | bytes 1179652
  93.4 15.7 %all-to-all-start.1 = ((bf16[32,8,768]{2,1,0:T(8,128)(2,1)}), bf16[32,8,768]{2,1,0:T(8,128)(2,1)S(1)}, u32[]{:S(2)}, u32[]{:S(2)}) async-start(bf16[32,8,768]{2,1,0:T(8,128)(2,1)} %bitcast.10), calls=%async_computation.1 | async-start | bytes 786432 | tf_op jit(solution)/shard_map/all_to_all | solution.py:296
  109.1 2.8 %copy-start.5 = (bf16[8,32,768]{2,1,0:T(8,128)(2,1)S(1)}, bf16[8,32,768]{2,1,0:T(8,128)(2,1)}, u32[]{:S(2)}) copy-start(bf16[8,32,768]{2,1,0:T(8,128)(2,1)} %field_ref.3) | copy-start | bytes 1179652
  109.1 2.9 %copy-start.7 = (bf16[8,32,768]{2,1,0:T(8,128)(2,1)S(1)}, bf16[8,32,768]{2,1,0:T(8,128)(2,1)}, u32[]{:S(2)}) copy-start(bf16[8,32,768]{2,1,0:T(8,128)(2,1)} %param.15) | copy-start | bytes 1179652
  109.1 2.9 %copy-start.10 = (bf16[256,768]{1,0:T(8,128)(2,1)S(1)}, bf16[256,768]{1,0:T(8,128)(2,1)}, u32[]{:S(2)}) copy-start(bf16[256,768]{1,0:T(8,128)(2,1)} %copy-done.9) | copy-start | bytes 1179652
  109.1 2.9 %copy-start.15 = (bf16[32,768]{1,0:T(8,128)(2,1)S(1)}, bf16[32,768]{1,0:T(8,128)(2,1)}, u32[]{:S(2)}) copy-start(bf16[32,768]{1,0:T(8,128)(2,1)} %copy-done.13) | copy-start | bytes 147460
  109.1 2.9 %copy-start.18 = (bf16[32,768]{1,0:T(8,128)(2,1)S(1)}, bf16[32,768]{1,0:T(8,128)(2,1)}, u32[]{:S(2)}) copy-start(bf16[32,768]{1,0:T(8,128)(2,1)} %copy-done.16) | copy-start | bytes 147460
  109.1 2.9 %copy-start.22 = (s32[1,1,256]{2,1,0:T(1,128)S(1)}, s32[1,1,256]{2,1,0:T(1,128)}, u32[]{:S(2)}) copy-start(s32[1,1,256]{2,1,0:T(1,128)} %param.14) | copy-start | bytes 3076
  109.1 44.6 %all-to-all-start.4 = ((bf16[32,48,384]{2,1,0:T(8,128)(2,1)}), bf16[32,48,384]{2,1,0:T(8,128)(2,1)S(1)}, u32[]{:S(2)}, u32[]{:S(2)}) async-start(bf16[32,48,384]{2,1,0:T(8,128)(2,1)} %bitcast.21), calls=%async_computation.4 | async-start | bytes 2359296 | tf_op jit(solution)/shard_map/all_to_all | solution.py:373
  114.6 2.2 %collective-permute-start.6 = (f32[16,768]{1,0:T(8,128)S(1)}, f32[16,768]{1,0:T(8,128)S(1)}, u32[]{:S(2)}, u32[]{:S(2)}) collective-permute-start(f32[16,768]{1,0:T(8,128)S(1)} %get-tuple-element.24), channel_id=1, source_target_pairs={{0,1},{1,0},{2,3},{3,2},{4,5},{5,4},{6,7},{7,6},{8,9},{9,8},{10,11... | collective-permute-start | bytes 147464 | tf_op jit(solution)/shard_map/ppermute | solution.py:307
  115.0 35.8 %copy-start.20 = (f32[9,768]{1,0:T(8,128)S(1)}, f32[9,768]{1,0:T(8,128)}, u32[]{:S(2)}) copy-start(f32[9,768]{1,0:T(8,128)} %reshape.64.taps_ref) | copy-start | bytes 82948
  115.0 7.4 %collective-permute-start.3 = (bf16[32,768]{1,0:T(8,128)(2,1)S(1)}, bf16[32,768]{1,0:T(8,128)(2,1)S(1)}, u32[]{:S(2)}, u32[]{:S(2)}) collective-permute-start(bf16[32,768]{1,0:T(8,128)(2,1)S(1)} %select_bitcast_fusion), channel_id=1, source_target_pairs={{0,16},{16,0},{1,17},{17,1},{2,18},{18,2},{3,19},{19,3},{4,20},{20... | collective-permute-start | bytes 147464 | tf_op jit(solution)/shard_map/ppermute | solution.py:275
  116.8 5.7 %collective-permute-start.7 = (f32[16,768]{1,0:T(8,128)S(1)}, f32[16,768]{1,0:T(8,128)S(1)}, u32[]{:S(2)}, u32[]{:S(2)}) collective-permute-start(f32[16,768]{1,0:T(8,128)S(1)} %add.15), channel_id=1, source_target_pairs={{0,2},{1,3},{2,0},{3,1},{4,6},{5,7},{6,4},{7,5},{8,10},{9,11},{10,... | collective-permute-start | bytes 147464 | tf_op jit(solution)/shard_map/ppermute | solution.py:307
  122.5 10.3 %collective-permute-start.8 = (f32[16,768]{1,0:T(8,128)S(1)}, f32[16,768]{1,0:T(8,128)S(1)}, u32[]{:S(2)}, u32[]{:S(2)}) collective-permute-start(f32[16,768]{1,0:T(8,128)S(1)} %add.16), channel_id=1, source_target_pairs={{0,4},{1,5},{2,6},{3,7},{4,0},{5,1},{6,2},{7,3},{8,12},{9,13},{10,... | collective-permute-start | bytes 147464 | tf_op jit(solution)/shard_map/ppermute | solution.py:307
  132.8 10.4 %collective-permute-start.9 = (f32[16,768]{1,0:T(8,128)S(1)}, f32[16,768]{1,0:T(8,128)S(1)}, u32[]{:S(2)}, u32[]{:S(2)}) collective-permute-start(f32[16,768]{1,0:T(8,128)S(1)} %add.17), channel_id=1, source_target_pairs={{0,8},{1,9},{2,10},{3,11},{4,12},{5,13},{6,14},{7,15},{8,0},{9,1},... | collective-permute-start | bytes 147464 | tf_op jit(solution)/shard_map/ppermute | solution.py:307
  137.5 8.4 %collective-permute-start.5 = (bf16[10,768]{1,0:T(8,128)(2,1)S(1)}, bf16[10,768]{1,0:T(8,128)(2,1)S(1)}, u32[]{:S(2)}, u32[]{:S(2)}) collective-permute-start(bf16[10,768]{1,0:T(8,128)(2,1)S(1)} %pad_maximum_fusion.4), channel_id=1, source_target_pairs={{1,0},{2,1},{3,2},{4,3},{5,4},{6,5},{7,6},{8,7},{9,8},{10,9},{11,1... | collective-permute-start | bytes 46088 | tf_op jit(solution)/shard_map/ppermute | solution.py:288
  143.2 9.3 %collective-permute-start.10 = (f32[16,768]{1,0:T(8,128)S(1)}, f32[16,768]{1,0:T(8,128)S(1)}, u32[]{:S(2)}, u32[]{:S(2)}) collective-permute-start(f32[16,768]{1,0:T(8,128)S(1)} %add.18), channel_id=1, source_target_pairs={{0,16},{16,0},{1,17},{17,1},{2,18},{18,2},{3,19},{19,3},{4,20},{20... | collective-permute-start | bytes 147464 | tf_op jit(solution)/shard_map/ppermute | solution.py:307
  144.8 6.0 %collective-permute-start.4 = (bf16[10,768]{1,0:T(8,128)(2,1)S(1)}, bf16[10,768]{1,0:T(8,128)(2,1)S(1)}, u32[]{:S(2)}, u32[]{:S(2)}) collective-permute-start(bf16[10,768]{1,0:T(8,128)(2,1)S(1)} %pad_maximum_fusion.3), channel_id=1, source_target_pairs={{0,1},{1,2},{2,3},{3,4},{4,5},{5,6},{6,7},{7,8},{8,9},{9,10},{10,1... | collective-permute-start | bytes 46088 | tf_op jit(solution)/shard_map/ppermute | solution.py:287

commit v2 on v1

--- a/solution.py
+++ b/solution.py
@@ -12,6 +12,8 @@
 GROUP = 64
 PAIR = 2 * GROUP
 EDGE = 8
+UNROLL_F = 4
+UNROLL_B = 4
 
 epsilon = 1e-05
 f32, bf16 = jnp.float32, jnp.bfloat16
@@ -20,20 +22,28 @@
 NT = (((1,), (1,)), ((), ()))
 TN = (((0,), (0,)), ((), ()))
 VMEM = pl.BlockSpec(memory_space=pltpu.VMEM)
+SMEM = pl.BlockSpec(memory_space=pltpu.SMEM)
+ANY = pl.BlockSpec(memory_space=pl.ANY)
 
 
 def dot(a, b, dims=NN):
     return lax.dot_general(a, b, dims, preferred_element_type=f32)
 
 
-def call(kernel, name, out_shape, operands, scratch=(), flops=0):
+def whole(x):
+    return pl.BlockSpec(x.shape, lambda step: (0,) * len(x.shape))
+
+
+def call(kernel, name, out_shape, operands, scratch=(), flops=0, specs=()):
     size = sum(math.prod(x.shape) * x.dtype.itemsize for x in (*operands, *out_shape))
+    specs = dict(specs)
     return pl.pallas_call(
         kernel,
         name=name,
+        grid=(1,),
         out_shape=list(out_shape),
-        in_specs=[VMEM] * len(operands),
-        out_specs=[VMEM] * len(out_shape),
+        in_specs=[specs.get(i, whole(x)) for i, x in enumerate(operands)],
+        out_specs=[whole(x) for x in out_shape],
         scratch_shapes=list(scratch),
         compiler_params=pltpu.CompilerParams(vmem_limit_bytes=40 * 1024 * 1024),
         cost_estimate=pl.CostEstimate(flops=flops, bytes_accessed=size, transcendentals=0),
@@ -47,11 +57,6 @@
 def by_cell(pattern_row, cells):
     cell = lax.broadcasted_iota(jnp.int32, (cells, cells), 0)
     return jnp.where(pattern_row == cell, 1.0, 0.0).astype(bf16)
-
-
-def by_slot(pattern_col, cells):
-    cell = lax.broadcasted_iota(jnp.int32, (cells, cells), 1)
-    return jnp.where(pattern_col == cell, 1.0, 0.0).astype(bf16)
 
 
 def position_by_row(cells, slots, blocks, row_dim):
@@ -63,7 +68,7 @@
 
 def pack_kernel(pattern_ref, rows_ref, out_ref):
     cells = rows_ref.shape[0]
-    out_ref[...] = dot(by_slot(pattern_ref[...], cells), rows_ref[...]).astype(bf16)
+    out_ref[...] = dot(by_cell(pattern_ref[...], cells), rows_ref[...], TN).astype(bf16)
 
 
 def fill_pad(pad, field_ref, before_ref, after_ref, left_ref, right_ref):
@@ -82,8 +87,8 @@
     summed = pad[row + 1, EDGE : EDGE + cols]
     for a in range(3):
         for b in range(3):
-            at = 3 * (2 - a) + 2 - b if flip else 3 * a + b
-            summed = summed + taps[at : at + 1] * pad[row + a, EDGE - 1 + b : EDGE - 1 + b + cols]
+            tap = taps[2 - a, 2 - b : 3 - b] if flip else taps[a, b : b + 1]
+            summed = summed + tap * pad[row + a, EDGE - 1 + b : EDGE - 1 + b + cols]
     return summed
 
 
@@ -107,7 +112,7 @@
         h_ref[row * cols : (row + 1) * cols] = h
         xhat, _ = normalized(h.astype(f32))
         normed[row * cols : (row + 1) * cols] = (xhat * gain).astype(bf16)
-    out_ref[...] = dot(by_slot(pattern_ref[...], rows * cols), normed[...]).astype(bf16)
+    out_ref[...] = dot(by_cell(pattern_ref[...], rows * cols), normed[...], TN).astype(bf16)
 
 
 def cot_kernel(slots, blocks, arrived_ref, out_weight_ref, grad_att_ref, cot_ref):
@@ -135,33 +140,47 @@
 def forward_kernel(
     slots, blocks, unroll,
     arrived_ref, qkv_weight_t_ref, out_weight_t_ref, bias_ref,
-    mixed_ref, qkv_ref, probs_ref, att_ref,
+    mixed_ref, qkv_ref, probs_ref, att_ref, weight, sems,
 ):
     cells, width = arrived_ref.shape
+    step = width // 2
+    copies = [
+        pltpu.make_async_copy(
+            qkv_weight_t_ref.at[at : at + step], weight.at[at : at + step], sems.at[at // step]
+        )
+        for at in range(0, 3 * width, step)
+    ]
+    for copy in copies:
+        copy.start()
     grouped = dot(position_by_row(cells, slots, blocks, 1), arrived_ref[...]).astype(bf16)
-    step = width // 2
-    for at in range(0, 3 * width, step):
-        qkv_ref[at : at + step] = dot(qkv_weight_t_ref[at : at + step], grouped, NT).astype(bf16)
+    for at, copy in zip(range(0, 3 * width, step), copies):
+        copy.wait()
+        qkv_ref[at : at + step] = dot(weight[at : at + step], grouped, NT).astype(bf16)
     scale = HEAD_DIM ** (-0.5)
 
-    def head(e):
-        at = pl.multiple_of(e * HEAD_DIM, HEAD_DIM)
-        rows = pl.ds(at, HEAD_DIM)
-        bias = bias_ref[e]
-        for pair in range(cells // PAIR):
-            lanes = slice(pair * PAIR, (pair + 1) * PAIR)
-            q = qkv_ref[rows, lanes]
-            k = qkv_ref[pl.ds(width + at, HEAD_DIM), lanes]
-            v = qkv_ref[pl.ds(2 * width + at, HEAD_DIM), lanes]
-            scores = pair_scores(k, q) * scale + bias
-            lifted = jnp.exp(scores - jnp.max(scores, axis=0, keepdims=True))
-            probs = lifted / jnp.sum(lifted, axis=0, keepdims=True)
-            probs_ref[e, :, lanes] = probs
-            att_ref[rows, lanes] = dot(v, pair_diagonal(probs).astype(bf16)).astype(bf16)
-
     def heads(step, carry):
-        for u in range(unroll):
-            head(step * unroll + u)
+        some = [
+            (step * unroll + u, slice(pair * PAIR, (pair + 1) * PAIR))
+            for u in range(unroll)
+            for pair in range(cells // PAIR)
+        ]
+
+        def rows(part, e):
+            return pl.ds(pl.multiple_of(part * width + e * HEAD_DIM, HEAD_DIM), HEAD_DIM)
+
+        scores = [
+            pair_scores(qkv_ref[rows(1, e), at], qkv_ref[rows(0, e), at]) * scale + bias_ref[e]
+            for e, at in some
+        ]
+        lifted = [jnp.exp(x - jnp.max(x, axis=0, keepdims=True)) for x in scores]
+        probs = [x / jnp.sum(x, axis=0, keepdims=True) for x in lifted]
+        att = [
+            dot(qkv_ref[rows(2, e), at], pair_diagonal(x).astype(bf16))
+            for (e, at), x in zip(some, probs)
+        ]
+        for (e, at), x, y in zip(some, probs, att):
+            probs_ref[e, :, at] = x
+            att_ref[rows(0, e), at] = y.astype(bf16)
         return carry
 
     lax.fori_loop(0, HEADS // unroll, heads, 0)
@@ -177,25 +196,39 @@
     cells, width = out_ref.shape
     scale = HEAD_DIM ** (-0.5)
 
-    def head(e):
-        at = pl.multiple_of(e * HEAD_DIM, HEAD_DIM)
-        rows = pl.ds(at, HEAD_DIM)
-        key_rows, value_rows = pl.ds(width + at, HEAD_DIM), pl.ds(2 * width + at, HEAD_DIM)
-        for pair in range(cells // PAIR):
-            lanes = slice(pair * PAIR, (pair + 1) * PAIR)
-            q, k, v = qkv_ref[rows, lanes], qkv_ref[key_rows, lanes], qkv_ref[value_rows, lanes]
-            grad = grad_att_ref[rows, lanes]
-            probs = probs_ref[e, :, lanes]
-            grad_probs = pair_scores(v, grad)
-            dropped = jnp.sum(probs * grad_probs, axis=0, keepdims=True)
-            grad_scores = pair_diagonal(probs * (grad_probs - dropped)).astype(bf16)
-            grad_qkv[rows, lanes] = (dot(k, grad_scores) * scale).astype(bf16)
-            grad_qkv[key_rows, lanes] = (dot(q, grad_scores, NT) * scale).astype(bf16)
-            grad_qkv[value_rows, lanes] = dot(grad, pair_diagonal(probs).astype(bf16), NT).astype(bf16)
-
     def heads(step, carry):
-        for u in range(unroll):
-            head(step * unroll + u)
+        some = [
+            (step * unroll + u, slice(pair * PAIR, (pair + 1) * PAIR))
+            for u in range(unroll)
+            for pair in range(cells // PAIR)
+        ]
+
+        def rows(part, e):
+            return pl.ds(pl.multiple_of(part * width + e * HEAD_DIM, HEAD_DIM), HEAD_DIM)
+
+        grads = [grad_att_ref[rows(0, e), at] for e, at in some]
+        probs = [probs_ref[e, :, at] for e, at in some]
+        grad_probs = [
+            pair_scores(qkv_ref[rows(2, e), at], grad) for (e, at), grad in zip(some, grads)
+        ]
+        to_value = [
+            dot(grad, pair_diagonal(x).astype(bf16), NT) for grad, x in zip(grads, probs)
+        ]
+        grad_scores = []
+        for x, y in zip(probs, grad_probs):
+            product = x * y
+            z = product - x * jnp.sum(product, axis=0, keepdims=True)
+            grad_scores.append(pair_diagonal(z).astype(bf16))
+        to_query = [
+            dot(qkv_ref[rows(1, e), at], x) * scale for (e, at), x in zip(some, grad_scores)
+        ]
+        to_key = [
+            dot(qkv_ref[rows(0, e), at], x, NT) * scale for (e, at), x in zip(some, grad_scores)
+        ]
+        for (e, at), x, y, z in zip(some, to_query, to_key, to_value):
+            grad_qkv[rows(0, e), at] = x.astype(bf16)
+            grad_qkv[rows(1, e), at] = y.astype(bf16)
+            grad_qkv[rows(2, e), at] = z.astype(bf16)
         return carry
 
     lax.fori_loop(0, HEADS // unroll, heads, 0)
@@ -204,14 +237,23 @@
 
 
 def project_kernel(cot_ref, att_ref, out_ref):
-    if out_ref.ndim == 2:
-        out_ref[...] = dot(cot_ref[...], att_ref[...], NT).astype(bf16)
-        return
-    lats, lons, cols, rows = out_ref.shape
+    out_ref[...] = dot(cot_ref[...], att_ref[...], NT).astype(bf16)
+
+
+def project_halves_kernel(core_ref, cot_ref, att_ref, kept_ref, sent_ref, part):
+    lats, chips, cols, rows = kept_ref.shape
+    core = core_ref[0]
     for a in range(lats):
-        part = dot(cot_ref[...], att_ref[a * rows : (a + 1) * rows], NT).astype(bf16)
-        for b in range(lons):
-            out_ref[a, b] = part[b * cols : (b + 1) * cols]
+        part[...] = dot(cot_ref[...], att_ref[a * rows : (a + 1) * rows], NT).astype(bf16)
+        for chip in range(chips):
+            kept_ref[a, chip] = part[pl.ds(pl.multiple_of((2 * chip + core) * cols, 16), cols)]
+            sent_ref[a, chip] = part[pl.ds(pl.multiple_of((2 * chip + 1 - core) * cols, 16), cols)]
+
+
+def join_halves_kernel(lat_ref, kept_ref, met_ref, out_ref, sent_ref):
+    lat = lat_ref[0]
+    out_ref[...] = (kept_ref[lat].astype(f32) + met_ref[lat].astype(f32)).astype(bf16)
+    sent_ref[...] = (kept_ref[1 - lat].astype(f32) + met_ref[1 - lat].astype(f32)).astype(bf16)
 
 
 def leave_kernel(pattern_ref, mixed_ref, h_ref, out_ref):
@@ -220,9 +262,9 @@
 
 
 def return_kernel(
-    pattern_ref, arrived_ref, h_ref, cot_ref, gain_ref,
+    lat_ref, pattern_ref, arrived_ref, h_ref, cot_ref, gain_ref,
     field_ref, before_ref, after_ref, left_ref, right_ref,
-    grad_ref, sums_ref, pad, normed_grad,
+    grad_ref, sums_ref, message_ref, pad, normed_grad,
 ):
     rows, cols, width = field_ref.shape
     fill_pad(pad, field_ref, before_ref, after_ref, left_ref, right_ref)
@@ -251,6 +293,12 @@
     for i in range(10):
         sums_ref[i : i + 1] = jnp.sum(sums[i], axis=0, keepdims=True)
     sums_ref[10:16] = jnp.zeros((6, width), f32)
+    low = lat_ref[0] == 0
+    message_ref[:cols] = jnp.where(low, grad_ref[rows - 1], grad_ref[0])
+    total = sums_ref[...]
+    high = total.astype(bf16)
+    message_ref[cols : cols + 16] = high
+    message_ref[cols + 16 :] = (total - high.astype(f32)).astype(bf16)
 
 
 def spread_kernel(
@@ -267,12 +315,13 @@
     return [(i, i ^ bit) for i in range(size)]
 
 
-def rims(field):
+def rims(field, met=None):
     lat_count, lon_count = lax.axis_size("lat"), lax.axis_size("lon")
     first, last = field[0], field[-1]
     if lat_count == 2:
         low = lax.axis_index("lat") == 0
-        met = lax.ppermute(jnp.where(low, last, first), "lat", [(0, 1), (1, 0)])
+        if met is None:
+            met = lax.ppermute(jnp.where(low, last, first), "lat", swap_pairs(2, 1))
         none = jnp.zeros_like(met)
         before, after = jnp.where(low, none, met), jnp.where(low, met, none)
     else:
@@ -296,16 +345,45 @@
     return lax.all_to_all(sent, AXES, split_axis=0, concat_axis=0, tiled=True).reshape(cells, width)
 
 
-def total_over_devices(x):
-    for axis in ("lon", "lat"):
-        size = lax.axis_size(axis)
-        if size & (size - 1):
-            x = lax.psum(x, axis)
-            continue
-        bit = 1
-        while bit < size:
-            x = x + lax.ppermute(x, axis, swap_pairs(size, bit))
-            bit *= 2
+def scattered_project(cot_cols, att):
+    width = att.shape[0]
+    lat_count, lon_count = lax.axis_size("lat"), lax.axis_size("lon")
+    rows, cols = width // lat_count, width // lon_count
+    if lat_count != 2 or lon_count % 2 or rows % 128 or cols % 16:
+        parts = call(project_kernel, "project_gradient", [shape((width, width), bf16)], [cot_cols, att])[0]
+        parts = parts.reshape(lon_count, cols, lat_count, rows).transpose(2, 0, 1, 3)
+        parts = parts.reshape(lat_count * lon_count, cols, rows)
+        parts = lax.all_to_all(parts, AXES, split_axis=0, concat_axis=0, tiled=True)
+        return jnp.sum(parts.astype(f32), axis=0).T
+    chips = lon_count // 2
+    lat, lon = lax.axis_index("lat").reshape(1), lax.axis_index("lon").reshape(1)
+    halves = shape((lat_count, chips, cols, rows), bf16)
+    quarters = shape((chips, cols, rows), bf16)
+    kept, sent = call(
+        project_halves_kernel, "project_gradient", [halves, halves],
+        [lax.rem(lon, 2), cot_cols, att], [pltpu.VMEM((width, rows), bf16)], specs={0: SMEM},
+    )
+    met = lax.ppermute(sent, "lon", swap_pairs(lon_count, 1))
+    kept, sent = call(
+        join_halves_kernel, "project_join", [quarters, quarters], [lat, kept, met], specs={0: SMEM}
+    )
+    met = lax.ppermute(sent, "lat", swap_pairs(2, 1))
+    parts = (kept.astype(f32) + met.astype(f32)).astype(bf16)
+    groups = [[2 * chip + core for chip in range(chips)] for core in range(2)]
+    parts = lax.all_to_all(
+        parts, "lon", split_axis=0, concat_axis=0, axis_index_groups=groups, tiled=True
+    )
+    return jnp.sum(parts.astype(f32), axis=0).T
+
+
+def total_over(axis, x, first=1, end=None):
+    size = lax.axis_size(axis)
+    if size & (size - 1):
+        return lax.psum(x, axis) if end is None else x
+    bit = first
+    while bit < (end or size):
+        x = x + lax.ppermute(x, axis, swap_pairs(size, bit))
+        bit *= 2
     return x
 
 
@@ -319,9 +397,7 @@
     slots = cells // blocks
     scale_everywhere = 1.0 / math.sqrt(cells * blocks)
     pattern_row = pattern.reshape(1, cells)
-    pattern_col = pattern.reshape(cells, 1)
     gain = layer_norm_gain.reshape(1, width)
-    taps = conv_kernel.reshape(9, width)
     cot_rows = cotangent.reshape(cells, width)
     qkv_weight_t = qkv_weight.T
     out_weight_t = out_weight.T
@@ -332,7 +408,7 @@
     cols_shape = shape((width, cells), bf16)
     tall_shape = shape((3 * width, cells), bf16)
 
-    cot_packed = call(pack_kernel, "pack_cotangent", [rows_shape], [pattern_col, cot_rows])[0]
+    cot_packed = call(pack_kernel, "pack_cotangent", [rows_shape], [pattern_row, cot_rows])[0]
     cot_arrived = exchange(cot_packed)
     grad_att, cot_cols = call(
         lambda *refs: cot_kernel(slots, blocks, *refs),
@@ -342,49 +418,55 @@
     beside = rims(fields)
     h, packed = call(
         enter_kernel, "convolve_normalize_pack", [rows_shape, rows_shape],
-        [pattern_col, fields, *beside, taps, gain],
+        [pattern_row, fields, *beside, conv_kernel, gain],
         [pad, pltpu.VMEM((cells, width), bf16)],
     )
     arrived = exchange(packed)
     mixed, qkv, probs, att = call(
-        lambda *refs: forward_kernel(slots, blocks, 2, *refs),
+        lambda *refs: forward_kernel(slots, blocks, UNROLL_F, *refs),
         "attention_forward",
         [rows_shape, tall_shape, shape((HEADS, GROUP, cells), f32), cols_shape],
         [arrived, qkv_weight_t, out_weight_t, bias],
+        [pltpu.VMEM((3 * width, width), bf16), pltpu.SemaphoreType.DMA((6,))],
         flops=5_000_000_000,
-    )
-    mixed_home = exchange(mixed)
+        specs={1: ANY},
+    )
     grad_grouped = call(
-        lambda *refs: backward_kernel(slots, blocks, 2, *refs),
+        lambda *refs: backward_kernel(slots, blocks, UNROLL_B, *refs),
         "attention_backward", [rows_shape], [qkv, probs, grad_att, qkv_weight],
         [pltpu.VMEM((3 * width, cells), bf16)],
         flops=10_000_000_000,
     )[0]
     grad_home = exchange(grad_grouped)
-
-    part_rows, part_cols = width // lat_count, width // lon_count
-    parts = (lat_count, lon_count, part_cols, part_rows)
-    if part_rows % 128 == 0 and part_cols % 16 == 0:
-        project = call(project_kernel, "project_gradient", [shape(parts, bf16)], [cot_cols, att])[0]
+    grad_home, mixed = lax.optimization_barrier((grad_home, mixed))
+    mixed_home = exchange(mixed)
+
+    grad_project = scattered_project(cot_cols, att) * scale_everywhere
+
+    block_out = call(leave_kernel, "block_out", [rows_shape], [pattern_row, mixed_home, h])[0]
+    grad_h, sums, message = call(
+        return_kernel, "normalize_back",
+        [shape(fields.shape, bf16), shape((16, width), f32), shape((cols + 32, width), bf16)],
+        [
+            lax.axis_index("lat").reshape(1), pattern_row, grad_home, h, cot_rows, gain,
+            fields, *beside,
+        ],
+        [pad, pltpu.VMEM((cells, width), f32)], specs={0: SMEM},
+    )
+    if lat_count == 2:
+        met = lax.ppermute(message, "lat", swap_pairs(2, 1))
+        sums = sums + met[cols : cols + 16].astype(f32) + met[cols + 16 :].astype(f32)
+        beside = rims(grad_h, met[:cols])
     else:
-        project = call(project_kernel, "project_gradient", [shape((width, width), bf16)], [cot_cols, att])[0]
-        project = project.reshape(lon_count, part_cols, lat_count, part_rows).transpose(2, 0, 1, 3)
-    project = project.reshape(blocks, part_cols, part_rows)
-    project = lax.all_to_all(project, AXES, split_axis=0, concat_axis=0, tiled=True)
-    grad_project = jnp.sum(project.astype(f32), axis=0).T * scale_everywhere
-
-    block_out = call(leave_kernel, "block_out", [rows_shape], [pattern_row, mixed_home, h])[0]
-    grad_h, sums = call(
-        return_kernel, "normalize_back",
-        [shape(fields.shape, bf16), shape((16, width), f32)],
-        [pattern_row, grad_home, h, cot_rows, gain, fields, *beside],
-        [pad, pltpu.VMEM((cells, width), f32)],
-    )
+        sums = total_over("lat", sums)
+        beside = rims(grad_h)
+    sums = total_over("lon", sums, 1, 4)
+    sums, *beside = lax.optimization_barrier((sums, *beside))
+    sums = total_over("lon", sums, 4) * scale_everywhere
     grad_fields = call(
         spread_kernel, "convolve_back", [shape(fields.shape, bf16)],
-        [grad_h, *rims(grad_h), taps], [pad],
+        [grad_h, *beside, conv_kernel], [pad],
     )[0]
-    sums = total_over_devices(sums) * scale_everywhere
     return (
         block_out.reshape(rows, cols, width),
         grad_fields,

time: 156 us -> 125 us (0.80)
  blocking collectives: 16.3 us -> 0 us
  Pallas kernels: 32.5 us -> 23.9 us
  local copies, waits for them, and re-layouts: 24.4 us -> 18.8 us
  starting transfers between devices: 31.9 us -> 35.5 us
  waiting for transfers between devices: 42.4 us -> 38.9 us
    all_to_all x1 -> x0, blocking collectives: 16.3 us -> none  [exchange(): lax.all_to_all(sent, AXES, split_axis=0, concat_axis=0, tiled=True)]
    pallas_call x9 -> x10, Pallas kernels: 32.5 us -> 23.9 us  [call(): pl.pallas_call(kernel, name=name, grid=(1,), out_shape=list(out_shape), i...]
    ppermute x7 -> x8, starting transfers between devices: 13.5 us -> 8.01 us  [the longest x1 2.94 us: rims(): met = lax.ppermute(jnp.where(low, last, first), 'lat', swap_pairs(2, 1))]
    ppermute x2, starting transfers between devices: 4.54 us -> 9.09 us  [rims(): from_right = lax.ppermute(column(0), 'lon', [(j, i) for i, j in right])]
    all_to_all x3 -> x4, starting transfers between devices: 10.9 us -> 14.8 us  [exchange(): lax.all_to_all(sent, AXES, split_axis=0, concat_axis=0, tiled=True)]
    ppermute x2, waiting for transfers between devices: 9.77 us -> 6.56 us  [rims(): from_left = lax.ppermute(column(field.shape[1] - 1), 'lon', right)]
    all_to_all x3 -> x4, waiting for transfers between devices: 13.8 us -> 10.7 us  [exchange(): lax.all_to_all(sent, AXES, split_axis=0, concat_axis=0, tiled=True)]
    reshape x2 -> x0, local copies, waits for them, and re-layouts: 2.88 us -> none  [the longest x1 1.49 us: body(): pattern_col = pattern.reshape(cells, 1)]
  transfers between devices with their start and end apart: 15 -> 17, of which waited for: 7 -> 10; matrix products, arithmetic and copies ran while one was open for 10% -> 10% of each run, Pallas kernels for 7% -> 6%
where the time goes in v2:
time: 125 us; the launch traced here: 124 us
  waiting for transfers between devices  38.9 us (31%)
  starting transfers between devices  35.5 us (28%)
  Pallas kernels  23.9 us (19%)
  local copies, waits for them, and re-layouts  18.8 us (15%)
  other arithmetic  5.65 us (5%)
    pallas_call x10, Pallas kernels, call(): pl.pallas_call(kernel, name=name, grid=(1,), out_shape=list(out_shape), i...  23.9 us
    unnamed x59, local copies, waits for them, and re-layouts  16.3 us
    ppermute x4, waiting for transfers between devices, total_over(): x = x + lax.ppermute(x, axis, swap_pairs(size, bit))  14.9 us
    all_to_all x4, starting transfers between devices, exchange(): lax.all_to_all(sent, AXES, split_axis=0, concat_axis=0, tiled=True)  14.8 us
    all_to_all x4, waiting for transfers between devices, exchange(): lax.all_to_all(sent, AXES, split_axis=0, concat_axis=0, tiled=True)  10.7 us
    ppermute x2, starting transfers between devices, rims(): from_right = lax.ppermute(column(0), 'lon', [(j, i) for i, j in right])  9.09 us
    ppermute x2, waiting for transfers between devices, rims(): from_left = lax.ppermute(column(field.shape[1] - 1), 'lon', right)  6.56 us
    ppermute x1, waiting for transfers between devices, body(): met = lax.ppermute(message, 'lat', swap_pairs(2, 1))  3.61 us
  transfers between devices with their start and end apart: 17, of which 10 were waited for; matrix products, arithmetic and copies ran while one was open for 10% of the time, Pallas kernels for 6%

profile of v2, /device:TPU:0, one launch (start us, length us, event | category | flops | bytes accessed | tf_op | source)
XLA Modules:
  0.0 123.8 jit_solution(11004100758521166654)
XLA Ops:
  0.6 0.0 copy-start.23
  0.7 0.0 copy-start.1
  0.7 1.6 %select_bitcast_fusion = bf16[32,768]{1,0:T(8,128)(2,1)} fusion(bf16[8,32,768]{2,1,0:T(8,128)(2,1)} %field_ref.3, pred[]{:T(512)S(6)} %eq.4), kind=kLoop, calls=%fused_computation.6 | loop fusion | flops 24576 | bytes 147457 | tf_op jit(solution)/shard_map/jit(_where)/select_n | solution.py:324
  2.3 2.9 %collective-permute-start = (bf16[32,768]{1,0:T(8,128)(2,1)}, bf16[32,768]{1,0:T(8,128)(2,1)}, u32[]{:S(2)}, u32[]{:S(2)}) collective-permute-start(bf16[32,768]{1,0:T(8,128)(2,1)} %select_bitcast_fusion), channel_id=1, source_target_pairs={{0,16},{16,0},{1,17},{17,1},{2,18},{18,2},{3,19},{19,3},{4,20},{20... | collective-permute-start | bytes 147464 | tf_op jit(solution)/shard_map/ppermute | solution.py:324
  5.2 1.0 copy-done.7
  6.2 0.7 copy-done.22
  6.9 0.3 pack_cotangent.1
  7.2 0.0 copy-start.6
  7.2 0.7 copy-done.6
  8.0 5.0 %all-to-all-start.1 = ((bf16[32,8,768]{2,1,0:T(8,128)(2,1)}), bf16[32,8,768]{2,1,0:T(8,128)(2,1)}, u32[]{:S(2)}, u32[]{:S(2)}) async-start(bf16[32,8,768]{2,1,0:T(8,128)(2,1)} %bitcast.32), calls=%async_computation.1 | async-start | bytes 786432 | tf_op jit(solution)/shard_map/all_to_all | solution.py:345
  13.0 1.0 fusion
  14.0 0.8 broadcast_select_fusion.2
  14.9 4.3 %collective-permute-start.2 = (bf16[10,768]{1,0:T(8,128)(2,1)S(1)}, bf16[10,768]{1,0:T(8,128)(2,1)S(1)}, u32[]{:S(2)}, u32[]{:S(2)}) collective-permute-start(bf16[10,768]{1,0:T(8,128)(2,1)S(1)} %pad_maximum_fusion.2), channel_id=1, source_target_pairs={{1,0},{2,1},{3,2},{4,3},{5,4},{6,5},{7,6},{8,7},{9,8},{10,9},{11,1... | collective-permute-start | bytes 46088 | tf_op jit(solution)/shard_map/ppermute | solution.py:337
  19.2 0.1 collective-permute-start.1
  19.3 1.4 %collective-permute-done.2.right_ref = bf16[10,768]{1,0:T(8,128)(2,1)S(1)} collective-permute-done((bf16[10,768]{1,0:T(8,128)(2,1)S(1)}, bf16[10,768]{1,0:T(8,128)(2,1)S(1)}, u32[]{:S(2)}, u32[]{:S(2)}) %collective-permute-start.2) | collective-permute-done | bytes 15392 | tf_op jit(solution)/shard_map/ppermute | solution.py:337
  20.7 4.6 %collective-permute-done.1.left_ref = bf16[10,768]{1,0:T(8,128)(2,1)S(1)} collective-permute-done((bf16[10,768]{1,0:T(8,128)(2,1)S(1)}, bf16[10,768]{1,0:T(8,128)(2,1)S(1)}, u32[]{:S(2)}, u32[]{:S(2)}) %collective-permute-start.1) | collective-permute-done | bytes 15392 | tf_op jit(solution)/shard_map/ppermute | solution.py:336
  25.4 1.0 copy-done.4
  26.4 0.8 copy-done.16
  27.1 1.5 %convolve_normalize_pack.1 = (bf16[256,768]{1,0:T(8,128)(2,1)S(1)}, bf16[256,768]{1,0:T(8,128)(2,1)S(1)}) custom-call(s32[1,256]{1,0:T(1,128)S(1)} %bitcast.40, bf16[8,32,768]{2,1,0:T(8,128)(2,1)S(1)} %copy-done.4, bf16[32,768]{1,0:T(8,128)(2,1)S(1)} %get-tuple-element.64.before_ref, bf16[32,768]{1,0:T(8,128)(2,1)S(1)} %get-tuple-element.63.after_ref, ...), custom_call_target="tpu_custom_call" | custom-call | bytes 1340416 | tf_op jit(solution)/shard_map/convolve_normalize_pack/pallas_call | solution.py:40
  28.6 0.8 copy-done.9
  29.4 0.7 copy-done.15
  30.1 0.6 copy-done.18
  30.7 0.6 copy-done.20
  31.4 3.3 %all-to-all-start = ((bf16[32,8,768]{2,1,0:T(8,128)(2,1)}), bf16[32,8,768]{2,1,0:T(8,128)(2,1)}, u32[]{:S(2)}, u32[]{:S(2)}) async-start(bf16[32,8,768]{2,1,0:T(8,128)(2,1)} %bitcast.38), calls=%async_computation | async-start | bytes 786432 | tf_op jit(solution)/shard_map/all_to_all | solution.py:345
  34.7 3.6 %copy.15 = bf16[768,2304]{0,1:T(8,128)(2,1)} copy(bf16[768,2304]{1,0:T(8,128)(2,1)S(1)} %copy-done.1) | data formatting | bytes 7077888 | tf_op args[3]
  38.3 2.4 %copy.17 = f32[24,64,64]{1,2,0:T(8,128)} copy(f32[24,64,64]{2,1,0:T(8,128)} %param.13) | data formatting | bytes 786432 | tf_op args[5]
  40.7 0.6 copy.16
  41.3 1.6 %pad_maximum_fusion.refs_3_ = f32[24,64,128]{2,1,0:T(8,128)S(1)} fusion(f32[24,64,64]{2,1,0:T(8,128)} %bitcast.43), kind=kLoop, calls=%fused_computation | loop fusion | flops 196608 | bytes 1179648 | tf_op jit(solution)/shard_map/concatenate | solution.py:405
  43.0 1.7 %cotangent_products.1 = (bf16[768,256]{1,0:T(8,128)(2,1)S(1)}, bf16[768,256]{1,0:T(8,128)(2,1)S(1)}) custom-call(bf16[256,768]{1,0:T(8,128)(2,1)} %bitcast.11.refs_0_, bf16[768,768]{1,0:T(8,128)(2,1)S(1)} %copy-done), custom_call_target="tpu_custom_call" | custom-call | bytes 2359296 | tf_op jit(solution)/shard_map/cotangent_products/pallas_call | solution.py:40
  44.7 0.8 copy-done.24
  45.4 2.3 %all-to-all-done = bf16[32,8,768]{2,1,0:T(8,128)(2,1)} async-done(((bf16[32,8,768]{2,1,0:T(8,128)(2,1)}), bf16[32,8,768]{2,1,0:T(8,128)(2,1)}, u32[]{:S(2)}, u32[]{:S(2)}) %all-to-all-start) | async-done | bytes 393248 | tf_op jit(solution)/shard_map/all_to_all | solution.py:345
  47.8 2.0 %copy-done.3 = bf16[768,2304]{0,1:T(8,128)(2,1)S(1)} copy-done((bf16[768,2304]{0,1:T(8,128)(2,1)S(1)}, bf16[768,2304]{0,1:T(8,128)(2,1)}, u32[]{:S(2)}) %copy-start.3) | copy-done | bytes 3538968
  49.8 9.3 %attention_forward.1 = (bf16[256,768]{1,0:T(8,128)(2,1)}, bf16[2304,256]{1,0:T(8,128)(2,1)S(1)}, f32[24,64,256]{2,1,0:T(8,128)S(1)}, bf16[768,256]{1,0:T(8,128)(2,1)S(1)}) custom-call(bf16[256,768]{1,0:T(8,128)(2,1)} %bitcast.5.refs_0_, bf16[2304,768]{1,0:T(8,128)(2,1)S(1)} %bitcast.31, bf16[768,768]{1,0:T(8,128)(2,1)S(1)} %bitcast.37, ...), custom_call_target="tpu_custom_call" | custom-call | flops 5000000000 | bytes 9437184 | tf_op jit(solution)/shard_map/attention_forward/pallas_call | solution.py:40
  59.1 5.7 %attention_backward.1 = bf16[256,768]{1,0:T(8,128)(2,1)} custom-call(bf16[2304,256]{1,0:T(8,128)(2,1)S(1)} %get-tuple-element.28.refs_0_, f32[24,64,256]{2,1,0:T(8,128)S(1)} %get-tuple-element.29.refs_1_, bf16[768,256]{1,0:T(8,128)(2,1)S(1)} %copy-done.25, bf16[768,2304]{1,0:T(8,128)(2,1)S(1)} %copy-done.2), custom_call_target="tpu_custom_call" | custom-call | flops 10000000000 | bytes 7077888 | tf_op jit(solution)/shard_map/attention_backward/pallas_call | solution.py:40
  64.8 0.0 copy-start.14
  64.8 0.0 copy-start.21
  64.8 3.5 %all-to-all-start.2 = ((bf16[32,8,768]{2,1,0:T(8,128)(2,1)}), bf16[32,8,768]{2,1,0:T(8,128)(2,1)S(1)}, u32[]{:S(2)}, u32[]{:S(2)}) async-start(bf16[32,8,768]{2,1,0:T(8,128)(2,1)} %bitcast.12), calls=%async_computation.2 | async-start | bytes 786432 | tf_op jit(solution)/shard_map/all_to_all | solution.py:345
  68.3 0.7 project_gradient.1
  69.0 0.3 collective-permute-start.8
  69.3 1.7 %collective-permute-done.8.met_ref = bf16[2,8,48,384]{3,2,1,0:T(8,128)(2,1)S(1)} collective-permute-done((bf16[2,8,48,384]{3,2,1,0:T(8,128)(2,1)S(1)}, bf16[2,8,48,384]{3,2,1,0:T(8,128)(2,1)S(1)}, u32[]{:S(2)}, u32[]{:S(2)}) %collective-permute-start.8) | collective-permute-done | bytes 589856 | tf_op jit(solution)/shard_map/ppermute | solution.py:366
  71.1 0.2 project_join.1
  71.2 1.8 %collective-permute-start.9 = (bf16[8,48,384]{2,1,0:T(8,128)(2,1)S(1)}, bf16[8,48,384]{2,1,0:T(8,128)(2,1)S(1)}, u32[]{:S(2)}, u32[]{:S(2)}) collective-permute-start(bf16[8,48,384]{2,1,0:T(8,128)(2,1)S(1)} %get-tuple-element.47), channel_id=1, source_target_pairs={{0,16},{16,0},{1,17},{17,1},{2,18},{18,2},{3,19},{19,3},{4,20},{20... | collective-permute-start | bytes 884744 | tf_op jit(solution)/shard_map/ppermute | solution.py:370
  73.1 8.4 %all-to-all-done.2 = bf16[32,8,768]{2,1,0:T(8,128)(2,1)S(1)} async-done(((bf16[32,8,768]{2,1,0:T(8,128)(2,1)}), bf16[32,8,768]{2,1,0:T(8,128)(2,1)S(1)}, u32[]{:S(2)}, u32[]{:S(2)}) %all-to-all-start.2) | async-done | bytes 393248 | tf_op jit(solution)/shard_map/all_to_all | solution.py:345
  81.5 1.8 %normalize_back.1 = (bf16[8,32,768]{2,1,0:T(8,128)(2,1)S(1)}, f32[16,768]{1,0:T(8,128)S(1)}, bf16[64,768]{1,0:T(8,128)(2,1)S(1)}) custom-call(s32[1]{0:T(128)} %bitcast.17.lat_ref, s32[1,256]{1,0:T(1,128)S(1)} %bitcast.41, bf16[256,768]{1,0:T(8,128)(2,1)S(1)} %bitcast.35, bf16[256,768]{1,0:T(8,128)(2,1)S(1)} %copy-done.10, bf16[256,768]{1,0:T(8,128)(2,1)S(1)} %bitcast.34, ...), custom_call_target="tpu_custom_call" | custom-call | bytes 2246660 | tf_op jit(solution)/shard_map/normalize_back/pallas_call | solution.py:40
  83.3 0.2 copy.18
  83.5 1.1 collective-permute-start.3
  84.6 3.6 %collective-permute-done.3 = bf16[64,768]{1,0:T(8,128)(2,1)S(1)} collective-permute-done((bf16[64,768]{1,0:T(8,128)(2,1)S(1)}, bf16[64,768]{1,0:T(8,128)(2,1)S(1)}, u32[]{:S(2)}, u32[]{:S(2)}) %collective-permute-start.3) | collective-permute-done | bytes 98336 | tf_op jit(solution)/shard_map/ppermute | solution.py:457
  88.3 0.8 add_convert_fusion
  89.1 3.4 %all-to-all-start.4 = ((bf16[8,48,384]{2,1,0:T(8,128)(2,1)}), bf16[8,48,384]{2,1,0:T(8,128)(2,1)S(1)}, u32[]{:S(2)}, u32[]{:S(2)}) async-start(bf16[8,48,384]{2,1,0:T(8,128)(2,1)} %add_convert_fusion), calls=%async_computation.4 | async-start | bytes 589824 | tf_op jit(solution)/shard_map/all_to_all | solution.py:373
  92.5 0.1 collective-permute-start.4
  92.6 4.8 %collective-permute-start.7 = (bf16[10,768]{1,0:T(8,128)(2,1)S(1)}, bf16[10,768]{1,0:T(8,128)(2,1)S(1)}, u32[]{:S(2)}, u32[]{:S(2)}) collective-permute-start(bf16[10,768]{1,0:T(8,128)(2,1)S(1)} %pad_maximum_fusion.4), channel_id=1, source_target_pairs={{1,0},{2,1},{3,2},{4,3},{5,4},{6,5},{7,6},{8,7},{9,8},{10,9},{11,1... | collective-permute-start | bytes 46088 | tf_op jit(solution)/shard_map/ppermute | solution.py:337
  97.4 0.1 collective-permute-start.5
  97.5 0.1 collective-permute-start.6
  97.6 4.0 %collective-permute-done.5 = f32[16,768]{1,0:T(8,128)S(1)} collective-permute-done((f32[16,768]{1,0:T(8,128)S(1)}, f32[16,768]{1,0:T(8,128)S(1)}, u32[]{:S(2)}, u32[]{:S(2)}) %collective-permute-start.5) | collective-permute-done | bytes 49184 | tf_op jit(solution)/shard_map/ppermute | solution.py:385
  101.6 1.9 %collective-permute-done.6.left_ref = bf16[10,768]{1,0:T(8,128)(2,1)S(1)} collective-permute-done((bf16[10,768]{1,0:T(8,128)(2,1)S(1)}, bf16[10,768]{1,0:T(8,128)(2,1)S(1)}, u32[]{:S(2)}, u32[]{:S(2)}) %collective-permute-start.6) | collective-permute-done | bytes 15392 | tf_op jit(solution)/shard_map/ppermute | solution.py:336
  103.6 3.0 %all-to-all-start.3 = ((bf16[32,8,768]{2,1,0:T(8,128)(2,1)}), bf16[32,8,768]{2,1,0:T(8,128)(2,1)S(1)}, u32[]{:S(2)}, u32[]{:S(2)}) async-start(bf16[32,8,768]{2,1,0:T(8,128)(2,1)} %bitcast.14), calls=%async_computation.3 | async-start | bytes 786432 | tf_op jit(solution)/shard_map/all_to_all | solution.py:345
  106.6 1.1 collective-permute-done.10
  107.6 1.7 %collective-permute-start.11 = (f32[16,768]{1,0:T(8,128)S(1)}, f32[16,768]{1,0:T(8,128)S(1)}, u32[]{:S(2)}, u32[]{:S(2)}) collective-permute-start(f32[16,768]{1,0:T(8,128)S(1)} %add.26), channel_id=1, source_target_pairs={{0,8},{1,9},{2,10},{3,11},{4,12},{5,13},{6,14},{7,15},{8,0},{9,1},... | collective-permute-start | bytes 147464 | tf_op jit(solution)/shard_map/ppermute | solution.py:385
  109.4 1.7 %convolve_back.1 = bf16[8,32,768]{2,1,0:T(8,128)(2,1)} custom-call(bf16[8,32,768]{2,1,0:T(8,128)(2,1)S(1)} %get-tuple-element.35.field_ref, bf16[32,768]{1,0:T(8,128)(2,1)S(1)} %get-tuple-element.38.before_ref, bf16[32,768]{1,0:T(8,128)(2,1)S(1)} %get-tuple-element.39.after_ref, bf16[10,768]{1,0:T(8,128)(2,1)S(1)} %collective-permute-done.6.left_ref, ...), custom_call_target="tpu_custom_call" | custom-call | bytes 943104 | tf_op jit(solution)/shard_map/convolve_back/pallas_call | solution.py:40
  111.1 9.8 %collective-permute-done.11 = f32[16,768]{1,0:T(8,128)S(1)} collective-permute-done((f32[16,768]{1,0:T(8,128)S(1)}, f32[16,768]{1,0:T(8,128)S(1)}, u32[]{:S(2)}, u32[]{:S(2)}) %collective-permute-start.11) | collective-permute-done | bytes 49184 | tf_op jit(solution)/shard_map/ppermute | solution.py:385
  120.9 0.6 reshape.74
  121.5 0.6 slice_reduce_fusion
  122.2 0.6 multiply_bitcast_fusion
  122.8 1.0 block_out.1
  (64 shorter events, 0.3 us)
Async XLA Ops:
  0.6 24.7 %copy-start.23 = (s32[1,1,256]{2,1,0:T(1,128)S(1)}, s32[1,1,256]{2,1,0:T(1,128)}, u32[]{:S(2)}) copy-start(s32[1,1,256]{2,1,0:T(1,128)} %param.14) | copy-start | bytes 3076
  0.6 18.6 %copy-start.26 = (f32[768]{0:T(1024)S(1)}, f32[768]{0:T(1024)}, u32[]{:S(2)}) copy-start(f32[768]{0:T(1024)} %param.10) | copy-start | bytes 9220
  0.7 34.0 %copy-start.1 = (bf16[768,2304]{1,0:T(8,128)(2,1)S(1)}, bf16[768,2304]{1,0:T(8,128)(2,1)}, u32[]{:S(2)}) copy-start(bf16[768,2304]{1,0:T(8,128)(2,1)} %refs_3_.1) | copy-start | bytes 10616836
  2.3 11.7 %collective-permute-start = (bf16[32,768]{1,0:T(8,128)(2,1)}, bf16[32,768]{1,0:T(8,128)(2,1)}, u32[]{:S(2)}, u32[]{:S(2)}) collective-permute-start(bf16[32,768]{1,0:T(8,128)(2,1)} %select_bitcast_fusion), channel_id=1, source_target_pairs={{0,16},{16,0},{1,17},{17,1},{2,18},{18,2},{3,19},{19,3},{4,20},{20... | collective-permute-start | bytes 147464 | tf_op jit(solution)/shard_map/ppermute | solution.py:324
  5.2 1.0 copy-start.7
  6.2 0.7 copy-start.22
  7.2 0.7 copy-start.6
  8.0 23.4 %all-to-all-start.1 = ((bf16[32,8,768]{2,1,0:T(8,128)(2,1)}), bf16[32,8,768]{2,1,0:T(8,128)(2,1)}, u32[]{:S(2)}, u32[]{:S(2)}) async-start(bf16[32,8,768]{2,1,0:T(8,128)(2,1)} %bitcast.32), calls=%async_computation.1 | async-start | bytes 786432 | tf_op jit(solution)/shard_map/all_to_all | solution.py:345
  14.8 10.5 %copy-start.11 = (bf16[32,768]{1,0:T(8,128)(2,1)}, bf16[32,768]{1,0:T(8,128)(2,1)S(1)}, u32[]{:S(2)}) copy-start(bf16[32,768]{1,0:T(8,128)(2,1)S(1)} %get-tuple-element.63.after_ref) | copy-start | bytes 147460
  14.8 10.5 %copy-start.13 = (bf16[32,768]{1,0:T(8,128)(2,1)}, bf16[32,768]{1,0:T(8,128)(2,1)S(1)}, u32[]{:S(2)}) copy-start(bf16[32,768]{1,0:T(8,128)(2,1)S(1)} %get-tuple-element.64.before_ref) | copy-start | bytes 147460
  14.9 5.8 %collective-permute-start.2 = (bf16[10,768]{1,0:T(8,128)(2,1)S(1)}, bf16[10,768]{1,0:T(8,128)(2,1)S(1)}, u32[]{:S(2)}, u32[]{:S(2)}) collective-permute-start(bf16[10,768]{1,0:T(8,128)(2,1)S(1)} %pad_maximum_fusion.2), channel_id=1, source_target_pairs={{1,0},{2,1},{3,2},{4,3},{5,4},{6,5},{7,6},{8,7},{9,8},{10,9},{11,1... | collective-permute-start | bytes 46088 | tf_op jit(solution)/shard_map/ppermute | solution.py:337
  19.2 6.1 %collective-permute-start.1 = (bf16[10,768]{1,0:T(8,128)(2,1)S(1)}, bf16[10,768]{1,0:T(8,128)(2,1)S(1)}, u32[]{:S(2)}, u32[]{:S(2)}) collective-permute-start(bf16[10,768]{1,0:T(8,128)(2,1)S(1)} %pad_maximum_fusion.1), channel_id=1, source_target_pairs={{0,1},{1,2},{2,3},{3,4},{4,5},{5,6},{6,7},{7,8},{8,9},{9,10},{10,1... | collective-permute-start | bytes 46088 | tf_op jit(solution)/shard_map/ppermute | solution.py:336
  25.4 1.0 copy-start.4
  26.4 0.8 copy-start.16
  28.6 0.8 copy-start.9
  29.4 0.7 copy-start.15
  30.1 0.6 copy-start.18
  30.7 0.6 copy-start.20
  31.4 16.4 %all-to-all-start = ((bf16[32,8,768]{2,1,0:T(8,128)(2,1)}), bf16[32,8,768]{2,1,0:T(8,128)(2,1)}, u32[]{:S(2)}, u32[]{:S(2)}) async-start(bf16[32,8,768]{2,1,0:T(8,128)(2,1)} %bitcast.38), calls=%async_computation | async-start | bytes 786432 | tf_op jit(solution)/shard_map/all_to_all | solution.py:345
  38.3 2.4 %copy-start = (bf16[768,768]{1,0:T(8,128)(2,1)S(1)}, bf16[768,768]{1,0:T(8,128)(2,1)}, u32[]{:S(2)}) copy-start(bf16[768,768]{1,0:T(8,128)(2,1)} %refs_1_.1) | copy-start | bytes 3538948
  44.7 0.8 copy-start.24
  47.8 2.0 %copy-start.3 = (bf16[768,2304]{0,1:T(8,128)(2,1)S(1)}, bf16[768,2304]{0,1:T(8,128)(2,1)}, u32[]{:S(2)}) copy-start(bf16[768,2304]{0,1:T(8,128)(2,1)} %copy.15) | copy-start | bytes 10616836
  49.8 9.3 %copy-start.2 = (bf16[768,2304]{1,0:T(8,128)(2,1)S(1)}, bf16[768,2304]{1,0:T(8,128)(2,1)}, u32[]{:S(2)}) copy-start(bf16[768,2304]{1,0:T(8,128)(2,1)} %refs_3_.1) | copy-start | bytes 10616836
  49.8 9.3 %copy-start.25 = (bf16[768,256]{1,0:T(8,128)(2,1)S(1)}, bf16[768,256]{1,0:T(8,128)(2,1)}, u32[]{:S(2)}) copy-start(bf16[768,256]{1,0:T(8,128)(2,1)} %copy-done.24) | copy-start | bytes 1179652
  64.8 16.6 %copy-start.5 = (bf16[8,32,768]{2,1,0:T(8,128)(2,1)S(1)}, bf16[8,32,768]{2,1,0:T(8,128)(2,1)}, u32[]{:S(2)}) copy-start(bf16[8,32,768]{2,1,0:T(8,128)(2,1)} %field_ref.3) | copy-start | bytes 1179652
  64.8 16.6 %copy-start.8 = (bf16[8,32,768]{2,1,0:T(8,128)(2,1)S(1)}, bf16[8,32,768]{2,1,0:T(8,128)(2,1)}, u32[]{:S(2)}) copy-start(bf16[8,32,768]{2,1,0:T(8,128)(2,1)} %param.15) | copy-start | bytes 1179652
  64.8 16.6 %copy-start.10 = (bf16[256,768]{1,0:T(8,128)(2,1)S(1)}, bf16[256,768]{1,0:T(8,128)(2,1)}, u32[]{:S(2)}) copy-start(bf16[256,768]{1,0:T(8,128)(2,1)} %copy-done.9) | copy-start | bytes 1179652
  64.8 16.6 %copy-start.12 = (bf16[32,768]{1,0:T(8,128)(2,1)S(1)}, bf16[32,768]{1,0:T(8,128)(2,1)}, u32[]{:S(2)}) copy-start(bf16[32,768]{1,0:T(8,128)(2,1)} %copy-done.11) | copy-start | bytes 147460
  64.8 16.6 %copy-start.14 = (bf16[32,768]{1,0:T(8,128)(2,1)S(1)}, bf16[32,768]{1,0:T(8,128)(2,1)}, u32[]{:S(2)}) copy-start(bf16[32,768]{1,0:T(8,128)(2,1)} %copy-done.13) | copy-start | bytes 147460
  64.8 16.6 %copy-start.19 = (bf16[10,768]{1,0:T(8,128)(2,1)S(1)}, bf16[10,768]{1,0:T(8,128)(2,1)}, u32[]{:S(2)}) copy-start(bf16[10,768]{1,0:T(8,128)(2,1)} %copy-done.18) | copy-start | bytes 46084
  64.8 16.6 %copy-start.21 = (bf16[10,768]{1,0:T(8,128)(2,1)S(1)}, bf16[10,768]{1,0:T(8,128)(2,1)}, u32[]{:S(2)}) copy-start(bf16[10,768]{1,0:T(8,128)(2,1)} %copy-done.20) | copy-start | bytes 46084
  64.8 16.6 %all-to-all-start.2 = ((bf16[32,8,768]{2,1,0:T(8,128)(2,1)}), bf16[32,8,768]{2,1,0:T(8,128)(2,1)S(1)}, u32[]{:S(2)}, u32[]{:S(2)}) async-start(bf16[32,8,768]{2,1,0:T(8,128)(2,1)} %bitcast.12), calls=%async_computation.2 | async-start | bytes 786432 | tf_op jit(solution)/shard_map/all_to_all | solution.py:345
  69.0 2.1 %collective-permute-start.8 = (bf16[2,8,48,384]{3,2,1,0:T(8,128)(2,1)S(1)}, bf16[2,8,48,384]{3,2,1,0:T(8,128)(2,1)S(1)}, u32[]{:S(2)}, u32[]{:S(2)}) collective-permute-start(bf16[2,8,48,384]{3,2,1,0:T(8,128)(2,1)S(1)} %get-tuple-element.45), channel_id=1, source_target_pairs={{0,1},{1,0},{2,3},{3,2},{4,5},{5,4},{6,7},{7,6},{8,9},{9,8},{10,11... | collective-permute-start | bytes 1769480 | tf_op jit(solution)/shard_map/ppermute | solution.py:366
  71.2 17.0 %collective-permute-start.9 = (bf16[8,48,384]{2,1,0:T(8,128)(2,1)S(1)}, bf16[8,48,384]{2,1,0:T(8,128)(2,1)S(1)}, u32[]{:S(2)}, u32[]{:S(2)}) collective-permute-start(bf16[8,48,384]{2,1,0:T(8,128)(2,1)S(1)} %get-tuple-element.47), channel_id=1, source_target_pairs={{0,16},{16,0},{1,17},{17,1},{2,18},{18,2},{3,19},{19,3},{4,20},{20... | collective-permute-start | bytes 884744 | tf_op jit(solution)/shard_map/ppermute | solution.py:370
  83.5 4.7 %collective-permute-start.3 = (bf16[64,768]{1,0:T(8,128)(2,1)S(1)}, bf16[64,768]{1,0:T(8,128)(2,1)S(1)}, u32[]{:S(2)}, u32[]{:S(2)}) collective-permute-start(bf16[64,768]{1,0:T(8,128)(2,1)S(1)} %get-tuple-element.37), channel_id=1, source_target_pairs={{0,16},{16,0},{1,17},{17,1},{2,18},{18,2},{3,19},{19,3},{4,20},{20... | collective-permute-start | bytes 294920 | tf_op jit(solution)/shard_map/ppermute | solution.py:457
  84.6 24.7 %copy-start.17 = (f32[3,3,768]{2,1,0:T(4,128)S(1)}, f32[3,3,768]{2,1,0:T(4,128)}, u32[]{:S(2)}) copy-start(f32[3,3,768]{2,1,0:T(4,128)} %taps_ref.3) | copy-start | bytes 82948
  89.1 14.5 %all-to-all-start.4 = ((bf16[8,48,384]{2,1,0:T(8,128)(2,1)}), bf16[8,48,384]{2,1,0:T(8,128)(2,1)S(1)}, u32[]{:S(2)}, u32[]{:S(2)}) async-start(bf16[8,48,384]{2,1,0:T(8,128)(2,1)} %add_convert_fusion), calls=%async_computation.4 | async-start | bytes 589824 | tf_op jit(solution)/shard_map/all_to_all | solution.py:373
  92.5 4.9 %collective-permute-start.4 = (f32[16,768]{1,0:T(8,128)S(1)}, f32[16,768]{1,0:T(8,128)S(1)}, u32[]{:S(2)}, u32[]{:S(2)}) collective-permute-start(f32[16,768]{1,0:T(8,128)S(1)} %convert_add_fusion), channel_id=1, source_target_pairs={{0,1},{1,0},{2,3},{3,2},{4,5},{5,4},{6,7},{7,6},{8,9},{9,8},{10,11... | collective-permute-start | bytes 147464 | tf_op jit(solution)/shard_map/ppermute | solution.py:385
  92.6 9.0 %collective-permute-start.7 = (bf16[10,768]{1,0:T(8,128)(2,1)S(1)}, bf16[10,768]{1,0:T(8,128)(2,1)S(1)}, u32[]{:S(2)}, u32[]{:S(2)}) collective-permute-start(bf16[10,768]{1,0:T(8,128)(2,1)S(1)} %pad_maximum_fusion.4), channel_id=1, source_target_pairs={{1,0},{2,1},{3,2},{4,3},{5,4},{6,5},{7,6},{8,7},{9,8},{10,9},{11,1... | collective-permute-start | bytes 46088 | tf_op jit(solution)/shard_map/ppermute | solution.py:337
  97.4 4.2 %collective-permute-start.5 = (f32[16,768]{1,0:T(8,128)S(1)}, f32[16,768]{1,0:T(8,128)S(1)}, u32[]{:S(2)}, u32[]{:S(2)}) collective-permute-start(f32[16,768]{1,0:T(8,128)S(1)} %add.23), channel_id=1, source_target_pairs={{0,2},{1,3},{2,0},{3,1},{4,6},{5,7},{6,4},{7,5},{8,10},{9,11},{10,... | collective-permute-start | bytes 147464 | tf_op jit(solution)/shard_map/ppermute | solution.py:385
  97.5 6.0 %collective-permute-start.6 = (bf16[10,768]{1,0:T(8,128)(2,1)S(1)}, bf16[10,768]{1,0:T(8,128)(2,1)S(1)}, u32[]{:S(2)}, u32[]{:S(2)}) collective-permute-start(bf16[10,768]{1,0:T(8,128)(2,1)S(1)} %pad_maximum_fusion.3), channel_id=1, source_target_pairs={{0,1},{1,2},{2,3},{3,4},{4,5},{5,6},{6,7},{7,8},{8,9},{9,10},{10,1... | collective-permute-start | bytes 46088 | tf_op jit(solution)/shard_map/ppermute | solution.py:336
  103.5 4.1 %collective-permute-start.10 = (f32[16,768]{1,0:T(8,128)S(1)}, f32[16,768]{1,0:T(8,128)S(1)}, u32[]{:S(2)}, u32[]{:S(2)}) collective-permute-start(f32[16,768]{1,0:T(8,128)S(1)} %add.24), channel_id=1, source_target_pairs={{0,4},{1,5},{2,6},{3,7},{4,0},{5,1},{6,2},{7,3},{8,12},{9,13},{10,... | collective-permute-start | bytes 147464 | tf_op jit(solution)/shard_map/ppermute | solution.py:385
  103.6 19.3 %all-to-all-start.3 = ((bf16[32,8,768]{2,1,0:T(8,128)(2,1)}), bf16[32,8,768]{2,1,0:T(8,128)(2,1)S(1)}, u32[]{:S(2)}, u32[]{:S(2)}) async-start(bf16[32,8,768]{2,1,0:T(8,128)(2,1)} %bitcast.14), calls=%async_computation.3 | async-start | bytes 786432 | tf_op jit(solution)/shard_map/all_to_all | solution.py:345
  107.6 13.2 %collective-permute-start.11 = (f32[16,768]{1,0:T(8,128)S(1)}, f32[16,768]{1,0:T(8,128)S(1)}, u32[]{:S(2)}, u32[]{:S(2)}) collective-permute-start(f32[16,768]{1,0:T(8,128)S(1)} %add.26), channel_id=1, source_target_pairs={{0,8},{1,9},{2,10},{3,11},{4,12},{5,13},{6,14},{7,15},{8,0},{9,1},... | collective-permute-start | bytes 147464 | tf_op jit(solution)/shard_map/ppermute | solution.py:385

commit v3 on v2

v3 whole, which is shorter than its diff:
```python
import math

import jax
import jax.numpy as jnp
from jax import lax
from jax.experimental import pallas as pl
from jax.experimental.pallas import tpu as pltpu
from jax.sharding import PartitionSpec as P

HEADS = 24
HEAD_DIM = 32
GROUP = 64
PAIR = 2 * GROUP
EDGE = 8
UNROLL = 6

epsilon = 1e-05
f32, bf16 = jnp.float32, jnp.bfloat16
AXES = ("lat", "lon")
NN = (((1,), (0,)), ((), ()))
NT = (((1,), (1,)), ((), ()))
TN = (((0,), (0,)), ((), ()))
VMEM = pl.BlockSpec(memory_space=pltpu.VMEM)
SMEM = pl.BlockSpec(memory_space=pltpu.SMEM)
ANY = pl.BlockSpec(memory_space=pl.ANY)
BIG = 60


def dot(a, b, dims=NN):
    return lax.dot_general(a, b, dims, preferred_element_type=f32)


def whole(x):
    return pl.BlockSpec(x.shape, lambda step: (0,) * len(x.shape))


def call(kernel, name, out_shape, operands, scratch=(), flops=0, specs=(), mib=40):
    size = sum(math.prod(x.shape) * x.dtype.itemsize for x in (*operands, *out_shape))
    specs = dict(specs)
    return pl.pallas_call(
        kernel,
        name=name,
        grid=(1,),
        out_shape=list(out_shape),
        in_specs=[specs.get(i, whole(x)) for i, x in enumerate(operands)],
        out_specs=[whole(x) for x in out_shape],
        scratch_shapes=list(scratch),
        compiler_params=pltpu.CompilerParams(vmem_limit_bytes=mib * 1024 * 1024),
        cost_estimate=pl.CostEstimate(flops=flops, bytes_accessed=size, transcendentals=0),
    )(*operands)


def shape(dims, dtype):
    return jax.ShapeDtypeStruct(dims, dtype)


def by_cell(pattern_row, cells):
    cell = lax.broadcasted_iota(jnp.int32, (cells, cells), 0)
    return jnp.where(pattern_row == cell, 1.0, 0.0).astype(bf16)


def position_by_row(cells, slots, blocks, row_dim):
    row = lax.broadcasted_iota(jnp.int32, (cells, cells), row_dim)
    position = lax.broadcasted_iota(jnp.int32, (cells, cells), 1 - row_dim)
    place = lax.rem(row, slots) * blocks + lax.div(row, slots)
    return jnp.where(place == position, 1.0, 0.0).astype(bf16)


def rim_cells(flags_ref, field_ref, row_ref, cols_ref):
    rows, cols, _ = field_ref.shape
    low, even = flags_ref[0] == 0, flags_ref[2] == 0
    row_ref[...] = jnp.where(low, field_ref[rows - 1], field_ref[0])
    first = jnp.concatenate([field_ref[row, 0:1] for row in range(rows)], axis=0)
    last = jnp.concatenate([field_ref[row, cols - 1 : cols] for row in range(rows)], axis=0)
    cols_ref[0] = jnp.where(even, last, first)
    cols_ref[1] = jnp.where(even, first, last)


def start_kernel(flags_ref, pattern_ref, rows_ref, field_ref, out_ref, row_ref, cols_ref):
    cells = rows_ref.shape[0]
    rim_cells(flags_ref, field_ref, row_ref, cols_ref)
    out_ref[...] = dot(by_cell(pattern_ref[...], cells), rows_ref[...], TN).astype(bf16)


def fill_pad(pad, flags_ref, field_ref, before_ref, after_ref, even_ref, odd_ref):
    rows, cols, _ = field_ref.shape
    before, after = before_ref[...].astype(f32), after_ref[...].astype(f32)
    pad[0, EDGE : EDGE + cols] = jnp.where(flags_ref[0] != 0, before, jnp.zeros_like(before))
    pad[rows + 1, EDGE : EDGE + cols] = jnp.where(flags_ref[1] != 0, after, jnp.zeros_like(after))
    for row in range(rows):
        pad[row + 1, EDGE : EDGE + cols] = field_ref[row].astype(f32)
    even, odd = even_ref[...].astype(f32), odd_ref[...].astype(f32)
    left = jnp.where(flags_ref[2] == 0, odd, even)
    right = jnp.where(flags_ref[2] == 0, even, odd)
    for row in range(rows + 2):
        pad[row, EDGE - 1 : EDGE] = left[row : row + 1]
        pad[row, EDGE + cols : EDGE + cols + 1] = right[row : row + 1]


def taps_row(pad, taps, row, cols, flip):
    summed = pad[row + 1, EDGE : EDGE + cols]
    for a in range(3):
        for b in range(3):
            tap = taps[2 - a, 2 - b : 3 - b] if flip else taps[a, b : b + 1]
            summed = summed + tap * pad[row + a, EDGE - 1 + b : EDGE - 1 + b + cols]
    return summed


def normalized(h):
    mean = jnp.mean(h, axis=-1, keepdims=True)
    centred = h - mean
    var = jnp.mean(centred * centred, axis=-1, keepdims=True)
    deviation = lax.rsqrt(var + epsilon)
    return centred * deviation, deviation


def enter_kernel(
    flags_ref, pattern_ref, field_ref, before_ref, after_ref, even_ref, odd_ref, taps_ref, gain_ref,
    h_ref, out_ref, pad, normed,
):
    rows, cols, _ = field_ref.shape
    fill_pad(pad, flags_ref, field_ref, before_ref, after_ref, even_ref, odd_ref)
    taps, gain = taps_ref[...], gain_ref[...]
    for row in range(rows):
        h = taps_row(pad, taps, row, cols, False).astype(bf16)
        h_ref[row * cols : (row + 1) * cols] = h
        xhat, _ = normalized(h.astype(f32))
        normed[row * cols : (row + 1) * cols] = (xhat * gain).astype(bf16)
    out_ref[...] = dot(by_cell(pattern_ref[...], rows * cols), normed[...], TN).astype(bf16)


def cot_kernel(slots, blocks, arrived_ref, out_weight_ref, grad_att_ref, cot_ref):
    cells = arrived_ref.shape[0]
    grouped = dot(position_by_row(cells, slots, blocks, 1), arrived_ref[...]).astype(bf16)
    grad_att_ref[...] = dot(out_weight_ref[...], grouped, NT).astype(bf16)
    cot_ref[...] = grouped.T


def low_lanes(dims):
    return lax.broadcasted_iota(jnp.int32, dims, len(dims) - 1) < GROUP


def pair_scores(left, right):
    both = dot(left, right, TN)
    return jnp.where(low_lanes((GROUP, PAIR)), both[:GROUP], both[GROUP:])


def pair_diagonal(compact):
    low = low_lanes((GROUP, PAIR))
    zero = jnp.zeros_like(compact)
    return jnp.concatenate([jnp.where(low, compact, zero), jnp.where(low, zero, compact)], axis=0)


def attention_kernel(
    slots, blocks, unroll,
    arrived_hbm, qkv_weight_t_hbm, bias_hbm, grad_att_hbm, qkv_weight_hbm,
    grad_ref, att_ref,
    arrived, qkv_weight_t, bias, grad_att, qkv_weight, qkv, grad_qkv, sems,
):
    cells, width = arrived.shape
    step = width // 2
    parts = [pl.ds(at, step) for at in range(0, 3 * width, step)]
    fetches = [
        pltpu.make_async_copy(source, target, sems.at[i])
        for i, (source, target) in enumerate(
            [
                (arrived_hbm, arrived),
                *((qkv_weight_t_hbm.at[part], qkv_weight_t.at[part]) for part in parts),
                (bias_hbm, bias),
                (grad_att_hbm, grad_att),
                (qkv_weight_hbm, qkv_weight),
            ]
        )
    ]
    for fetch in fetches:
        fetch.start()
    gather = position_by_row(cells, slots, blocks, 1)
    fetches[0].wait()
    grouped = dot(gather, arrived[...]).astype(bf16)
    for part, fetch in zip(parts, fetches[1:]):
        fetch.wait()
        qkv[part] = dot(qkv_weight_t[part], grouped, NT).astype(bf16)
    fetches[-3].wait()
    fetches[-2].wait()
    scale = HEAD_DIM ** (-0.5)

    def heads(step, carry):
        some = [
            (step * unroll + u, slice(pair * PAIR, (pair + 1) * PAIR))
            for u in range(unroll)
            for pair in range(cells // PAIR)
        ]

        def rows(part, e):
            return pl.ds(pl.multiple_of(part * width + e * HEAD_DIM, HEAD_DIM), HEAD_DIM)

        def q(e, at):
            return qkv[rows(0, e), at]

        def k(e, at):
            return qkv[rows(1, e), at]

        def v(e, at):
            return qkv[rows(2, e), at]

        def grad(e, at):
            return grad_att[rows(0, e), at]

        scores = [pair_scores(k(*x), q(*x)) * scale + bias[x[0]] for x in some]
        grad_probs = [pair_scores(v(*x), grad(*x)) for x in some]
        lifted = [jnp.exp(y - jnp.max(y, axis=0, keepdims=True)) for y in scores]
        probs = [y / jnp.sum(y, axis=0, keepdims=True) for y in lifted]
        probs_low = [pair_diagonal(y).astype(bf16) for y in probs]
        att = [dot(v(*x), y) for x, y in zip(some, probs_low)]
        to_value = [dot(grad(*x), y, NT) for x, y in zip(some, probs_low)]
        grad_scores = []
        for y, z in zip(probs, grad_probs):
            product = y * z
            inner = product - y * jnp.sum(product, axis=0, keepdims=True)
            grad_scores.append(pair_diagonal(inner).astype(bf16))
        to_query = [dot(k(*x), y) * scale for x, y in zip(some, grad_scores)]
        to_key = [dot(q(*x), y, NT) * scale for x, y in zip(some, grad_scores)]
        for i, (e, at) in enumerate(some):
            att_ref[rows(0, e), at] = att[i].astype(bf16)
            grad_qkv[rows(0, e), at] = to_query[i].astype(bf16)
            grad_qkv[rows(1, e), at] = to_key[i].astype(bf16)
            grad_qkv[rows(2, e), at] = to_value[i].astype(bf16)
        return carry

    lax.fori_loop(0, HEADS // unroll, heads, 0)
    fetches[-1].wait()
    grad = dot(qkv_weight[...], grad_qkv[...]).astype(bf16)
    grad_ref[...] = dot(position_by_row(cells, slots, blocks, 0), grad, NT).astype(bf16)


def mix(slots, blocks, out_weight_t_ref, att_ref, mixed_ref):
    mixed = dot(out_weight_t_ref[...], att_ref[...]).astype(bf16)
    scatter = position_by_row(att_ref.shape[1], slots, blocks, 0)
    mixed_ref[...] = dot(scatter, mixed, NT).astype(bf16)


def products_kernel(slots, blocks, cot_ref, att_ref, out_weight_t_ref, mixed_ref, out_ref):
    out_ref[...] = dot(cot_ref[...], att_ref[...], NT).astype(bf16)
    mix(slots, blocks, out_weight_t_ref, att_ref, mixed_ref)


def halves_kernel(
    slots, blocks, flags_ref, cot_ref, att_ref, out_weight_t_ref, mixed_ref, kept_ref, sent_ref, part
):
    lats, chips, cols, rows = kept_ref.shape
    core = flags_ref[2]
    for a in range(lats):
        part[...] = dot(cot_ref[...], att_ref[a * rows : (a + 1) * rows], NT).astype(bf16)
        for chip in range(chips):
            kept_ref[a, chip] = part[pl.ds(pl.multiple_of((2 * chip + core) * cols, 16), cols)]
            sent_ref[a, chip] = part[pl.ds(pl.multiple_of((2 * chip + 1 - core) * cols, 16), cols)]
    mix(slots, blocks, out_weight_t_ref, att_ref, mixed_ref)


def join_halves_kernel(flags_ref, kept_ref, met_ref, out_ref, sent_ref):
    lat = jnp.minimum(flags_ref[0], 1)
    out_ref[...] = (kept_ref[lat].astype(f32) + met_ref[lat].astype(f32)).astype(bf16)
    sent_ref[...] = (kept_ref[1 - lat].astype(f32) + met_ref[1 - lat].astype(f32)).astype(bf16)


def leave_kernel(pattern_ref, mixed_ref, h_ref, out_ref):
    mixed = dot(by_cell(pattern_ref[...], h_ref.shape[0]), mixed_ref[...])
    out_ref[...] = (h_ref[...].astype(f32) + mixed).astype(bf16)


def return_kernel(
    flags_ref, pattern_ref, arrived_ref, h_ref, cot_ref, gain_ref,
    field_ref, before_ref, after_ref, even_ref, odd_ref,
    grad_ref, sums_ref, message_ref, columns_ref, pad, normed_grad,
):
    rows, cols, width = field_ref.shape
    fill_pad(pad, flags_ref, field_ref, before_ref, after_ref, even_ref, odd_ref)
    normed_grad[...] = dot(by_cell(pattern_ref[...], rows * cols), arrived_ref[...])
    gain = gain_ref[...]

    def fold(x):
        return jnp.sum(x.reshape(cols // 8, 8, width), axis=0)

    sums = [jnp.zeros((8, width), f32) for _ in range(10)]
    for row in range(rows):
        at = slice(row * cols, (row + 1) * cols)
        xhat, deviation = normalized(h_ref[at].astype(f32))
        grad = normed_grad[at]
        sums[9] = sums[9] + fold(grad * xhat)
        u = grad * gain
        inner = u - jnp.mean(u, axis=-1, keepdims=True)
        inner = inner - xhat * jnp.mean(u * xhat, axis=-1, keepdims=True)
        grad_h = (cot_ref[at].astype(f32) + deviation * inner).astype(bf16)
        grad_ref[row] = grad_h
        grad_h = grad_h.astype(f32)
        for a in range(3):
            for b in range(3):
                moved = pad[row + a, EDGE - 1 + b : EDGE - 1 + b + cols]
                sums[3 * a + b] = sums[3 * a + b] + fold(moved * grad_h)
    for i in range(10):
        sums_ref[i : i + 1] = jnp.sum(sums[i], axis=0, keepdims=True)
    sums_ref[10:16] = jnp.zeros((6, width), f32)
    rim_cells(flags_ref, grad_ref, message_ref.at[:cols], columns_ref)
    total = sums_ref[...]
    high = total.astype(bf16)
    message_ref[cols : cols + 16] = high
    message_ref[cols + 16 :] = (total - high.astype(f32)).astype(bf16)


def spread_kernel(
    flags_ref, field_ref, before_ref, after_ref, even_ref, odd_ref, taps_ref, out_ref, pad
):
    rows, cols, _ = field_ref.shape
    fill_pad(pad, flags_ref, field_ref, before_ref, after_ref, even_ref, odd_ref)
    taps = taps_ref[...]
    for row in range(rows):
        out_ref[row] = taps_row(pad, taps, row, cols, True).astype(bf16)


def swap_pairs(size, bit):
    return [(i, i ^ bit) for i in range(size)]


def lat_rims(field, met):
    if lax.axis_size("lat") == 2:
        return met, met
    up = [(i, i + 1) for i in range(lax.axis_size("lat") - 1)]
    before = lax.ppermute(field[-1], "lat", up)
    after = lax.ppermute(field[0], "lat", [(j, i) for i, j in up])
    return before, after


def lon_rims(flags, rows, columns, riders=None):
    lon_count = lax.axis_size("lon")
    before, after = rows
    even = flags[2] == 0

    def column(which, last):
        at = before.shape[0] - 1

        def corner(row, there):
            cell = jnp.where(last, row[at:], row[:1])
            return jnp.where(there, cell, jnp.zeros_like(cell))

        return jnp.concatenate(
            [corner(before, flags[0] != 0), columns[which], corner(after, flags[1] != 0)], axis=0
        )

    sent = column(0, even)
    if riders is not None:
        sent = jnp.concatenate([riders, sent], axis=0)
    met_even = lax.ppermute(sent, "lon", swap_pairs(lon_count, 1))
    odd_pairs = [(i, (i + 1 if i % 2 else i - 1) % lon_count) for i in range(lon_count)]
    met_odd = lax.ppermute(column(1, jnp.logical_not(even)), "lon", odd_pairs)
    if riders is None:
        return met_even, met_odd
    count = riders.shape[0]
    return met_even[count:], met_odd, met_even[:count]


def exchange(rows):
    blocks = lax.axis_size("lat") * lax.axis_size("lon")
    cells, width = rows.shape
    sent = rows.reshape(blocks, cells // blocks, width)
    return lax.all_to_all(sent, AXES, split_axis=0, concat_axis=0, tiled=True).reshape(cells, width)


def attended_products(slots, blocks, flags, cot_cols, att, out_weight_t):
    width, cells = att.shape
    lat_count, lon_count = lax.axis_size("lat"), lax.axis_size("lon")
    rows, cols = width // lat_count, width // lon_count
    mixed_shape = shape((cells, width), bf16)
    if lat_count != 2 or lon_count % 4 or lon_count & (lon_count - 1) or rows % 128 or cols % 16:
        mixed, parts = call(
            lambda *refs: products_kernel(slots, blocks, *refs),
            "attended_products", [mixed_shape, shape((width, width), bf16)],
            [cot_cols, att, out_weight_t],
        )
        parts = parts.reshape(lon_count, cols, lat_count, rows).transpose(2, 0, 1, 3)
        parts = parts.reshape(lat_count * lon_count, cols, rows)
        parts = lax.all_to_all(parts, AXES, split_axis=0, concat_axis=0, tiled=True)
        return mixed, jnp.sum(parts.astype(f32), axis=0)
    halves = shape((lat_count, lon_count // 2, cols, rows), bf16)
    quarters = shape((lon_count // 2, cols, rows), bf16)
    mixed, kept, sent = call(
        lambda *refs: halves_kernel(slots, blocks, *refs),
        "attended_products", [mixed_shape, halves, halves],
        [flags, cot_cols, att, out_weight_t],
        [pltpu.VMEM((width, rows), bf16)], specs={0: SMEM},
    )
    met = lax.ppermute(sent, "lon", swap_pairs(lon_count, 1))
    kept, sent = call(
        join_halves_kernel, "project_join", [quarters, quarters], [flags, kept, met], specs={0: SMEM}
    )
    met = lax.ppermute(sent, "lat", swap_pairs(2, 1))
    parts = (kept.astype(f32) + met.astype(f32)).astype(bf16)
    kept, sent = halved(parts, 2)
    return mixed, (kept, lax.ppermute(sent, "lon", swap_pairs(lon_count, 2)))


def halved(parts, bit):
    mine = lax.rem(lax.div(lax.axis_index("lon"), bit), 2)
    pairs = parts.reshape(parts.shape[0] // 2, 2, *parts.shape[1:])
    kept = lax.dynamic_index_in_dim(pairs, mine, 1, keepdims=False)
    return kept, lax.dynamic_index_in_dim(pairs, 1 - mine, 1, keepdims=False)


def two_terms(x):
    high = x.astype(bf16)
    return jnp.concatenate([high, (x - high.astype(f32)).astype(bf16)], axis=0)


def one_term(x):
    half = x.shape[0] // 2
    return x[:half].astype(f32) + x[half:].astype(f32)


def total_over(axis, x):
    size, bit = lax.axis_size(axis), 1
    if size & (size - 1):
        return lax.psum(x, axis)
    while bit < size:
        x = x + lax.ppermute(x, axis, swap_pairs(size, bit))
        bit *= 2
    return x


def body(
    fields, conv_kernel, layer_norm_gain, qkv_weight, out_weight, score_bias, pattern, cotangent
):
    rows, cols, width = fields.shape
    cells = rows * cols
    lat_count, lon_count = lax.axis_size("lat"), lax.axis_size("lon")
    blocks = lat_count * lon_count
    slots = cells // blocks
    scale_everywhere = 1.0 / math.sqrt(cells * blocks)
    pattern_row = pattern.reshape(1, cells)
    gain = layer_norm_gain.reshape(1, width)
    cot_rows = cotangent.reshape(cells, width)
    qkv_weight_t = qkv_weight.T
    out_weight_t = out_weight.T
    bias = jnp.swapaxes(score_bias, 1, 2)
    bias = jnp.concatenate([bias, bias], axis=2)
    pad = pltpu.VMEM((rows + 2, cols + 2 * EDGE, width), f32)
    rows_shape = shape((cells, width), bf16)
    cols_shape = shape((width, cells), bf16)
    tall_shape = shape((3 * width, cells), bf16)

    lat, lon = lax.axis_index("lat"), lax.axis_index("lon")
    flags = jnp.stack([lat, lat_count - 1 - lat, lax.rem(lon, 2)]).astype(jnp.int32)
    row_shape, columns_shape = shape((cols, width), bf16), shape((2, rows, width), bf16)

    cot_packed, row, columns = call(
        start_kernel, "start", [rows_shape, row_shape, columns_shape],
        [flags, pattern_row, cot_rows, fields], specs={0: SMEM}, mib=BIG,
    )
    met = lax.ppermute(row, "lat", swap_pairs(2, 1)) if lat_count == 2 else None
    cot_arrived = exchange(cot_packed)
    grad_att, cot_cols = call(
        lambda *refs: cot_kernel(slots, blocks, *refs),
        "cotangent_products", [cols_shape, cols_shape], [cot_arrived, out_weight],
    )

    beside = lat_rims(fields, met)
    beside = (*beside, *lon_rims(flags, beside, columns))
    h, packed = call(
        enter_kernel, "convolve_normalize_pack", [rows_shape, rows_shape],
        [flags, pattern_row, fields, *beside, conv_kernel, gain],
        [pad, pltpu.VMEM((cells, width), bf16)], specs={0: SMEM}, mib=BIG,
    )
    arrived = exchange(packed)
    weight_shape = (width, 3 * width)
    grad_grouped, att = call(
        lambda *refs: attention_kernel(slots, blocks, UNROLL, *refs),
        "attention", [rows_shape, cols_shape],
        [arrived, qkv_weight_t, bias, grad_att, qkv_weight],
        [
            pltpu.VMEM((cells, width), bf16), pltpu.VMEM(weight_shape[::-1], bf16),
            pltpu.VMEM(bias.shape, f32), pltpu.VMEM((width, cells), bf16),
            pltpu.VMEM(weight_shape, bf16), pltpu.VMEM((3 * width, cells), bf16),
            pltpu.VMEM((3 * width, cells), bf16), pltpu.SemaphoreType.DMA((10,)),
        ],
        flops=12_000_000_000, specs=dict.fromkeys(range(5), ANY), mib=BIG,
    )
    grad_home = exchange(grad_grouped)
    mixed, project = attended_products(slots, blocks, flags, cot_cols, att, out_weight_t)
    grad_home, mixed = lax.optimization_barrier((grad_home, mixed))
    mixed_home = exchange(mixed)

    grad_h, sums, message, columns = call(
        return_kernel, "normalize_back",
        [
            shape(fields.shape, bf16), shape((16, width), f32),
            shape((cols + 32, width), bf16), columns_shape,
        ],
        [flags, pattern_row, grad_home, h, cot_rows, gain, fields, *beside],
        [pad, pltpu.VMEM((cells, width), f32)], specs={0: SMEM},
    )
    if lat_count == 2:
        met = lax.ppermute(message, "lat", swap_pairs(2, 1))
        sums = sums + one_term(met[cols:])
        beside = lat_rims(grad_h, met[:cols])
    else:
        sums = total_over("lat", sums)
        beside = lat_rims(grad_h, None)
    staged = isinstance(project, tuple)
    if staged:
        even, odd, met = lon_rims(flags, beside, columns, two_terms(sums))
        beside = (*beside, even, odd)
        sums = sums + one_term(met)
        sums = sums + lax.ppermute(sums, "lon", swap_pairs(lon_count, 2))
        sums, odd = lax.optimization_barrier((sums, odd))
        beside = (*beside[:2], even, odd)
        project = (project[0].astype(f32) + project[1].astype(f32)).astype(bf16)
        bit = 4
        while bit < lon_count:
            if 2 * bit == lon_count:
                sums, mixed_home = lax.optimization_barrier((sums, mixed_home))
            kept, sent = halved(project, bit)
            high_low = two_terms(sums).reshape(-1, sent.shape[-1])
            sent = sent.reshape(-1, sent.shape[-1])
            met = lax.ppermute(
                jnp.concatenate([high_low, sent], axis=0), "lon", swap_pairs(lon_count, bit)
            )
            sums = sums + one_term(met[: high_low.shape[0]].reshape(2 * sums.shape[0], width))
            project = kept.astype(f32) + met[high_low.shape[0] :].reshape(kept.shape).astype(f32)
            bit *= 2
            if bit < lon_count:
                project = project.astype(bf16)
        grad_project = project[0].T * scale_everywhere
    else:
        beside = (*beside, *lon_rims(flags, beside, columns))
        sums = total_over("lon", sums)
        grad_project = project.T * scale_everywhere
    sums = sums * scale_everywhere
    grad_fields = call(
        spread_kernel, "convolve_back", [shape(fields.shape, bf16)],
        [flags, grad_h, *beside, conv_kernel], [pad], specs={0: SMEM},
    )[0]
    block_out = call(leave_kernel, "block_out", [rows_shape], [pattern_row, mixed_home, h])[0]
    return (
        block_out.reshape(rows, cols, width),
        grad_fields,
        grad_project,
        sums[:9].reshape(3, 3, width),
        sums[9],
    )


def solution(mesh):
    placed = (
        P("lat", "lon", None),
        P(),
        P(),
        P(),
        P(),
        P(),
        P("lat", "lon", None),
        P("lat", "lon", None),
    )
    return jax.shard_map(
        body,
        mesh=mesh,
        in_specs=placed,
        out_specs=(P("lat", "lon", None), P("lat", "lon", None), P("lat", "lon"), P(), P()),
        check_vma=False,
    )
```

time: 125 us -> 110 us (0.88)
  waiting for transfers between devices: 38.9 us -> 29 us
  starting transfers between devices: 35.5 us -> 30.4 us
  other arithmetic: 5.65 us -> 2.89 us
  Pallas kernels: 23.9 us -> 25.5 us
    all_to_all x4, waiting for transfers between devices: 10.7 us -> 6.5 us  [exchange(): lax.all_to_all(sent, AXES, split_axis=0, concat_axis=0, tiled=True)]
    all_to_all x1 -> x0, starting transfers between devices: 3.42 us -> none  [scattered_project(): lax.all_to_all(parts, 'lon', split_axis=0, concat_axis=0, axis_index_grou...]
    ppermute x11, waiting for transfers between devices: 24.6 us -> 21.7 us  [the longest x2 6.64 us: body(): lax.ppermute(jnp.concatenate([high_low, sent], axis=0), 'lon', swap_pairs...]
    ppermute x1, waiting for transfers between devices: 3.61 us -> 0.76 us  [body(): met = lax.ppermute(message, 'lat', swap_pairs(2, 1))]
    select_n x3 -> x6, other arithmetic: 2.43 us -> 0.07 us  [corner(): return jnp.where(there, cell, jnp.zeros_like(cell))]
    pallas_call x10 -> x9, Pallas kernels: 23.9 us -> 25.5 us  [call(): pl.pallas_call(kernel, name=name, grid=(1,), out_shape=list(out_shape), i...]
    reshape x1, local copies, waits for them, and re-layouts: 0.01 us -> 1.27 us  [body(): gain = layer_norm_gain.reshape(1, width)]
    unnamed x59 -> x47, local copies, waits for them, and re-layouts: 16.3 us -> 16.3 us
  transfers between devices with their start and end apart: 17 -> 16, of which waited for: 10 -> 11; matrix products, arithmetic and copies ran while one was open for 10% -> 10% of each run, Pallas kernels for 6% -> 12%
where the time goes in v3:
time: 110 us; the launch traced here: 109 us
  starting transfers between devices  30.4 us (28%)
  waiting for transfers between devices  29 us (26%)
  Pallas kernels  25.5 us (23%)
  local copies, waits for them, and re-layouts  19.8 us (18%)
  other arithmetic  2.89 us (3%)
  between operations  1.11 us (1%)
    pallas_call x9, Pallas kernels, call(): pl.pallas_call(kernel, name=name, grid=(1,), out_shape=list(out_shape), i...  25.5 us
    unnamed x47, local copies, waits for them, and re-layouts  16.3 us
    all_to_all x4, starting transfers between devices, exchange(): lax.all_to_all(sent, AXES, split_axis=0, concat_axis=0, tiled=True)  13.6 us
    ppermute x2, starting transfers between devices, lon_rims(): met_odd = lax.ppermute(column(1, jnp.logical_not(even)), 'lon', odd_pairs)  7.83 us
    ppermute x2, waiting for transfers between devices, body(): lax.ppermute(jnp.concatenate([high_low, sent], axis=0), 'lon', swap_pairs...  6.64 us
    all_to_all x4, waiting for transfers between devices, exchange(): lax.all_to_all(sent, AXES, split_axis=0, concat_axis=0, tiled=True)  6.5 us
    ppermute x2, waiting for transfers between devices, lon_rims(): met_odd = lax.ppermute(column(1, jnp.logical_not(even)), 'lon', odd_pairs)  6.29 us
    ppermute x1, waiting for transfers between devices, body(): sums = sums + lax.ppermute(sums, 'lon', swap_pairs(lon_count, 2))  3 us
  transfers between devices with their start and end apart: 16, of which 11 were waited for; matrix products, arithmetic and copies ran while one was open for 10% of the time, Pallas kernels for 12%

profile of v3, /device:TPU:0, one launch (start us, length us, event | category | flops | bytes accessed | tf_op | source)
XLA Modules:
  0.0 108.7 jit_solution(10163602909907301942)
XLA Ops:
  0.6 0.7 pad_add_fusion.flags_ref.refs_0_
  1.3 2.2 %start.1 = (bf16[256,768]{1,0:T(8,128)(2,1)}, bf16[32,768]{1,0:T(8,128)(2,1)}, bf16[2,8,768]{2,1,0:T(8,128)(2,1)}) custom-call(s32[3]{0:T(128)} %pad_add_fusion.flags_ref.refs_0_, s32[1,256]{1,0:T(1,128)} %bitcast.55, bf16[256,768]{1,0:T(8,128)(2,1)} %bitcast.52, bf16[8,32,768]{2,1,0:T(8,128)(2,1)} %field_ref.5), custom_call_target="tpu_custom_call" | custom-call | bytes 1254412 | tf_op jit(solution)/shard_map/start/pallas_call | solution.py:40
  3.5 2.9 %collective-permute-start = (bf16[32,768]{1,0:T(8,128)(2,1)}, bf16[32,768]{1,0:T(8,128)(2,1)S(1)}, u32[]{:S(2)}, u32[]{:S(2)}) collective-permute-start(bf16[32,768]{1,0:T(8,128)(2,1)} %get-tuple-element.29), channel_id=1, source_target_pairs={{0,16},{16,0},{1,17},{17,1},{2,18},{18,2},{3,19},{19,3},{4,20},{20... | collective-permute-start | bytes 147464 | tf_op jit(solution)/shard_map/ppermute | solution.py:457
  6.4 4.9 %all-to-all-start.1 = ((bf16[32,8,768]{2,1,0:T(8,128)(2,1)}), bf16[32,8,768]{2,1,0:T(8,128)(2,1)S(1)}, u32[]{:S(2)}, u32[]{:S(2)}) async-start(bf16[32,8,768]{2,1,0:T(8,128)(2,1)} %bitcast.66), calls=%async_computation.1 | async-start | bytes 786432 | tf_op jit(solution)/shard_map/all_to_all | solution.py:365
  11.4 0.7 slice_bitcast_fusion.2
  12.2 4.4 %collective-permute-start.2 = (bf16[10,768]{1,0:T(8,128)(2,1)S(1)}, bf16[10,768]{1,0:T(8,128)(2,1)S(1)}, u32[]{:S(2)}, u32[]{:S(2)}) collective-permute-start(bf16[10,768]{1,0:T(8,128)(2,1)S(1)} %pad_maximum_fusion.6), channel_id=1, source_target_pairs={{0,15},{1,2},{2,1},{3,4},{4,3},{5,6},{6,5},{7,8},{8,7},{9,10},{10,... | collective-permute-start | bytes 46088 | tf_op jit(solution)/shard_map/ppermute | solution.py:354
  16.6 0.1 collective-permute-start.1
  16.7 1.3 %reshape.103.gain_ref = f32[1,768]{1,0:T(1,128)} reshape(f32[768]{0:T(1024)} %param.10) | data formatting | bytes 6144 | tf_op jit(solution)/shard_map/reshape | solution.py:438
  17.9 5.5 %collective-permute-done.2.odd_ref = bf16[10,768]{1,0:T(8,128)(2,1)S(1)} collective-permute-done((bf16[10,768]{1,0:T(8,128)(2,1)S(1)}, bf16[10,768]{1,0:T(8,128)(2,1)S(1)}, u32[]{:S(2)}, u32[]{:S(2)}) %collective-permute-start.2) | collective-permute-done | bytes 15392 | tf_op jit(solution)/shard_map/ppermute | solution.py:354
  23.4 0.6 copy-done.12
  24.0 0.6 copy-done.14
  24.6 3.3 %convolve_normalize_pack.1 = (bf16[256,768]{1,0:T(8,128)(2,1)}, bf16[256,768]{1,0:T(8,128)(2,1)}) custom-call(s32[3]{0:T(128)} %pad_add_fusion.flags_ref.refs_0_, s32[1,256]{1,0:T(1,128)} %bitcast.56, bf16[8,32,768]{2,1,0:T(8,128)(2,1)} %field_ref.5, bf16[32,768]{1,0:T(8,128)(2,1)} %copy-done.5, bf16[32,768]{1,0:T(8,128)(2,1)} %copy-done.5, ...), custom_call_target="tpu_custom_call" | custom-call | bytes 1340428 | tf_op jit(solution)/shard_map/convolve_normalize_pack/pallas_call | solution.py:40
  27.9 3.2 %all-to-all-start = ((bf16[32,8,768]{2,1,0:T(8,128)(2,1)}), bf16[32,8,768]{2,1,0:T(8,128)(2,1)S(1)}, u32[]{:S(2)}, u32[]{:S(2)}) async-start(bf16[32,8,768]{2,1,0:T(8,128)(2,1)} %bitcast.67), calls=%async_computation | async-start | bytes 786432 | tf_op jit(solution)/shard_map/all_to_all | solution.py:365
  31.1 0.0 copy-start.20
  31.1 5.9 %copy.16 = bf16[768,2304]{0,1:T(8,128)(2,1)} copy(bf16[768,2304]{1,0:T(8,128)(2,1)} %refs_4_.1) | data formatting | bytes 7077888 | tf_op args[3]
  37.0 0.3 copy.17
  37.2 1.2 %pad_maximum_fusion.refs_2_ = f32[24,64,128]{2,1,0:T(8,128)} fusion(f32[24,64,64]{2,1,0:T(8,128)S(1)} %bitcast.60), kind=kLoop, calls=%fused_computation | loop fusion | flops 196608 | bytes 1179648 | tf_op jit(solution)/shard_map/concatenate | solution.py:443
  38.4 0.7 cotangent_products.1
  39.1 0.0 copy-start.8
  39.1 0.7 copy-done.8
  39.9 0.8 copy-done.19
  40.6 3.5 %all-to-all-done = bf16[32,8,768]{2,1,0:T(8,128)(2,1)S(1)} async-done(((bf16[32,8,768]{2,1,0:T(8,128)(2,1)}), bf16[32,8,768]{2,1,0:T(8,128)(2,1)S(1)}, u32[]{:S(2)}, u32[]{:S(2)}) %all-to-all-start) | async-done | bytes 393248 | tf_op jit(solution)/shard_map/all_to_all | solution.py:365
  44.2 0.7 copy-done.21
  44.9 10.7 %attention.1 = (bf16[256,768]{1,0:T(8,128)(2,1)}, bf16[768,256]{1,0:T(8,128)(2,1)}) custom-call(bf16[256,768]{1,0:T(8,128)(2,1)} %bitcast.68, bf16[2304,768]{1,0:T(8,128)(2,1)} %bitcast.59, f32[24,64,128]{2,1,0:T(8,128)} %pad_maximum_fusion.refs_2_, bf16[768,256]{1,0:T(8,128)(2,1)} %copy-done.19, bf16[768,2304]{1,0:T(8,128)(2,1)} %refs_4_.1), custom_call_target="tpu_custom_call" | custom-call | flops 12000000000 | bytes 9437184 | tf_op jit(solution)/shard_map/attention/pallas_call | solution.py:40
  55.6 0.0 copy-start.1
  55.7 0.0 copy-start.16
  55.7 2.7 %all-to-all-start.2 = ((bf16[32,8,768]{2,1,0:T(8,128)(2,1)}), bf16[32,8,768]{2,1,0:T(8,128)(2,1)S(1)}, u32[]{:S(2)}, u32[]{:S(2)}) async-start(bf16[32,8,768]{2,1,0:T(8,128)(2,1)} %bitcast.65), calls=%async_computation.2 | async-start | bytes 786432 | tf_op jit(solution)/shard_map/all_to_all | solution.py:365
  58.4 0.6 copy.18
  59.1 1.0 copy-done.9
  60.1 1.0 copy-done.10
  61.1 2.1 %attended_products.1 = (bf16[256,768]{1,0:T(8,128)(2,1)S(1)}, bf16[2,8,48,384]{3,2,1,0:T(8,128)(2,1)S(1)}, bf16[2,8,48,384]{3,2,1,0:T(8,128)(2,1)}) custom-call(s32[3]{0:T(128)S(1)} %copy-done.17, bf16[768,256]{1,0:T(8,128)(2,1)S(1)} %copy-done.9, bf16[768,256]{1,0:T(8,128)(2,1)S(1)} %copy-done.10, bf16[768,768]{1,0:T(8,128)(2,1)S(1)} %bitcast.48), custom_call_target="tpu_custom_call" | custom-call | bytes 3538956 | tf_op jit(solution)/shard_map/attended_products/pallas_call | solution.py:40
  63.2 0.7 copy-done.7
  63.9 0.1 collective-permute-start.7
  64.1 2.1 %collective-permute-done.7.met_ref = bf16[2,8,48,384]{3,2,1,0:T(8,128)(2,1)S(1)} collective-permute-done((bf16[2,8,48,384]{3,2,1,0:T(8,128)(2,1)}, bf16[2,8,48,384]{3,2,1,0:T(8,128)(2,1)S(1)}, u32[]{:S(2)}, u32[]{:S(2)}) %collective-permute-start.7) | collective-permute-done | bytes 589856 | tf_op jit(solution)/shard_map/ppermute | solution.py:391
  66.2 0.7 project_join.1
  66.9 1.7 %collective-permute-start.8 = (bf16[8,48,384]{2,1,0:T(8,128)(2,1)S(1)}, bf16[8,48,384]{2,1,0:T(8,128)(2,1)S(1)}, u32[]{:S(2)}, u32[]{:S(2)}) collective-permute-start(bf16[8,48,384]{2,1,0:T(8,128)(2,1)S(1)} %get-tuple-element.47), channel_id=1, source_target_pairs={{0,16},{16,0},{1,17},{17,1},{2,18},{18,2},{3,19},{19,3},{4,20},{20... | collective-permute-start | bytes 884744 | tf_op jit(solution)/shard_map/ppermute | solution.py:395
  68.6 3.0 %all-to-all-done.2 = bf16[32,8,768]{2,1,0:T(8,128)(2,1)S(1)} async-done(((bf16[32,8,768]{2,1,0:T(8,128)(2,1)}), bf16[32,8,768]{2,1,0:T(8,128)(2,1)S(1)}, u32[]{:S(2)}, u32[]{:S(2)}) %all-to-all-start.2) | async-done | bytes 393248 | tf_op jit(solution)/shard_map/all_to_all | solution.py:365
  71.6 1.0 copy-done.3
  72.6 0.8 copy-done.6
  73.4 0.7 copy-done.13
  74.1 0.7 copy-done.15
  74.8 2.5 %normalize_back.1 = (bf16[8,32,768]{2,1,0:T(8,128)(2,1)S(1)}, f32[16,768]{1,0:T(8,128)S(1)}, bf16[64,768]{1,0:T(8,128)(2,1)S(1)}, bf16[2,8,768]{2,1,0:T(8,128)(2,1)S(1)}) custom-call(s32[3]{0:T(128)S(1)} %copy-done.17, s32[1,256]{1,0:T(1,128)S(1)} %bitcast.57, bf16[256,768]{1,0:T(8,128)(2,1)S(1)} %bitcast.50, bf16[256,768]{1,0:T(8,128)(2,1)S(1)} %copy-done.3, ...), custom_call_target="tpu_custom_call" | custom-call | bytes 2271244 | tf_op jit(solution)/shard_map/normalize_back/pallas_call | solution.py:40
  77.3 1.1 %collective-permute-start.3 = (bf16[64,768]{1,0:T(8,128)(2,1)S(1)}, bf16[64,768]{1,0:T(8,128)(2,1)S(1)}, u32[]{:S(2)}, u32[]{:S(2)}) collective-permute-start(bf16[64,768]{1,0:T(8,128)(2,1)S(1)} %get-tuple-element.41), channel_id=1, source_target_pairs={{0,16},{16,0},{1,17},{17,1},{2,18},{18,2},{3,19},{19,3},{4,20},{20... | collective-permute-start | bytes 294920 | tf_op jit(solution)/shard_map/ppermute | solution.py:500
  78.4 2.8 %all-to-all-start.3 = ((bf16[32,8,768]{2,1,0:T(8,128)(2,1)}), bf16[32,8,768]{2,1,0:T(8,128)(2,1)S(1)}, u32[]{:S(2)}, u32[]{:S(2)}) async-start(bf16[32,8,768]{2,1,0:T(8,128)(2,1)} %bitcast.54), calls=%async_computation.3 | async-start | bytes 786432 | tf_op jit(solution)/shard_map/all_to_all | solution.py:365
  81.2 0.8 collective-permute-done.3
  82.1 3.5 %collective-permute-start.6 = (bf16[10,768]{1,0:T(8,128)(2,1)S(1)}, bf16[10,768]{1,0:T(8,128)(2,1)S(1)}, u32[]{:S(2)}, u32[]{:S(2)}) collective-permute-start(bf16[10,768]{1,0:T(8,128)(2,1)S(1)} %pad_maximum_fusion.7), channel_id=1, source_target_pairs={{0,15},{1,2},{2,1},{3,4},{4,3},{5,6},{6,5},{7,8},{8,7},{9,10},{10,... | collective-permute-start | bytes 46088 | tf_op jit(solution)/shard_map/ppermute | solution.py:354
  85.5 0.2 concatenate.30
  85.7 0.1 collective-permute-start.4
  85.8 0.1 add_convert_fusion
  85.9 1.2 %collective-permute-done.4 = bf16[42,768]{1,0:T(8,128)(2,1)S(1)} collective-permute-done((bf16[42,768]{1,0:T(8,128)(2,1)S(1)}, bf16[42,768]{1,0:T(8,128)(2,1)S(1)}, u32[]{:S(2)}, u32[]{:S(2)}) %collective-permute-start.4) | collective-permute-done | bytes 64544 | tf_op jit(solution)/shard_map/ppermute | solution.py:352
  87.0 0.1 collective-permute-start.5
  87.2 2.1 %collective-permute-start.9 = (bf16[4,48,384]{2,1,0:T(8,128)(2,1)S(1)}, bf16[4,48,384]{2,1,0:T(8,128)(2,1)S(1)}, u32[]{:S(2)}, u32[]{:S(2)}) collective-permute-start(bf16[4,48,384]{2,1,0:T(8,128)(2,1)S(1)} %dynamic-slice_bitcast_fusion), channel_id=1, source_target_pairs={{0,2},{1,3},{2,0},{3,1},{4,6},{5,7},{6,4},{7,5},{8,10},{9,11},{10,... | collective-permute-start | bytes 442376 | tf_op jit(solution)/shard_map/ppermute | solution.py:398
  89.2 3.0 %collective-permute-done.5 = f32[16,768]{1,0:T(8,128)S(1)} collective-permute-done((f32[16,768]{1,0:T(8,128)S(1)}, f32[16,768]{1,0:T(8,128)S(1)}, u32[]{:S(2)}, u32[]{:S(2)}) %collective-permute-start.5) | collective-permute-done | bytes 49184 | tf_op jit(solution)/shard_map/ppermute | solution.py:511
  92.2 0.8 collective-permute-done.6.odd_ref
  93.1 2.5 %collective-permute-done.9 = bf16[4,48,384]{2,1,0:T(8,128)(2,1)S(1)} collective-permute-done((bf16[4,48,384]{2,1,0:T(8,128)(2,1)S(1)}, bf16[4,48,384]{2,1,0:T(8,128)(2,1)S(1)}, u32[]{:S(2)}, u32[]{:S(2)}) %collective-permute-start.9) | collective-permute-done | bytes 147488 | tf_op jit(solution)/shard_map/ppermute | solution.py:398
  95.7 0.1 collective-permute-start.10
  95.8 4.8 %collective-permute-done.10 = bf16[160,384]{1,0:T(8,128)(2,1)S(1)} collective-permute-done((bf16[160,384]{1,0:T(8,128)(2,1)S(1)}, bf16[160,384]{1,0:T(8,128)(2,1)S(1)}, u32[]{:S(2)}, u32[]{:S(2)}) %collective-permute-start.10) | collective-permute-done | bytes 122912 | tf_op jit(solution)/shard_map/ppermute | solution.py:522
  100.9 0.7 collective-permute-start.11
  101.6 2.3 %convolve_back.1 = bf16[8,32,768]{2,1,0:T(8,128)(2,1)} custom-call(s32[3]{0:T(128)S(1)} %copy-done.17, bf16[8,32,768]{2,1,0:T(8,128)(2,1)S(1)} %get-tuple-element.50.field_ref, bf16[32,768]{1,0:T(8,128)(2,1)S(1)} %slice.128.before_ref.after_ref, bf16[32,768]{1,0:T(8,128)(2,1)S(1)} %slice.128.before_ref.after_ref, bf16[10,768]{1,0:T(8,128)(2,1)S(1)} %slice.129.even_ref, ...), custom_call_target="tpu_custom_call" | custom-call | bytes 943116 | tf_op jit(solution)/shard_map/convolve_back/pallas_call | solution.py:40
  103.9 1.0 block_out.1
  104.9 1.8 %collective-permute-done.11 = bf16[112,384]{1,0:T(8,128)(2,1)S(1)} collective-permute-done((bf16[112,384]{1,0:T(8,128)(2,1)S(1)}, bf16[112,384]{1,0:T(8,128)(2,1)S(1)}, u32[]{:S(2)}, u32[]{:S(2)}) %collective-permute-start.11) | collective-permute-done | bytes 86048 | tf_op jit(solution)/shard_map/ppermute | solution.py:522
  106.8 0.6 slice_reduce_fusion
  107.4 0.6 reshape.119
  108.0 0.6 fusion.3
  (68 shorter events, 0.6 us)
Async XLA Ops:
  3.5 8.6 %collective-permute-start = (bf16[32,768]{1,0:T(8,128)(2,1)}, bf16[32,768]{1,0:T(8,128)(2,1)S(1)}, u32[]{:S(2)}, u32[]{:S(2)}) collective-permute-start(bf16[32,768]{1,0:T(8,128)(2,1)} %get-tuple-element.29), channel_id=1, source_target_pairs={{0,16},{16,0},{1,17},{17,1},{2,18},{18,2},{3,19},{19,3},{4,20},{20... | collective-permute-start | bytes 147464 | tf_op jit(solution)/shard_map/ppermute | solution.py:457
  6.4 21.4 %all-to-all-start.1 = ((bf16[32,8,768]{2,1,0:T(8,128)(2,1)}), bf16[32,8,768]{2,1,0:T(8,128)(2,1)S(1)}, u32[]{:S(2)}, u32[]{:S(2)}) async-start(bf16[32,8,768]{2,1,0:T(8,128)(2,1)} %bitcast.66), calls=%async_computation.1 | async-start | bytes 786432 | tf_op jit(solution)/shard_map/all_to_all | solution.py:365
  12.1 11.3 %copy-start.5 = (bf16[32,768]{1,0:T(8,128)(2,1)}, bf16[32,768]{1,0:T(8,128)(2,1)S(1)}, u32[]{:S(2)}) copy-start(bf16[32,768]{1,0:T(8,128)(2,1)S(1)} %collective-permute-done.before_ref.after_ref) | copy-start | bytes 147460
  12.2 11.2 %collective-permute-start.2 = (bf16[10,768]{1,0:T(8,128)(2,1)S(1)}, bf16[10,768]{1,0:T(8,128)(2,1)S(1)}, u32[]{:S(2)}, u32[]{:S(2)}) collective-permute-start(bf16[10,768]{1,0:T(8,128)(2,1)S(1)} %pad_maximum_fusion.6), channel_id=1, source_target_pairs={{0,15},{1,2},{2,1},{3,4},{4,3},{5,6},{6,5},{7,8},{8,7},{9,10},{10,... | collective-permute-start | bytes 46088 | tf_op jit(solution)/shard_map/ppermute | solution.py:354
  16.6 6.8 %collective-permute-start.1 = (bf16[10,768]{1,0:T(8,128)(2,1)S(1)}, bf16[10,768]{1,0:T(8,128)(2,1)S(1)}, u32[]{:S(2)}, u32[]{:S(2)}) collective-permute-start(bf16[10,768]{1,0:T(8,128)(2,1)S(1)} %pad_maximum_fusion.5), channel_id=1, source_target_pairs={{0,1},{1,0},{2,3},{3,2},{4,5},{5,4},{6,7},{7,6},{8,9},{9,8},{10,11... | collective-permute-start | bytes 46088 | tf_op jit(solution)/shard_map/ppermute | solution.py:352
  23.4 0.6 copy-start.12
  24.0 0.6 copy-start.14
  27.9 16.3 %all-to-all-start = ((bf16[32,8,768]{2,1,0:T(8,128)(2,1)}), bf16[32,8,768]{2,1,0:T(8,128)(2,1)S(1)}, u32[]{:S(2)}, u32[]{:S(2)}) async-start(bf16[32,8,768]{2,1,0:T(8,128)(2,1)} %bitcast.67), calls=%async_computation | async-start | bytes 786432 | tf_op jit(solution)/shard_map/all_to_all | solution.py:365
  31.1 5.9 %copy-start.20 = (f32[24,64,64]{2,1,0:T(8,128)S(1)}, f32[24,64,64]{2,1,0:T(8,128)}, u32[]{:S(2)}) copy-start(f32[24,64,64]{2,1,0:T(8,128)} %param.13) | copy-start | bytes 1179652
  31.1 7.3 %copy-start = (bf16[768,768]{1,0:T(8,128)(2,1)S(1)}, bf16[768,768]{1,0:T(8,128)(2,1)}, u32[]{:S(2)}) copy-start(bf16[768,768]{1,0:T(8,128)(2,1)} %refs_1_.1) | copy-start | bytes 3538948
  39.1 0.7 copy-start.8
  39.9 0.8 copy-start.19
  44.1 0.7 copy-start.21
  44.9 14.2 %copy-start.17 = (s32[3]{0:T(128)S(1)}, s32[3]{0:T(128)}, u32[]{:S(2)}) copy-start(s32[3]{0:T(128)} %pad_add_fusion.flags_ref.refs_0_) | copy-start | bytes 40
  55.6 15.9 %copy-start.1 = (bf16[8,32,768]{2,1,0:T(8,128)(2,1)S(1)}, bf16[8,32,768]{2,1,0:T(8,128)(2,1)}, u32[]{:S(2)}) copy-start(bf16[8,32,768]{2,1,0:T(8,128)(2,1)} %field_ref.5) | copy-start | bytes 1179652
  55.7 15.9 %copy-start.2 = (bf16[8,32,768]{2,1,0:T(8,128)(2,1)S(1)}, bf16[8,32,768]{2,1,0:T(8,128)(2,1)}, u32[]{:S(2)}) copy-start(bf16[8,32,768]{2,1,0:T(8,128)(2,1)} %param.15) | copy-start | bytes 1179652
  55.7 15.9 %copy-start.16 = (f32[1,768]{1,0:T(1,128)S(1)}, f32[1,768]{1,0:T(1,128)}, u32[]{:S(2)}) copy-start(f32[1,768]{1,0:T(1,128)} %reshape.103.gain_ref) | copy-start | bytes 9220
  55.7 15.9 %copy-start.18 = (s32[1,1,256]{2,1,0:T(1,128)S(1)}, s32[1,1,256]{2,1,0:T(1,128)}, u32[]{:S(2)}) copy-start(s32[1,1,256]{2,1,0:T(1,128)} %param.14) | copy-start | bytes 3076
  55.7 15.9 %all-to-all-start.2 = ((bf16[32,8,768]{2,1,0:T(8,128)(2,1)}), bf16[32,8,768]{2,1,0:T(8,128)(2,1)S(1)}, u32[]{:S(2)}, u32[]{:S(2)}) async-start(bf16[32,8,768]{2,1,0:T(8,128)(2,1)} %bitcast.65), calls=%async_computation.2 | async-start | bytes 786432 | tf_op jit(solution)/shard_map/all_to_all | solution.py:365
  59.1 1.0 copy-start.9
  60.1 1.0 copy-start.10
  63.2 0.7 copy-start.7
  63.9 2.2 %collective-permute-start.7 = (bf16[2,8,48,384]{3,2,1,0:T(8,128)(2,1)}, bf16[2,8,48,384]{3,2,1,0:T(8,128)(2,1)S(1)}, u32[]{:S(2)}, u32[]{:S(2)}) collective-permute-start(bf16[2,8,48,384]{3,2,1,0:T(8,128)(2,1)} %get-tuple-element.45), channel_id=1, source_target_pairs={{0,1},{1,0},{2,3},{3,2},{4,5},{5,4},{6,7},{7,6},{8,9},{9,8},{10,11... | collective-permute-start | bytes 1769480 | tf_op jit(solution)/shard_map/ppermute | solution.py:391
  66.2 35.5 %copy-start.11 = (f32[3,3,768]{2,1,0:T(4,128)S(1)}, f32[3,3,768]{2,1,0:T(4,128)}, u32[]{:S(2)}) copy-start(f32[3,3,768]{2,1,0:T(4,128)} %taps_ref.3) | copy-start | bytes 82948
  66.9 18.9 %collective-permute-start.8 = (bf16[8,48,384]{2,1,0:T(8,128)(2,1)S(1)}, bf16[8,48,384]{2,1,0:T(8,128)(2,1)S(1)}, u32[]{:S(2)}, u32[]{:S(2)}) collective-permute-start(bf16[8,48,384]{2,1,0:T(8,128)(2,1)S(1)} %get-tuple-element.47), channel_id=1, source_target_pairs={{0,16},{16,0},{1,17},{17,1},{2,18},{18,2},{3,19},{19,3},{4,20},{20... | collective-permute-start | bytes 884744 | tf_op jit(solution)/shard_map/ppermute | solution.py:395
  71.6 1.0 copy-start.3
  72.6 0.8 copy-start.6
  73.4 0.7 copy-start.13
  74.1 0.7 copy-start.15
  77.3 26.6 %copy-start.4 = (bf16[256,768]{1,0:T(8,128)(2,1)S(1)}, bf16[256,768]{1,0:T(8,128)(2,1)}, u32[]{:S(2)}) copy-start(bf16[256,768]{1,0:T(8,128)(2,1)} %get-tuple-element.39.h_ref) | copy-start | bytes 1179652
  77.3 4.7 %collective-permute-start.3 = (bf16[64,768]{1,0:T(8,128)(2,1)S(1)}, bf16[64,768]{1,0:T(8,128)(2,1)S(1)}, u32[]{:S(2)}, u32[]{:S(2)}) collective-permute-start(bf16[64,768]{1,0:T(8,128)(2,1)S(1)} %get-tuple-element.41), channel_id=1, source_target_pairs={{0,16},{16,0},{1,17},{17,1},{2,18},{18,2},{3,19},{19,3},{4,20},{20... | collective-permute-start | bytes 294920 | tf_op jit(solution)/shard_map/ppermute | solution.py:500
  78.4 22.4 %all-to-all-start.3 = ((bf16[32,8,768]{2,1,0:T(8,128)(2,1)}), bf16[32,8,768]{2,1,0:T(8,128)(2,1)S(1)}, u32[]{:S(2)}, u32[]{:S(2)}) async-start(bf16[32,8,768]{2,1,0:T(8,128)(2,1)} %bitcast.54), calls=%async_computation.3 | async-start | bytes 786432 | tf_op jit(solution)/shard_map/all_to_all | solution.py:365
  82.1 11.0 %collective-permute-start.6 = (bf16[10,768]{1,0:T(8,128)(2,1)S(1)}, bf16[10,768]{1,0:T(8,128)(2,1)S(1)}, u32[]{:S(2)}, u32[]{:S(2)}) collective-permute-start(bf16[10,768]{1,0:T(8,128)(2,1)S(1)} %pad_maximum_fusion.7), channel_id=1, source_target_pairs={{0,15},{1,2},{2,1},{3,4},{4,3},{5,6},{6,5},{7,8},{8,7},{9,10},{10,... | collective-permute-start | bytes 46088 | tf_op jit(solution)/shard_map/ppermute | solution.py:354
  85.7 1.3 %collective-permute-start.4 = (bf16[42,768]{1,0:T(8,128)(2,1)S(1)}, bf16[42,768]{1,0:T(8,128)(2,1)S(1)}, u32[]{:S(2)}, u32[]{:S(2)}) collective-permute-start(bf16[42,768]{1,0:T(8,128)(2,1)S(1)} %concatenate.30), channel_id=1, source_target_pairs={{0,1},{1,0},{2,3},{3,2},{4,5},{5,4},{6,7},{7,6},{8,9},{9,8},{10,11... | collective-permute-start | bytes 193544 | tf_op jit(solution)/shard_map/ppermute | solution.py:352
  87.0 5.2 %collective-permute-start.5 = (f32[16,768]{1,0:T(8,128)S(1)}, f32[16,768]{1,0:T(8,128)S(1)}, u32[]{:S(2)}, u32[]{:S(2)}) collective-permute-start(f32[16,768]{1,0:T(8,128)S(1)} %add_add_fusion), channel_id=1, source_target_pairs={{0,2},{1,3},{2,0},{3,1},{4,6},{5,7},{6,4},{7,5},{8,10},{9,11},{10,... | collective-permute-start | bytes 147464 | tf_op jit(solution)/shard_map/ppermute | solution.py:511
  87.2 8.4 %collective-permute-start.9 = (bf16[4,48,384]{2,1,0:T(8,128)(2,1)S(1)}, bf16[4,48,384]{2,1,0:T(8,128)(2,1)S(1)}, u32[]{:S(2)}, u32[]{:S(2)}) collective-permute-start(bf16[4,48,384]{2,1,0:T(8,128)(2,1)S(1)} %dynamic-slice_bitcast_fusion), channel_id=1, source_target_pairs={{0,2},{1,3},{2,0},{3,1},{4,6},{5,7},{6,4},{7,5},{8,10},{9,11},{10,... | collective-permute-start | bytes 442376 | tf_op jit(solution)/shard_map/ppermute | solution.py:398
  95.7 4.9 %collective-permute-start.10 = (bf16[160,384]{1,0:T(8,128)(2,1)S(1)}, bf16[160,384]{1,0:T(8,128)(2,1)S(1)}, u32[]{:S(2)}, u32[]{:S(2)}) collective-permute-start(bf16[160,384]{1,0:T(8,128)(2,1)S(1)} %pad_maximum_fusion.1), channel_id=1, source_target_pairs={{0,4},{1,5},{2,6},{3,7},{4,0},{5,1},{6,2},{7,3},{8,12},{9,13},{10,... | collective-permute-start | bytes 368648 | tf_op jit(solution)/shard_map/ppermute | solution.py:522
  100.9 5.8 %collective-permute-start.11 = (bf16[112,384]{1,0:T(8,128)(2,1)S(1)}, bf16[112,384]{1,0:T(8,128)(2,1)S(1)}, u32[]{:S(2)}, u32[]{:S(2)}) collective-permute-start(bf16[112,384]{1,0:T(8,128)(2,1)S(1)} %pad_maximum_fusion.2), channel_id=1, source_target_pairs={{0,8},{1,9},{2,10},{3,11},{4,12},{5,13},{6,14},{7,15},{8,0},{9,1},... | collective-permute-start | bytes 258056 | tf_op jit(solution)/shard_map/ppermute | solution.py:522

commit v4 on v3

--- a/solution.py
+++ b/solution.py
@@ -12,7 +12,7 @@
 GROUP = 64
 PAIR = 2 * GROUP
 EDGE = 8
-UNROLL = 6
+UNROLL = 24
 
 epsilon = 1e-05
 f32, bf16 = jnp.float32, jnp.bfloat16
@@ -20,6 +20,7 @@
 NN = (((1,), (0,)), ((), ()))
 NT = (((1,), (1,)), ((), ()))
 TN = (((0,), (0,)), ((), ()))
+TT = (((0,), (1,)), ((), ()))
 VMEM = pl.BlockSpec(memory_space=pltpu.VMEM)
 SMEM = pl.BlockSpec(memory_space=pltpu.SMEM)
 ANY = pl.BlockSpec(memory_space=pl.ANY)
@@ -50,8 +51,20 @@
     )(*operands)
 
 
+def fetch(sems, *pairs):
+    copies = [pltpu.make_async_copy(x, y, sems.at[i]) for i, (x, y) in enumerate(pairs)]
+    for copy in copies:
+        copy.start()
+    return copies
+
+
 def shape(dims, dtype):
     return jax.ShapeDtypeStruct(dims, dtype)
+
+
+def place():
+    lat, lon = lax.axis_index("lat"), lax.axis_index("lon")
+    return lat, lax.axis_size("lat") - 1 - lat, lax.rem(lon, 2)
 
 
 def by_cell(pattern_row, cells):
@@ -66,9 +79,9 @@
     return jnp.where(place == position, 1.0, 0.0).astype(bf16)
 
 
-def rim_cells(flags_ref, field_ref, row_ref, cols_ref):
+def rim_cells(field_ref, row_ref, cols_ref):
     rows, cols, _ = field_ref.shape
-    low, even = flags_ref[0] == 0, flags_ref[2] == 0
+    low, even = place()[0] == 0, place()[2] == 0
     row_ref[...] = jnp.where(low, field_ref[rows - 1], field_ref[0])
     first = jnp.concatenate([field_ref[row, 0:1] for row in range(rows)], axis=0)
     last = jnp.concatenate([field_ref[row, cols - 1 : cols] for row in range(rows)], axis=0)
@@ -76,22 +89,22 @@
     cols_ref[1] = jnp.where(even, first, last)
 
 
-def start_kernel(flags_ref, pattern_ref, rows_ref, field_ref, out_ref, row_ref, cols_ref):
+def start_kernel(pattern_ref, rows_ref, field_ref, out_ref, row_ref, cols_ref):
     cells = rows_ref.shape[0]
-    rim_cells(flags_ref, field_ref, row_ref, cols_ref)
+    rim_cells(field_ref, row_ref, cols_ref)
     out_ref[...] = dot(by_cell(pattern_ref[...], cells), rows_ref[...], TN).astype(bf16)
 
 
-def fill_pad(pad, flags_ref, field_ref, before_ref, after_ref, even_ref, odd_ref):
+def fill_pad(pad, field_ref, before_ref, after_ref, even_ref, odd_ref):
     rows, cols, _ = field_ref.shape
     before, after = before_ref[...].astype(f32), after_ref[...].astype(f32)
-    pad[0, EDGE : EDGE + cols] = jnp.where(flags_ref[0] != 0, before, jnp.zeros_like(before))
-    pad[rows + 1, EDGE : EDGE + cols] = jnp.where(flags_ref[1] != 0, after, jnp.zeros_like(after))
+    pad[0, EDGE : EDGE + cols] = jnp.where(place()[0] != 0, before, jnp.zeros_like(before))
+    pad[rows + 1, EDGE : EDGE + cols] = jnp.where(place()[1] != 0, after, jnp.zeros_like(after))
     for row in range(rows):
         pad[row + 1, EDGE : EDGE + cols] = field_ref[row].astype(f32)
     even, odd = even_ref[...].astype(f32), odd_ref[...].astype(f32)
-    left = jnp.where(flags_ref[2] == 0, odd, even)
-    right = jnp.where(flags_ref[2] == 0, even, odd)
+    left = jnp.where(place()[2] == 0, odd, even)
+    right = jnp.where(place()[2] == 0, even, odd)
     for row in range(rows + 2):
         pad[row, EDGE - 1 : EDGE] = left[row : row + 1]
         pad[row, EDGE + cols : EDGE + cols + 1] = right[row : row + 1]
@@ -115,11 +128,11 @@
 
 
 def enter_kernel(
-    flags_ref, pattern_ref, field_ref, before_ref, after_ref, even_ref, odd_ref, taps_ref, gain_ref,
+    pattern_ref, field_ref, before_ref, after_ref, even_ref, odd_ref, taps_ref, gain_ref,
     h_ref, out_ref, pad, normed,
 ):
     rows, cols, _ = field_ref.shape
-    fill_pad(pad, flags_ref, field_ref, before_ref, after_ref, even_ref, odd_ref)
+    fill_pad(pad, field_ref, before_ref, after_ref, even_ref, odd_ref)
     taps, gain = taps_ref[...], gain_ref[...]
     for row in range(rows):
         h = taps_row(pad, taps, row, cols, False).astype(bf16)
@@ -153,35 +166,24 @@
 
 def attention_kernel(
     slots, blocks, unroll,
-    arrived_hbm, qkv_weight_t_hbm, bias_hbm, grad_att_hbm, qkv_weight_hbm,
-    grad_ref, att_ref,
-    arrived, qkv_weight_t, bias, grad_att, qkv_weight, qkv, grad_qkv, sems,
+    arrived_hbm, qkv_weight_hbm, bias_hbm, grad_att_hbm,
+    grad_hbm, att_hbm,
+    rows_buffer, qkv_weight, bias, grad_att, att_ref, qkv, grad_qkv, sems,
 ):
-    cells, width = arrived.shape
+    cells, width = rows_buffer.shape
+    copies = fetch(
+        sems,
+        (arrived_hbm, rows_buffer), (qkv_weight_hbm, qkv_weight), (bias_hbm, bias), (grad_att_hbm, grad_att),
+    )
+    gather = position_by_row(cells, slots, blocks, 1)
+    copies[0].wait()
+    grouped = dot(gather, rows_buffer[...]).astype(bf16)
+    copies[1].wait()
     step = width // 2
-    parts = [pl.ds(at, step) for at in range(0, 3 * width, step)]
-    fetches = [
-        pltpu.make_async_copy(source, target, sems.at[i])
-        for i, (source, target) in enumerate(
-            [
-                (arrived_hbm, arrived),
-                *((qkv_weight_t_hbm.at[part], qkv_weight_t.at[part]) for part in parts),
-                (bias_hbm, bias),
-                (grad_att_hbm, grad_att),
-                (qkv_weight_hbm, qkv_weight),
-            ]
-        )
-    ]
-    for fetch in fetches:
-        fetch.start()
-    gather = position_by_row(cells, slots, blocks, 1)
-    fetches[0].wait()
-    grouped = dot(gather, arrived[...]).astype(bf16)
-    for part, fetch in zip(parts, fetches[1:]):
-        fetch.wait()
-        qkv[part] = dot(qkv_weight_t[part], grouped, NT).astype(bf16)
-    fetches[-3].wait()
-    fetches[-2].wait()
+    for at in range(0, 3 * width, step):
+        qkv[at : at + step] = dot(qkv_weight[:, at : at + step], grouped, TT).astype(bf16)
+    copies[2].wait()
+    copies[3].wait()
     scale = HEAD_DIM ** (-0.5)
 
     def heads(step, carry):
@@ -227,38 +229,44 @@
             grad_qkv[rows(2, e), at] = to_value[i].astype(bf16)
         return carry
 
-    lax.fori_loop(0, HEADS // unroll, heads, 0)
-    fetches[-1].wait()
+    if unroll == HEADS:
+        heads(0, 0)
+    else:
+        lax.fori_loop(0, HEADS // unroll, heads, 0)
+    last = pltpu.make_async_copy(att_ref, att_hbm, sems.at[1])
+    last.start()
     grad = dot(qkv_weight[...], grad_qkv[...]).astype(bf16)
-    grad_ref[...] = dot(position_by_row(cells, slots, blocks, 0), grad, NT).astype(bf16)
-
-
-def mix(slots, blocks, out_weight_t_ref, att_ref, mixed_ref):
-    mixed = dot(out_weight_t_ref[...], att_ref[...]).astype(bf16)
+    rows_buffer[...] = dot(position_by_row(cells, slots, blocks, 0), grad, NT).astype(bf16)
+    for copy in [last, *fetch(sems, (rows_buffer, grad_hbm))]:
+        copy.wait()
+
+
+def mix(slots, blocks, out_weight_ref, att_ref, mixed_ref):
+    mixed = dot(out_weight_ref[...], att_ref[...], TN).astype(bf16)
     scatter = position_by_row(att_ref.shape[1], slots, blocks, 0)
     mixed_ref[...] = dot(scatter, mixed, NT).astype(bf16)
 
 
-def products_kernel(slots, blocks, cot_ref, att_ref, out_weight_t_ref, mixed_ref, out_ref):
+def products_kernel(slots, blocks, cot_ref, att_ref, out_weight_ref, mixed_ref, out_ref):
     out_ref[...] = dot(cot_ref[...], att_ref[...], NT).astype(bf16)
-    mix(slots, blocks, out_weight_t_ref, att_ref, mixed_ref)
+    mix(slots, blocks, out_weight_ref, att_ref, mixed_ref)
 
 
 def halves_kernel(
-    slots, blocks, flags_ref, cot_ref, att_ref, out_weight_t_ref, mixed_ref, kept_ref, sent_ref, part
+    slots, blocks, cot_ref, att_ref, out_weight_ref, mixed_ref, kept_ref, sent_ref, part
 ):
     lats, chips, cols, rows = kept_ref.shape
-    core = flags_ref[2]
+    core = place()[2]
     for a in range(lats):
         part[...] = dot(cot_ref[...], att_ref[a * rows : (a + 1) * rows], NT).astype(bf16)
         for chip in range(chips):
             kept_ref[a, chip] = part[pl.ds(pl.multiple_of((2 * chip + core) * cols, 16), cols)]
             sent_ref[a, chip] = part[pl.ds(pl.multiple_of((2 * chip + 1 - core) * cols, 16), cols)]
-    mix(slots, blocks, out_weight_t_ref, att_ref, mixed_ref)
-
-
-def join_halves_kernel(flags_ref, kept_ref, met_ref, out_ref, sent_ref):
-    lat = jnp.minimum(flags_ref[0], 1)
+    mix(slots, blocks, out_weight_ref, att_ref, mixed_ref)
+
+
+def join_halves_kernel(kept_ref, met_ref, out_ref, sent_ref):
+    lat = jnp.minimum(place()[0], 1)
     out_ref[...] = (kept_ref[lat].astype(f32) + met_ref[lat].astype(f32)).astype(bf16)
     sent_ref[...] = (kept_ref[1 - lat].astype(f32) + met_ref[1 - lat].astype(f32)).astype(bf16)
 
@@ -269,12 +277,12 @@
 
 
 def return_kernel(
-    flags_ref, pattern_ref, arrived_ref, h_ref, cot_ref, gain_ref,
+    pattern_ref, arrived_ref, h_ref, cot_ref, gain_ref,
     field_ref, before_ref, after_ref, even_ref, odd_ref,
     grad_ref, sums_ref, message_ref, columns_ref, pad, normed_grad,
 ):
     rows, cols, width = field_ref.shape
-    fill_pad(pad, flags_ref, field_ref, before_ref, after_ref, even_ref, odd_ref)
+    fill_pad(pad, field_ref, before_ref, after_ref, even_ref, odd_ref)
     normed_grad[...] = dot(by_cell(pattern_ref[...], rows * cols), arrived_ref[...])
     gain = gain_ref[...]
 
@@ -300,18 +308,26 @@
     for i in range(10):
         sums_ref[i : i + 1] = jnp.sum(sums[i], axis=0, keepdims=True)
     sums_ref[10:16] = jnp.zeros((6, width), f32)
-    rim_cells(flags_ref, grad_ref, message_ref.at[:cols], columns_ref)
+    rim_cells(grad_ref, message_ref.at[:cols], columns_ref)
     total = sums_ref[...]
     high = total.astype(bf16)
     message_ref[cols : cols + 16] = high
     message_ref[cols + 16 :] = (total - high.astype(f32)).astype(bf16)
 
 
+def finish_kernel(scale, sums_ref, kept_ref, met_ref, taps_ref, gain_ref, project_ref):
+    sums = sums_ref[...] * scale
+    for a in range(3):
+        taps_ref[a] = sums[3 * a : 3 * a + 3]
+    gain_ref[...] = sums[9]
+    project_ref[...] = (kept_ref[...].astype(f32) + met_ref[...].astype(f32)).T * scale
+
+
 def spread_kernel(
-    flags_ref, field_ref, before_ref, after_ref, even_ref, odd_ref, taps_ref, out_ref, pad
+    field_ref, before_ref, after_ref, even_ref, odd_ref, taps_ref, out_ref, pad
 ):
     rows, cols, _ = field_ref.shape
-    fill_pad(pad, flags_ref, field_ref, before_ref, after_ref, even_ref, odd_ref)
+    fill_pad(pad, field_ref, before_ref, after_ref, even_ref, odd_ref)
     taps = taps_ref[...]
     for row in range(rows):
         out_ref[row] = taps_row(pad, taps, row, cols, True).astype(bf16)
@@ -365,7 +381,7 @@
     return lax.all_to_all(sent, AXES, split_axis=0, concat_axis=0, tiled=True).reshape(cells, width)
 
 
-def attended_products(slots, blocks, flags, cot_cols, att, out_weight_t):
+def attended_products(slots, blocks, flags, cot_cols, att, out_weight):
     width, cells = att.shape
     lat_count, lon_count = lax.axis_size("lat"), lax.axis_size("lon")
     rows, cols = width // lat_count, width // lon_count
@@ -374,7 +390,7 @@
         mixed, parts = call(
             lambda *refs: products_kernel(slots, blocks, *refs),
             "attended_products", [mixed_shape, shape((width, width), bf16)],
-            [cot_cols, att, out_weight_t],
+            [cot_cols, att, out_weight],
         )
         parts = parts.reshape(lon_count, cols, lat_count, rows).transpose(2, 0, 1, 3)
         parts = parts.reshape(lat_count * lon_count, cols, rows)
@@ -385,12 +401,12 @@
     mixed, kept, sent = call(
         lambda *refs: halves_kernel(slots, blocks, *refs),
         "attended_products", [mixed_shape, halves, halves],
-        [flags, cot_cols, att, out_weight_t],
-        [pltpu.VMEM((width, rows), bf16)], specs={0: SMEM},
+        [cot_cols, att, out_weight],
+        [pltpu.VMEM((width, rows), bf16)],
     )
     met = lax.ppermute(sent, "lon", swap_pairs(lon_count, 1))
     kept, sent = call(
-        join_halves_kernel, "project_join", [quarters, quarters], [flags, kept, met], specs={0: SMEM}
+        join_halves_kernel, "project_join", [quarters, quarters], [kept, met]
     )
     met = lax.ppermute(sent, "lat", swap_pairs(2, 1))
     parts = (kept.astype(f32) + met.astype(f32)).astype(bf16)
@@ -437,8 +453,6 @@
     pattern_row = pattern.reshape(1, cells)
     gain = layer_norm_gain.reshape(1, width)
     cot_rows = cotangent.reshape(cells, width)
-    qkv_weight_t = qkv_weight.T
-    out_weight_t = out_weight.T
     bias = jnp.swapaxes(score_bias, 1, 2)
     bias = jnp.concatenate([bias, bias], axis=2)
     pad = pltpu.VMEM((rows + 2, cols + 2 * EDGE, width), f32)
@@ -446,44 +460,49 @@
     cols_shape = shape((width, cells), bf16)
     tall_shape = shape((3 * width, cells), bf16)
 
-    lat, lon = lax.axis_index("lat"), lax.axis_index("lon")
-    flags = jnp.stack([lat, lat_count - 1 - lat, lax.rem(lon, 2)]).astype(jnp.int32)
+    flags = (
+        lax.axis_index("lat"), lat_count - 1 - lax.axis_index("lat"), lax.rem(lax.axis_index("lon"), 2)
+    )
     row_shape, columns_shape = shape((cols, width), bf16), shape((2, rows, width), bf16)
 
     cot_packed, row, columns = call(
         start_kernel, "start", [rows_shape, row_shape, columns_shape],
-        [flags, pattern_row, cot_rows, fields], specs={0: SMEM}, mib=BIG,
+        [pattern_row, cot_rows, fields], mib=BIG,
     )
     met = lax.ppermute(row, "lat", swap_pairs(2, 1)) if lat_count == 2 else None
     cot_arrived = exchange(cot_packed)
     grad_att, cot_cols = call(
         lambda *refs: cot_kernel(slots, blocks, *refs),
-        "cotangent_products", [cols_shape, cols_shape], [cot_arrived, out_weight],
+        "cotangent_products", [cols_shape, cols_shape], [cot_arrived, out_weight], mib=BIG,
     )
 
     beside = lat_rims(fields, met)
     beside = (*beside, *lon_rims(flags, beside, columns))
     h, packed = call(
         enter_kernel, "convolve_normalize_pack", [rows_shape, rows_shape],
-        [flags, pattern_row, fields, *beside, conv_kernel, gain],
-        [pad, pltpu.VMEM((cells, width), bf16)], specs={0: SMEM}, mib=BIG,
+        [pattern_row, fields, *beside, conv_kernel, gain],
+        [pad, pltpu.VMEM((cells, width), bf16)], mib=BIG,
     )
     arrived = exchange(packed)
-    weight_shape = (width, 3 * width)
-    grad_grouped, att = call(
+    grad_grouped, att = pl.pallas_call(
         lambda *refs: attention_kernel(slots, blocks, UNROLL, *refs),
-        "attention", [rows_shape, cols_shape],
-        [arrived, qkv_weight_t, bias, grad_att, qkv_weight],
-        [
-            pltpu.VMEM((cells, width), bf16), pltpu.VMEM(weight_shape[::-1], bf16),
+        name="attention",
+        out_shape=[rows_shape, cols_shape],
+        in_specs=[ANY] * 4,
+        out_specs=[ANY] * 2,
+        scratch_shapes=[
+            pltpu.VMEM((cells, width), bf16), pltpu.VMEM(qkv_weight.shape, bf16),
             pltpu.VMEM(bias.shape, f32), pltpu.VMEM((width, cells), bf16),
-            pltpu.VMEM(weight_shape, bf16), pltpu.VMEM((3 * width, cells), bf16),
-            pltpu.VMEM((3 * width, cells), bf16), pltpu.SemaphoreType.DMA((10,)),
+            pltpu.VMEM((width, cells), bf16), pltpu.VMEM((3 * width, cells), bf16),
+            pltpu.VMEM((3 * width, cells), bf16), pltpu.SemaphoreType.DMA((4,)),
         ],
-        flops=12_000_000_000, specs=dict.fromkeys(range(5), ANY), mib=BIG,
-    )
+        compiler_params=pltpu.CompilerParams(vmem_limit_bytes=BIG * 1024 * 1024),
+        cost_estimate=pl.CostEstimate(
+            flops=12_000_000_000, bytes_accessed=8_000_000, transcendentals=0
+        ),
+    )(arrived, qkv_weight, bias, grad_att)
     grad_home = exchange(grad_grouped)
-    mixed, project = attended_products(slots, blocks, flags, cot_cols, att, out_weight_t)
+    mixed, project = attended_products(slots, blocks, flags, cot_cols, att, out_weight)
     grad_home, mixed = lax.optimization_barrier((grad_home, mixed))
     mixed_home = exchange(mixed)
 
@@ -493,8 +512,8 @@
             shape(fields.shape, bf16), shape((16, width), f32),
             shape((cols + 32, width), bf16), columns_shape,
         ],
-        [flags, pattern_row, grad_home, h, cot_rows, gain, fields, *beside],
-        [pad, pltpu.VMEM((cells, width), f32)], specs={0: SMEM},
+        [pattern_row, grad_home, h, cot_rows, gain, fields, *beside],
+        [pad, pltpu.VMEM((cells, width), f32)],
     )
     if lat_count == 2:
         met = lax.ppermute(message, "lat", swap_pairs(2, 1))
@@ -511,11 +530,12 @@
         sums = sums + lax.ppermute(sums, "lon", swap_pairs(lon_count, 2))
         sums, odd = lax.optimization_barrier((sums, odd))
         beside = (*beside[:2], even, odd)
-        project = (project[0].astype(f32) + project[1].astype(f32)).astype(bf16)
+        kept, met = project
         bit = 4
         while bit < lon_count:
             if 2 * bit == lon_count:
                 sums, mixed_home = lax.optimization_barrier((sums, mixed_home))
+            project = (kept.astype(f32) + met.astype(f32)).astype(bf16)
             kept, sent = halved(project, bit)
             high_low = two_terms(sums).reshape(-1, sent.shape[-1])
             sent = sent.reshape(-1, sent.shape[-1])
@@ -523,27 +543,29 @@
                 jnp.concatenate([high_low, sent], axis=0), "lon", swap_pairs(lon_count, bit)
             )
             sums = sums + one_term(met[: high_low.shape[0]].reshape(2 * sums.shape[0], width))
-            project = kept.astype(f32) + met[high_low.shape[0] :].reshape(kept.shape).astype(f32)
+            met = met[high_low.shape[0] :].reshape(kept.shape)
             bit *= 2
-            if bit < lon_count:
-                project = project.astype(bf16)
-        grad_project = project[0].T * scale_everywhere
+        kept, met = kept[0], met[0]
     else:
         beside = (*beside, *lon_rims(flags, beside, columns))
         sums = total_over("lon", sums)
-        grad_project = project.T * scale_everywhere
-    sums = sums * scale_everywhere
+        kept, met = project, jnp.zeros_like(project)
     grad_fields = call(
         spread_kernel, "convolve_back", [shape(fields.shape, bf16)],
-        [flags, grad_h, *beside, conv_kernel], [pad], specs={0: SMEM},
+        [grad_h, *beside, conv_kernel], [pad],
     )[0]
     block_out = call(leave_kernel, "block_out", [rows_shape], [pattern_row, mixed_home, h])[0]
+    grad_kernel, gain_gradient, grad_project = call(
+        lambda *refs: finish_kernel(scale_everywhere, *refs), "finish",
+        [shape((3, 3, width), f32), shape((width,), f32), shape(kept.shape[::-1], f32)],
+        [sums, kept, met],
+    )
     return (
         block_out.reshape(rows, cols, width),
         grad_fields,
         grad_project,
-        sums[:9].reshape(3, 3, width),
-        sums[9],
+        grad_kernel,
+        gain_gradient,
     )
 
 

time: 110 us -> 99.8 us (0.907)
  local copies, waits for them, and re-layouts: 19.8 us -> 7.47 us
  starting transfers between devices: 30.4 us -> 35.1 us
  other arithmetic: 2.89 us -> 1.58 us
    unnamed x47 -> x40, local copies, waits for them, and re-layouts: 16.3 us -> 5.15 us
    pallas_call x9, Pallas kernels: 25.5 us -> 16.1 us  [call(): pl.pallas_call(kernel, name=name, grid=(1,), out_shape=list(out_shape), i...]
    pallas_call x0 -> x1, Pallas kernels: none -> 8.99 us  [body(): pl.pallas_call(lambda *refs: attention_kernel(slots, blocks, UNROLL, *ref...]
    all_to_all x4, waiting for transfers between devices: 6.5 us -> 12.9 us  [exchange(): lax.all_to_all(sent, AXES, split_axis=0, concat_axis=0, tiled=True)]
    ppermute x2, starting transfers between devices: 0.81 us -> 5.05 us  [body(): lax.ppermute(jnp.concatenate([high_low, sent], axis=0), 'lon', swap_pairs...]
    ppermute x2, waiting for transfers between devices: 6.64 us -> 2.97 us  [body(): lax.ppermute(jnp.concatenate([high_low, sent], axis=0), 'lon', swap_pairs...]
    ppermute x1, waiting for transfers between devices: 2.5 us -> 0.05 us  [attended_products(): return (mixed, (kept, lax.ppermute(sent, 'lon', swap_pairs(lon_count, 2))))]
    ppermute x2, waiting for transfers between devices: 6.29 us -> 7.46 us  [lon_rims(): met_odd = lax.ppermute(column(1, jnp.logical_not(even)), 'lon', odd_pairs)]
  transfers between devices with their start and end apart: 16 -> 16, of which waited for: 11 -> 8; matrix products, arithmetic and copies ran while one was open for 10% -> 4% of each run, Pallas kernels for 12% -> 13%
where the time goes in v4:
time: 99.8 us; the launch traced here: 99.1 us
  starting transfers between devices  35.1 us (35%)
  waiting for transfers between devices  28.8 us (29%)
  Pallas kernels  25.1 us (25%)
  local copies, waits for them, and re-layouts  7.47 us (7%)
  other arithmetic  1.58 us (2%)
  between operations  1.08 us (1%)
    pallas_call x9, Pallas kernels, call(): pl.pallas_call(kernel, name=name, grid=(1,), out_shape=list(out_shape), i...  16.1 us
    all_to_all x4, starting transfers between devices, exchange(): lax.all_to_all(sent, AXES, split_axis=0, concat_axis=0, tiled=True)  13.6 us
    all_to_all x4, waiting for transfers between devices, exchange(): lax.all_to_all(sent, AXES, split_axis=0, concat_axis=0, tiled=True)  12.9 us
    pallas_call x1, Pallas kernels, body(): pl.pallas_call(lambda *refs: attention_kernel(slots, blocks, UNROLL, *ref...  8.99 us
    ppermute x2, starting transfers between devices, lon_rims(): met_odd = lax.ppermute(column(1, jnp.logical_not(even)), 'lon', odd_pairs)  8.28 us
    ppermute x2, waiting for transfers between devices, lon_rims(): met_odd = lax.ppermute(column(1, jnp.logical_not(even)), 'lon', odd_pairs)  7.46 us
    unnamed x40, local copies, waits for them, and re-layouts  5.15 us
    ppermute x2, starting transfers between devices, body(): lax.ppermute(jnp.concatenate([high_low, sent], axis=0), 'lon', swap_pairs...  5.05 us
  transfers between devices with their start and end apart: 16, of which 8 were waited for; matrix products, arithmetic and copies ran while one was open for 4% of the time, Pallas kernels for 13%

profile of v4, /device:TPU:0, one launch (start us, length us, event | category | flops | bytes accessed | tf_op | source)
XLA Modules:
  0.0 99.1 jit_solution(14132919076719353439)
XLA Ops:
  0.6 0.0 copy-start.17
  0.6 2.3 %start.1 = (bf16[256,768]{1,0:T(8,128)(2,1)}, bf16[32,768]{1,0:T(8,128)(2,1)}, bf16[2,8,768]{2,1,0:T(8,128)(2,1)}) custom-call(s32[1,256]{1,0:T(1,128)} %bitcast.44, bf16[256,768]{1,0:T(8,128)(2,1)} %bitcast.39, bf16[8,32,768]{2,1,0:T(8,128)(2,1)} %field_ref.5), custom_call_target="tpu_custom_call" | custom-call | bytes 1254400 | tf_op jit(solution)/shard_map/start/pallas_call | solution.py:41
  2.9 2.9 %collective-permute-start = (bf16[32,768]{1,0:T(8,128)(2,1)}, bf16[32,768]{1,0:T(8,128)(2,1)S(1)}, u32[]{:S(2)}, u32[]{:S(2)}) collective-permute-start(bf16[32,768]{1,0:T(8,128)(2,1)} %get-tuple-element.32), channel_id=1, source_target_pairs={{0,16},{16,0},{1,17},{17,1},{2,18},{18,2},{3,19},{19,3},{4,20},{20... | collective-permute-start | bytes 147464 | tf_op jit(solution)/shard_map/ppermute | solution.py:472
  5.8 4.9 %all-to-all-start.1 = ((bf16[32,8,768]{2,1,0:T(8,128)(2,1)}), bf16[32,8,768]{2,1,0:T(8,128)(2,1)S(1)}, u32[]{:S(2)}, u32[]{:S(2)}) async-start(bf16[32,8,768]{2,1,0:T(8,128)(2,1)} %bitcast.54), calls=%async_computation.1 | async-start | bytes 786432 | tf_op jit(solution)/shard_map/all_to_all | solution.py:381
  10.8 0.7 slice_bitcast_fusion.2
  11.5 0.0 collective-permute-done.before_ref.after_ref
  11.6 0.3 collective-permute-start.1
  11.9 4.5 %collective-permute-start.2 = (bf16[10,768]{1,0:T(8,128)(2,1)S(1)}, bf16[10,768]{1,0:T(8,128)(2,1)S(1)}, u32[]{:S(2)}, u32[]{:S(2)}) collective-permute-start(bf16[10,768]{1,0:T(8,128)(2,1)S(1)} %pad_maximum_fusion.6), channel_id=1, source_target_pairs={{0,15},{1,2},{2,1},{3,4},{4,3},{5,6},{6,5},{7,8},{8,7},{9,10},{10,... | collective-permute-start | bytes 46088 | tf_op jit(solution)/shard_map/ppermute | solution.py:370
  16.4 1.3 %reshape.93.gain_ref = f32[1,768]{1,0:T(1,128)} reshape(f32[768]{0:T(1024)} %param.10) | data formatting | bytes 6144 | tf_op jit(solution)/shard_map/reshape | solution.py:454
  17.7 0.0 collective-permute-done.1.even_ref
  17.7 5.1 %collective-permute-done.2.odd_ref = bf16[10,768]{1,0:T(8,128)(2,1)S(1)} collective-permute-done((bf16[10,768]{1,0:T(8,128)(2,1)S(1)}, bf16[10,768]{1,0:T(8,128)(2,1)S(1)}, u32[]{:S(2)}, u32[]{:S(2)}) %collective-permute-start.2) | collective-permute-done | bytes 15392 | tf_op jit(solution)/shard_map/ppermute | solution.py:370
  22.8 0.0 copy-done.4
  22.8 0.0 copy-done.10
  22.8 0.6 copy-done.12
  23.4 3.3 %convolve_normalize_pack.1 = (bf16[256,768]{1,0:T(8,128)(2,1)}, bf16[256,768]{1,0:T(8,128)(2,1)}) custom-call(s32[1,256]{1,0:T(1,128)} %bitcast.45, bf16[8,32,768]{2,1,0:T(8,128)(2,1)} %field_ref.5, bf16[32,768]{1,0:T(8,128)(2,1)} %copy-done.4, bf16[32,768]{1,0:T(8,128)(2,1)} %copy-done.4, bf16[10,768]{1,0:T(8,128)(2,1)} %copy-done.10, ...), custom_call_target="tpu_custom_call" | custom-call | bytes 1340416 | tf_op jit(solution)/shard_map/convolve_normalize_pack/pallas_call | solution.py:41
  26.7 0.0 all-to-all-done.1
  26.7 3.2 %all-to-all-start = ((bf16[32,8,768]{2,1,0:T(8,128)(2,1)}), bf16[32,8,768]{2,1,0:T(8,128)(2,1)S(1)}, u32[]{:S(2)}, u32[]{:S(2)}) async-start(bf16[32,8,768]{2,1,0:T(8,128)(2,1)} %bitcast.56), calls=%async_computation | async-start | bytes 786432 | tf_op jit(solution)/shard_map/all_to_all | solution.py:381
  29.9 0.3 copy.15
  30.2 1.2 %pad_maximum_fusion.refs_2_ = f32[24,64,128]{2,1,0:T(8,128)} fusion(f32[24,64,64]{2,1,0:T(8,128)S(1)} %bitcast.48), kind=kLoop, calls=%fused_computation | loop fusion | flops 196608 | bytes 1179648 | tf_op jit(solution)/shard_map/concatenate | solution.py:457
  31.3 0.0 copy-done.16
  31.3 2.9 %cotangent_products.1 = (bf16[768,256]{1,0:T(8,128)(2,1)}, bf16[768,256]{1,0:T(8,128)(2,1)}) custom-call(bf16[256,768]{1,0:T(8,128)(2,1)} %bitcast.49, bf16[768,768]{1,0:T(8,128)(2,1)} %refs_2_.1), custom_call_target="tpu_custom_call" | custom-call | bytes 2359296 | tf_op jit(solution)/shard_map/cotangent_products/pallas_call | solution.py:41
  34.3 8.7 %all-to-all-done = bf16[32,8,768]{2,1,0:T(8,128)(2,1)S(1)} async-done(((bf16[32,8,768]{2,1,0:T(8,128)(2,1)}), bf16[32,8,768]{2,1,0:T(8,128)(2,1)S(1)}, u32[]{:S(2)}, u32[]{:S(2)}) %all-to-all-start) | async-done | bytes 393248 | tf_op jit(solution)/shard_map/all_to_all | solution.py:381
  43.0 0.7 copy-done.18
  43.7 0.0 copy-start.15
  43.8 9.0 %attention.1 = (bf16[256,768]{1,0:T(8,128)(2,1)}, bf16[768,256]{1,0:T(8,128)(2,1)}) custom-call(bf16[256,768]{1,0:T(8,128)(2,1)} %bitcast.57, bf16[768,2304]{1,0:T(8,128)(2,1)} %refs_1_.3, f32[24,64,128]{2,1,0:T(8,128)} %pad_maximum_fusion.refs_2_, bf16[768,256]{1,0:T(8,128)(2,1)} %get-tuple-element.36.refs_3_), custom_call_target="tpu_custom_call" | custom-call | flops 12000000000 | bytes 8000000 | tf_op jit(solution)/shard_map/attention/pallas_call | solution.py:487
  52.7 0.0 copy-start.1
  52.8 0.0 copy-start.2
  52.8 0.0 copy-start.5
  52.8 2.9 %all-to-all-start.2 = ((bf16[32,8,768]{2,1,0:T(8,128)(2,1)}), bf16[32,8,768]{2,1,0:T(8,128)(2,1)S(1)}, u32[]{:S(2)}, u32[]{:S(2)}) async-start(bf16[32,8,768]{2,1,0:T(8,128)(2,1)} %bitcast.55), calls=%async_computation.2 | async-start | bytes 786432 | tf_op jit(solution)/shard_map/all_to_all | solution.py:381
  55.7 1.0 copy-done.7
  56.7 1.0 %copy-done.8 = bf16[768,256]{1,0:T(8,128)(2,1)S(1)} copy-done((bf16[768,256]{1,0:T(8,128)(2,1)S(1)}, bf16[768,256]{1,0:T(8,128)(2,1)}, u32[]{:S(2)}) %copy-start.8) | copy-done | bytes 393240
  57.7 2.1 %attended_products.1 = (bf16[256,768]{1,0:T(8,128)(2,1)S(1)}, bf16[2,8,48,384]{3,2,1,0:T(8,128)(2,1)S(1)}, bf16[2,8,48,384]{3,2,1,0:T(8,128)(2,1)}) custom-call(bf16[768,256]{1,0:T(8,128)(2,1)S(1)} %copy-done.7, bf16[768,256]{1,0:T(8,128)(2,1)S(1)} %copy-done.8, bf16[768,768]{1,0:T(8,128)(2,1)S(1)} %copy-done), custom_call_target="tpu_custom_call" | custom-call | bytes 3538944 | tf_op jit(solution)/shard_map/attended_products/pallas_call | solution.py:41
  59.8 0.7 copy-done.6
  60.6 0.0 collective-permute-start.7
  60.6 2.2 %collective-permute-done.7.met_ref = bf16[2,8,48,384]{3,2,1,0:T(8,128)(2,1)S(1)} collective-permute-done((bf16[2,8,48,384]{3,2,1,0:T(8,128)(2,1)}, bf16[2,8,48,384]{3,2,1,0:T(8,128)(2,1)S(1)}, u32[]{:S(2)}, u32[]{:S(2)}) %collective-permute-start.7) | collective-permute-done | bytes 589856 | tf_op jit(solution)/shard_map/ppermute | solution.py:407
  62.8 0.1 project_join.1
  62.9 1.5 %collective-permute-start.8 = (bf16[8,48,384]{2,1,0:T(8,128)(2,1)S(1)}, bf16[8,48,384]{2,1,0:T(8,128)(2,1)S(1)}, u32[]{:S(2)}, u32[]{:S(2)}) collective-permute-start(bf16[8,48,384]{2,1,0:T(8,128)(2,1)S(1)} %get-tuple-element.50), channel_id=1, source_target_pairs={{0,16},{16,0},{1,17},{17,1},{2,18},{18,2},{3,19},{19,3},{4,20},{20... | collective-permute-start | bytes 884744 | tf_op jit(solution)/shard_map/ppermute | solution.py:411
  64.5 4.2 %all-to-all-done.2 = bf16[32,8,768]{2,1,0:T(8,128)(2,1)S(1)} async-done(((bf16[32,8,768]{2,1,0:T(8,128)(2,1)}), bf16[32,8,768]{2,1,0:T(8,128)(2,1)S(1)}, u32[]{:S(2)}, u32[]{:S(2)}) %all-to-all-start.2) | async-done | bytes 393248 | tf_op jit(solution)/shard_map/all_to_all | solution.py:381
  68.7 0.0 copy-done.13
  68.7 0.0 copy-start.9
  68.7 1.9 %normalize_back.1 = (bf16[8,32,768]{2,1,0:T(8,128)(2,1)S(1)}, f32[16,768]{1,0:T(8,128)S(1)}, bf16[64,768]{1,0:T(8,128)(2,1)S(1)}, bf16[2,8,768]{2,1,0:T(8,128)(2,1)S(1)}) custom-call(s32[1,256]{1,0:T(1,128)S(1)} %bitcast.46, bf16[256,768]{1,0:T(8,128)(2,1)S(1)} %bitcast.42, bf16[256,768]{1,0:T(8,128)(2,1)S(1)} %copy-done.3, bf16[256,768]{1,0:T(8,128)(2,1)S(1)} %bitcast.40, ...), custom_call_target="tpu_custom_call" | custom-call | bytes 2271232 | tf_op jit(solution)/shard_map/normalize_back/pallas_call | solution.py:41
  70.6 1.1 %collective-permute-start.3 = (bf16[64,768]{1,0:T(8,128)(2,1)S(1)}, bf16[64,768]{1,0:T(8,128)(2,1)S(1)}, u32[]{:S(2)}, u32[]{:S(2)}) collective-permute-start(bf16[64,768]{1,0:T(8,128)(2,1)S(1)} %get-tuple-element.44), channel_id=1, source_target_pairs={{0,16},{16,0},{1,17},{17,1},{2,18},{18,2},{3,19},{19,3},{4,20},{20... | collective-permute-start | bytes 294920 | tf_op jit(solution)/shard_map/ppermute | solution.py:519
  71.7 2.6 %all-to-all-start.3 = ((bf16[32,8,768]{2,1,0:T(8,128)(2,1)}), bf16[32,8,768]{2,1,0:T(8,128)(2,1)S(1)}, u32[]{:S(2)}, u32[]{:S(2)}) async-start(bf16[32,8,768]{2,1,0:T(8,128)(2,1)} %bitcast.43), calls=%async_computation.3 | async-start | bytes 786432 | tf_op jit(solution)/shard_map/all_to_all | solution.py:381
  74.4 0.9 collective-permute-done.3
  75.4 0.2 concatenate.30
  75.5 0.1 collective-permute-start.4
  75.7 3.8 %collective-permute-start.6 = (bf16[10,768]{1,0:T(8,128)(2,1)S(1)}, bf16[10,768]{1,0:T(8,128)(2,1)S(1)}, u32[]{:S(2)}, u32[]{:S(2)}) collective-permute-start(bf16[10,768]{1,0:T(8,128)(2,1)S(1)} %pad_maximum_fusion.7), channel_id=1, source_target_pairs={{0,15},{1,2},{2,1},{3,4},{4,3},{5,6},{6,5},{7,8},{8,7},{9,10},{10,... | collective-permute-start | bytes 46088 | tf_op jit(solution)/shard_map/ppermute | solution.py:370
  79.5 0.0 collective-permute-done.8
  79.5 0.1 add_convert_fusion
  79.5 0.0 collective-permute-done.4
  79.6 0.1 collective-permute-start.5
  79.7 2.1 %collective-permute-start.9 = (bf16[4,48,384]{2,1,0:T(8,128)(2,1)S(1)}, bf16[4,48,384]{2,1,0:T(8,128)(2,1)S(1)}, u32[]{:S(2)}, u32[]{:S(2)}) collective-permute-start(bf16[4,48,384]{2,1,0:T(8,128)(2,1)S(1)} %dynamic-slice_bitcast_fusion), channel_id=1, source_target_pairs={{0,2},{1,3},{2,0},{3,1},{4,6},{5,7},{6,4},{7,5},{8,10},{9,11},{10,... | collective-permute-start | bytes 442376 | tf_op jit(solution)/shard_map/ppermute | solution.py:414
  81.8 2.3 %collective-permute-done.5 = f32[16,768]{1,0:T(8,128)S(1)} collective-permute-done((f32[16,768]{1,0:T(8,128)S(1)}, f32[16,768]{1,0:T(8,128)S(1)}, u32[]{:S(2)}, u32[]{:S(2)}) %collective-permute-start.5) | collective-permute-done | bytes 49184 | tf_op jit(solution)/shard_map/ppermute | solution.py:530
  84.1 2.4 %collective-permute-done.6.odd_ref = bf16[10,768]{1,0:T(8,128)(2,1)S(1)} collective-permute-done((bf16[10,768]{1,0:T(8,128)(2,1)S(1)}, bf16[10,768]{1,0:T(8,128)(2,1)S(1)}, u32[]{:S(2)}, u32[]{:S(2)}) %collective-permute-start.6) | collective-permute-done | bytes 15392 | tf_op jit(solution)/shard_map/ppermute | solution.py:370
  86.5 0.0 collective-permute-done.9
  86.6 2.1 %collective-permute-start.10 = (bf16[160,384]{1,0:T(8,128)(2,1)S(1)}, bf16[160,384]{1,0:T(8,128)(2,1)S(1)}, u32[]{:S(2)}, u32[]{:S(2)}) collective-permute-start(bf16[160,384]{1,0:T(8,128)(2,1)S(1)} %pad_maximum_fusion.1), channel_id=1, source_target_pairs={{0,4},{1,5},{2,6},{3,7},{4,0},{5,1},{6,2},{7,3},{8,12},{9,13},{10,... | collective-permute-start | bytes 368648 | tf_op jit(solution)/shard_map/ppermute | solution.py:542
  88.7 3.0 %collective-permute-done.10 = bf16[160,384]{1,0:T(8,128)(2,1)S(1)} collective-permute-done((bf16[160,384]{1,0:T(8,128)(2,1)S(1)}, bf16[160,384]{1,0:T(8,128)(2,1)S(1)}, u32[]{:S(2)}, u32[]{:S(2)}) %collective-permute-start.10) | collective-permute-done | bytes 122912 | tf_op jit(solution)/shard_map/ppermute | solution.py:542
  91.8 0.0 all-to-all-done.3
  91.8 3.0 %collective-permute-start.11 = (bf16[112,384]{1,0:T(8,128)(2,1)S(1)}, bf16[112,384]{1,0:T(8,128)(2,1)S(1)}, u32[]{:S(2)}, u32[]{:S(2)}) collective-permute-start(bf16[112,384]{1,0:T(8,128)(2,1)S(1)} %pad_maximum_fusion.2), channel_id=1, source_target_pairs={{0,8},{1,9},{2,10},{3,11},{4,12},{5,13},{6,14},{7,15},{8,0},{9,1},... | collective-permute-start | bytes 258056 | tf_op jit(solution)/shard_map/ppermute | solution.py:542
  94.9 1.7 %convolve_back.1 = bf16[8,32,768]{2,1,0:T(8,128)(2,1)} custom-call(bf16[8,32,768]{2,1,0:T(8,128)(2,1)S(1)} %get-tuple-element.53.field_ref, bf16[32,768]{1,0:T(8,128)(2,1)S(1)} %slice.120.before_ref.after_ref, bf16[32,768]{1,0:T(8,128)(2,1)S(1)} %slice.120.before_ref.after_ref, bf16[10,768]{1,0:T(8,128)(2,1)S(1)} %slice.121.even_ref, ...), custom_call_target="tpu_custom_call" | custom-call | bytes 943104 | tf_op jit(solution)/shard_map/convolve_back/pallas_call | solution.py:41
  96.6 1.0 %block_out.1 = bf16[256,768]{1,0:T(8,128)(2,1)} custom-call(s32[1,256]{1,0:T(1,128)S(1)} %bitcast.47, bf16[256,768]{1,0:T(8,128)(2,1)S(1)} %bitcast.41, bf16[256,768]{1,0:T(8,128)(2,1)S(1)} %copy-done.3), custom_call_target="tpu_custom_call" | custom-call | bytes 1180672 | tf_op jit(solution)/shard_map/block_out/pallas_call | solution.py:41
  97.6 0.0 collective-permute-done.11
  97.7 0.7 finish.1
  98.3 0.7 copy.17
  (59 shorter events, 0.5 us)
Async XLA Ops:
  0.6 29.3 %copy-start.17 = (f32[24,64,64]{2,1,0:T(8,128)S(1)}, f32[24,64,64]{2,1,0:T(8,128)}, u32[]{:S(2)}) copy-start(f32[24,64,64]{2,1,0:T(8,128)} %param.13) | copy-start | bytes 1179652
  2.9 8.6 %collective-permute-start = (bf16[32,768]{1,0:T(8,128)(2,1)}, bf16[32,768]{1,0:T(8,128)(2,1)S(1)}, u32[]{:S(2)}, u32[]{:S(2)}) collective-permute-start(bf16[32,768]{1,0:T(8,128)(2,1)} %get-tuple-element.32), channel_id=1, source_target_pairs={{0,16},{16,0},{1,17},{17,1},{2,18},{18,2},{3,19},{19,3},{4,20},{20... | collective-permute-start | bytes 147464 | tf_op jit(solution)/shard_map/ppermute | solution.py:472
  5.8 20.9 %all-to-all-start.1 = ((bf16[32,8,768]{2,1,0:T(8,128)(2,1)}), bf16[32,8,768]{2,1,0:T(8,128)(2,1)S(1)}, u32[]{:S(2)}, u32[]{:S(2)}) async-start(bf16[32,8,768]{2,1,0:T(8,128)(2,1)} %bitcast.54), calls=%async_computation.1 | async-start | bytes 786432 | tf_op jit(solution)/shard_map/all_to_all | solution.py:381
  11.5 11.3 %copy-start.4 = (bf16[32,768]{1,0:T(8,128)(2,1)}, bf16[32,768]{1,0:T(8,128)(2,1)S(1)}, u32[]{:S(2)}) copy-start(bf16[32,768]{1,0:T(8,128)(2,1)S(1)} %collective-permute-done.before_ref.after_ref) | copy-start | bytes 147460
  11.6 6.1 %collective-permute-start.1 = (bf16[10,768]{1,0:T(8,128)(2,1)S(1)}, bf16[10,768]{1,0:T(8,128)(2,1)S(1)}, u32[]{:S(2)}, u32[]{:S(2)}) collective-permute-start(bf16[10,768]{1,0:T(8,128)(2,1)S(1)} %pad_maximum_fusion.5), channel_id=1, source_target_pairs={{0,1},{1,0},{2,3},{3,2},{4,5},{5,4},{6,7},{7,6},{8,9},{9,8},{10,11... | collective-permute-start | bytes 46088 | tf_op jit(solution)/shard_map/ppermute | solution.py:368
  11.9 10.9 %collective-permute-start.2 = (bf16[10,768]{1,0:T(8,128)(2,1)S(1)}, bf16[10,768]{1,0:T(8,128)(2,1)S(1)}, u32[]{:S(2)}, u32[]{:S(2)}) collective-permute-start(bf16[10,768]{1,0:T(8,128)(2,1)S(1)} %pad_maximum_fusion.6), channel_id=1, source_target_pairs={{0,15},{1,2},{2,1},{3,4},{4,3},{5,6},{6,5},{7,8},{8,7},{9,10},{10,... | collective-permute-start | bytes 46088 | tf_op jit(solution)/shard_map/ppermute | solution.py:370
  17.7 5.1 %copy-start.10 = (bf16[10,768]{1,0:T(8,128)(2,1)}, bf16[10,768]{1,0:T(8,128)(2,1)S(1)}, u32[]{:S(2)}) copy-start(bf16[10,768]{1,0:T(8,128)(2,1)S(1)} %collective-permute-done.1.even_ref) | copy-start | bytes 46084
  22.8 0.6 copy-start.12
  26.7 4.6 %copy-start.16 = (bf16[32,8,768]{2,1,0:T(8,128)(2,1)}, bf16[32,8,768]{2,1,0:T(8,128)(2,1)S(1)}, u32[]{:S(2)}) copy-start(bf16[32,8,768]{2,1,0:T(8,128)(2,1)S(1)} %all-to-all-done.1) | copy-start | bytes 1179652
  26.7 16.3 %all-to-all-start = ((bf16[32,8,768]{2,1,0:T(8,128)(2,1)}), bf16[32,8,768]{2,1,0:T(8,128)(2,1)S(1)}, u32[]{:S(2)}, u32[]{:S(2)}) async-start(bf16[32,8,768]{2,1,0:T(8,128)(2,1)} %bitcast.56), calls=%async_computation | async-start | bytes 786432 | tf_op jit(solution)/shard_map/all_to_all | solution.py:381
  43.0 0.7 copy-start.18
  43.7 12.0 %copy-start = (bf16[768,768]{1,0:T(8,128)(2,1)S(1)}, bf16[768,768]{1,0:T(8,128)(2,1)}, u32[]{:S(2)}) copy-start(bf16[768,768]{1,0:T(8,128)(2,1)} %refs_2_.1) | copy-start | bytes 3538948
  43.7 24.9 %copy-start.11 = (bf16[10,768]{1,0:T(8,128)(2,1)S(1)}, bf16[10,768]{1,0:T(8,128)(2,1)}, u32[]{:S(2)}) copy-start(bf16[10,768]{1,0:T(8,128)(2,1)} %copy-done.10) | copy-start | bytes 46084
  43.7 24.9 %copy-start.13 = (bf16[10,768]{1,0:T(8,128)(2,1)S(1)}, bf16[10,768]{1,0:T(8,128)(2,1)}, u32[]{:S(2)}) copy-start(bf16[10,768]{1,0:T(8,128)(2,1)} %copy-done.12) | copy-start | bytes 46084
  43.7 24.9 %copy-start.14 = (f32[1,768]{1,0:T(1,128)S(1)}, f32[1,768]{1,0:T(1,128)}, u32[]{:S(2)}) copy-start(f32[1,768]{1,0:T(1,128)} %reshape.93.gain_ref) | copy-start | bytes 9220
  43.7 24.9 %copy-start.15 = (s32[1,1,256]{2,1,0:T(1,128)S(1)}, s32[1,1,256]{2,1,0:T(1,128)}, u32[]{:S(2)}) copy-start(s32[1,1,256]{2,1,0:T(1,128)} %param.14) | copy-start | bytes 3076
  52.7 15.9 %copy-start.1 = (bf16[8,32,768]{2,1,0:T(8,128)(2,1)S(1)}, bf16[8,32,768]{2,1,0:T(8,128)(2,1)}, u32[]{:S(2)}) copy-start(bf16[8,32,768]{2,1,0:T(8,128)(2,1)} %field_ref.5) | copy-start | bytes 1179652
  52.8 15.9 %copy-start.2 = (bf16[8,32,768]{2,1,0:T(8,128)(2,1)S(1)}, bf16[8,32,768]{2,1,0:T(8,128)(2,1)}, u32[]{:S(2)}) copy-start(bf16[8,32,768]{2,1,0:T(8,128)(2,1)} %param.15) | copy-start | bytes 1179652
  52.8 15.9 %copy-start.3 = (bf16[256,768]{1,0:T(8,128)(2,1)S(1)}, bf16[256,768]{1,0:T(8,128)(2,1)}, u32[]{:S(2)}) copy-start(bf16[256,768]{1,0:T(8,128)(2,1)} %get-tuple-element.42.h_ref) | copy-start | bytes 1179652
  52.8 15.9 %copy-start.5 = (bf16[32,768]{1,0:T(8,128)(2,1)S(1)}, bf16[32,768]{1,0:T(8,128)(2,1)}, u32[]{:S(2)}) copy-start(bf16[32,768]{1,0:T(8,128)(2,1)} %copy-done.4) | copy-start | bytes 147460
  52.8 15.9 %all-to-all-start.2 = ((bf16[32,8,768]{2,1,0:T(8,128)(2,1)}), bf16[32,8,768]{2,1,0:T(8,128)(2,1)S(1)}, u32[]{:S(2)}, u32[]{:S(2)}) async-start(bf16[32,8,768]{2,1,0:T(8,128)(2,1)} %bitcast.55), calls=%async_computation.2 | async-start | bytes 786432 | tf_op jit(solution)/shard_map/all_to_all | solution.py:381
  55.7 1.0 %copy-start.7 = (bf16[768,256]{1,0:T(8,128)(2,1)S(1)}, bf16[768,256]{1,0:T(8,128)(2,1)}, u32[]{:S(2)}) copy-start(bf16[768,256]{1,0:T(8,128)(2,1)} %get-tuple-element.38.refs_0_) | copy-start | bytes 1179652
  56.7 1.0 %copy-start.8 = (bf16[768,256]{1,0:T(8,128)(2,1)S(1)}, bf16[768,256]{1,0:T(8,128)(2,1)}, u32[]{:S(2)}) copy-start(bf16[768,256]{1,0:T(8,128)(2,1)} %get-tuple-element.39.refs_1_) | copy-start | bytes 1179652
  59.8 0.7 copy-start.6
  60.6 2.2 %collective-permute-start.7 = (bf16[2,8,48,384]{3,2,1,0:T(8,128)(2,1)}, bf16[2,8,48,384]{3,2,1,0:T(8,128)(2,1)S(1)}, u32[]{:S(2)}, u32[]{:S(2)}) collective-permute-start(bf16[2,8,48,384]{3,2,1,0:T(8,128)(2,1)} %get-tuple-element.48), channel_id=1, source_target_pairs={{0,1},{1,0},{2,3},{3,2},{4,5},{5,4},{6,7},{7,6},{8,9},{9,8},{10,11... | collective-permute-start | bytes 1769480 | tf_op jit(solution)/shard_map/ppermute | solution.py:407
  62.9 16.5 %collective-permute-start.8 = (bf16[8,48,384]{2,1,0:T(8,128)(2,1)S(1)}, bf16[8,48,384]{2,1,0:T(8,128)(2,1)S(1)}, u32[]{:S(2)}, u32[]{:S(2)}) collective-permute-start(bf16[8,48,384]{2,1,0:T(8,128)(2,1)S(1)} %get-tuple-element.50), channel_id=1, source_target_pairs={{0,16},{16,0},{1,17},{17,1},{2,18},{18,2},{3,19},{19,3},{4,20},{20... | collective-permute-start | bytes 884744 | tf_op jit(solution)/shard_map/ppermute | solution.py:411
  68.7 26.1 %copy-start.9 = (f32[3,3,768]{2,1,0:T(4,128)S(1)}, f32[3,3,768]{2,1,0:T(4,128)}, u32[]{:S(2)}) copy-start(f32[3,3,768]{2,1,0:T(4,128)} %taps_ref.3) | copy-start | bytes 82948
  70.6 4.7 %collective-permute-start.3 = (bf16[64,768]{1,0:T(8,128)(2,1)S(1)}, bf16[64,768]{1,0:T(8,128)(2,1)S(1)}, u32[]{:S(2)}, u32[]{:S(2)}) collective-permute-start(bf16[64,768]{1,0:T(8,128)(2,1)S(1)} %get-tuple-element.44), channel_id=1, source_target_pairs={{0,16},{16,0},{1,17},{17,1},{2,18},{18,2},{3,19},{19,3},{4,20},{20... | collective-permute-start | bytes 294920 | tf_op jit(solution)/shard_map/ppermute | solution.py:519
  71.7 20.0 %all-to-all-start.3 = ((bf16[32,8,768]{2,1,0:T(8,128)(2,1)}), bf16[32,8,768]{2,1,0:T(8,128)(2,1)S(1)}, u32[]{:S(2)}, u32[]{:S(2)}) async-start(bf16[32,8,768]{2,1,0:T(8,128)(2,1)} %bitcast.43), calls=%async_computation.3 | async-start | bytes 786432 | tf_op jit(solution)/shard_map/all_to_all | solution.py:381
  75.5 4.0 %collective-permute-start.4 = (bf16[42,768]{1,0:T(8,128)(2,1)S(1)}, bf16[42,768]{1,0:T(8,128)(2,1)S(1)}, u32[]{:S(2)}, u32[]{:S(2)}) collective-permute-start(bf16[42,768]{1,0:T(8,128)(2,1)S(1)} %concatenate.30), channel_id=1, source_target_pairs={{0,1},{1,0},{2,3},{3,2},{4,5},{5,4},{6,7},{7,6},{8,9},{9,8},{10,11... | collective-permute-start | bytes 193544 | tf_op jit(solution)/shard_map/ppermute | solution.py:368
  75.7 10.8 %collective-permute-start.6 = (bf16[10,768]{1,0:T(8,128)(2,1)S(1)}, bf16[10,768]{1,0:T(8,128)(2,1)S(1)}, u32[]{:S(2)}, u32[]{:S(2)}) collective-permute-start(bf16[10,768]{1,0:T(8,128)(2,1)S(1)} %pad_maximum_fusion.7), channel_id=1, source_target_pairs={{0,15},{1,2},{2,1},{3,4},{4,3},{5,6},{6,5},{7,8},{8,7},{9,10},{10,... | collective-permute-start | bytes 46088 | tf_op jit(solution)/shard_map/ppermute | solution.py:370
  79.6 4.5 %collective-permute-start.5 = (f32[16,768]{1,0:T(8,128)S(1)}, f32[16,768]{1,0:T(8,128)S(1)}, u32[]{:S(2)}, u32[]{:S(2)}) collective-permute-start(f32[16,768]{1,0:T(8,128)S(1)} %add_add_fusion), channel_id=1, source_target_pairs={{0,2},{1,3},{2,0},{3,1},{4,6},{5,7},{6,4},{7,5},{8,10},{9,11},{10,... | collective-permute-start | bytes 147464 | tf_op jit(solution)/shard_map/ppermute | solution.py:530
  79.7 6.8 %collective-permute-start.9 = (bf16[4,48,384]{2,1,0:T(8,128)(2,1)S(1)}, bf16[4,48,384]{2,1,0:T(8,128)(2,1)S(1)}, u32[]{:S(2)}, u32[]{:S(2)}) collective-permute-start(bf16[4,48,384]{2,1,0:T(8,128)(2,1)S(1)} %dynamic-slice_bitcast_fusion), channel_id=1, source_target_pairs={{0,2},{1,3},{2,0},{3,1},{4,6},{5,7},{6,4},{7,5},{8,10},{9,11},{10,... | collective-permute-start | bytes 442376 | tf_op jit(solution)/shard_map/ppermute | solution.py:414
  86.6 5.0 %collective-permute-start.10 = (bf16[160,384]{1,0:T(8,128)(2,1)S(1)}, bf16[160,384]{1,0:T(8,128)(2,1)S(1)}, u32[]{:S(2)}, u32[]{:S(2)}) collective-permute-start(bf16[160,384]{1,0:T(8,128)(2,1)S(1)} %pad_maximum_fusion.1), channel_id=1, source_target_pairs={{0,4},{1,5},{2,6},{3,7},{4,0},{5,1},{6,2},{7,3},{8,12},{9,13},{10,... | collective-permute-start | bytes 368648 | tf_op jit(solution)/shard_map/ppermute | solution.py:542
  91.8 5.8 %collective-permute-start.11 = (bf16[112,384]{1,0:T(8,128)(2,1)S(1)}, bf16[112,384]{1,0:T(8,128)(2,1)S(1)}, u32[]{:S(2)}, u32[]{:S(2)}) collective-permute-start(bf16[112,384]{1,0:T(8,128)(2,1)S(1)} %pad_maximum_fusion.2), channel_id=1, source_target_pairs={{0,8},{1,9},{2,10},{3,11},{4,12},{5,13},{6,14},{7,15},{8,0},{9,1},... | collective-permute-start | bytes 258056 | tf_op jit(solution)/shard_map/ppermute | solution.py:542

commit v5 on v4

--- a/solution.py
+++ b/solution.py
@@ -320,7 +320,7 @@
     for a in range(3):
         taps_ref[a] = sums[3 * a : 3 * a + 3]
     gain_ref[...] = sums[9]
-    project_ref[...] = (kept_ref[...].astype(f32) + met_ref[...].astype(f32)).T * scale
+    project_ref[...] = (kept_ref[...].astype(f32) + met_ref[...].astype(f32)) * scale
 
 
 def spread_kernel(
@@ -557,13 +557,13 @@
     block_out = call(leave_kernel, "block_out", [rows_shape], [pattern_row, mixed_home, h])[0]
     grad_kernel, gain_gradient, grad_project = call(
         lambda *refs: finish_kernel(scale_everywhere, *refs), "finish",
-        [shape((3, 3, width), f32), shape((width,), f32), shape(kept.shape[::-1], f32)],
+        [shape((3, 3, width), f32), shape((width,), f32), shape(kept.shape, f32)],
         [sums, kept, met],
     )
     return (
         block_out.reshape(rows, cols, width),
         grad_fields,
-        grad_project,
+        grad_project.T,
         grad_kernel,
         gain_gradient,
     )

time: 99.8 us -> 99 us (level)
    unnamed x40 -> x39, local copies, waits for them, and re-layouts: 5.15 us -> 4.41 us
where the time goes in v5:
time: 99 us; the launch traced here: 98.3 us
  starting transfers between devices  35.1 us (35%)
  waiting for transfers between devices  28.8 us (29%)
  Pallas kernels  25 us (25%)
  local copies, waits for them, and re-layouts  6.72 us (7%)
  other arithmetic  1.58 us (2%)
  between operations  1.08 us (1%)
    pallas_call x9, Pallas kernels, call(): pl.pallas_call(kernel, name=name, grid=(1,), out_shape=list(out_shape), i...  16.1 us
    all_to_all x4, starting transfers between devices, exchange(): lax.all_to_all(sent, AXES, split_axis=0, concat_axis=0, tiled=True)  13.6 us
    all_to_all x4, waiting for transfers between devices, exchange(): lax.all_to_all(sent, AXES, split_axis=0, concat_axis=0, tiled=True)  12.9 us
    pallas_call x1, Pallas kernels, body(): pl.pallas_call(lambda *refs: attention_kernel(slots, blocks, UNROLL, *ref...  8.99 us
    ppermute x2, starting transfers between devices, lon_rims(): met_odd = lax.ppermute(column(1, jnp.logical_not(even)), 'lon', odd_pairs)  8.28 us
    ppermute x2, waiting for transfers between devices, lon_rims(): met_odd = lax.ppermute(column(1, jnp.logical_not(even)), 'lon', odd_pairs)  7.46 us
    ppermute x2, starting transfers between devices, body(): lax.ppermute(jnp.concatenate([high_low, sent], axis=0), 'lon', swap_pairs...  5.05 us
    unnamed x39, local copies, waits for them, and re-layouts  4.41 us
  transfers between devices with their start and end apart: 16, of which 8 were waited for; matrix products, arithmetic and copies ran while one was open for 4% of the time, Pallas kernels for 13%

profile of v5, /device:TPU:0, one launch (start us, length us, event | category | flops | bytes accessed | tf_op | source)
XLA Modules:
  0.0 98.3 jit_solution(13234331695456331505)
XLA Ops:
  0.6 0.0 copy-start.17
  0.6 2.3 %start.1 = (bf16[256,768]{1,0:T(8,128)(2,1)}, bf16[32,768]{1,0:T(8,128)(2,1)}, bf16[2,8,768]{2,1,0:T(8,128)(2,1)}) custom-call(s32[1,256]{1,0:T(1,128)} %bitcast.45, bf16[256,768]{1,0:T(8,128)(2,1)} %bitcast.40, bf16[8,32,768]{2,1,0:T(8,128)(2,1)} %field_ref.5), custom_call_target="tpu_custom_call" | custom-call | bytes 1254400 | tf_op jit(solution)/shard_map/start/pallas_call | solution.py:41
  2.9 2.9 %collective-permute-start = (bf16[32,768]{1,0:T(8,128)(2,1)}, bf16[32,768]{1,0:T(8,128)(2,1)S(1)}, u32[]{:S(2)}, u32[]{:S(2)}) collective-permute-start(bf16[32,768]{1,0:T(8,128)(2,1)} %get-tuple-element.32), channel_id=1, source_target_pairs={{0,16},{16,0},{1,17},{17,1},{2,18},{18,2},{3,19},{19,3},{4,20},{20... | collective-permute-start | bytes 147464 | tf_op jit(solution)/shard_map/ppermute | solution.py:472
  5.8 4.9 %all-to-all-start.1 = ((bf16[32,8,768]{2,1,0:T(8,128)(2,1)}), bf16[32,8,768]{2,1,0:T(8,128)(2,1)S(1)}, u32[]{:S(2)}, u32[]{:S(2)}) async-start(bf16[32,8,768]{2,1,0:T(8,128)(2,1)} %bitcast.55), calls=%async_computation.1 | async-start | bytes 786432 | tf_op jit(solution)/shard_map/all_to_all | solution.py:381
  10.8 0.7 slice_bitcast_fusion.2
  11.5 0.0 collective-permute-done.before_ref.after_ref
  11.6 0.3 collective-permute-start.1
  11.9 4.5 %collective-permute-start.2 = (bf16[10,768]{1,0:T(8,128)(2,1)S(1)}, bf16[10,768]{1,0:T(8,128)(2,1)S(1)}, u32[]{:S(2)}, u32[]{:S(2)}) collective-permute-start(bf16[10,768]{1,0:T(8,128)(2,1)S(1)} %pad_maximum_fusion.6), channel_id=1, source_target_pairs={{0,15},{1,2},{2,1},{3,4},{4,3},{5,6},{6,5},{7,8},{8,7},{9,10},{10,... | collective-permute-start | bytes 46088 | tf_op jit(solution)/shard_map/ppermute | solution.py:370
  16.4 1.3 %reshape.93.gain_ref = f32[1,768]{1,0:T(1,128)} reshape(f32[768]{0:T(1024)} %param.10) | data formatting | bytes 6144 | tf_op jit(solution)/shard_map/reshape | solution.py:454
  17.7 0.0 collective-permute-done.1.even_ref
  17.7 5.1 %collective-permute-done.2.odd_ref = bf16[10,768]{1,0:T(8,128)(2,1)S(1)} collective-permute-done((bf16[10,768]{1,0:T(8,128)(2,1)S(1)}, bf16[10,768]{1,0:T(8,128)(2,1)S(1)}, u32[]{:S(2)}, u32[]{:S(2)}) %collective-permute-start.2) | collective-permute-done | bytes 15392 | tf_op jit(solution)/shard_map/ppermute | solution.py:370
  22.8 0.0 copy-done.4
  22.8 0.0 copy-done.10
  22.8 0.6 copy-done.12
  23.4 3.3 %convolve_normalize_pack.1 = (bf16[256,768]{1,0:T(8,128)(2,1)}, bf16[256,768]{1,0:T(8,128)(2,1)}) custom-call(s32[1,256]{1,0:T(1,128)} %bitcast.46, bf16[8,32,768]{2,1,0:T(8,128)(2,1)} %field_ref.5, bf16[32,768]{1,0:T(8,128)(2,1)} %copy-done.4, bf16[32,768]{1,0:T(8,128)(2,1)} %copy-done.4, bf16[10,768]{1,0:T(8,128)(2,1)} %copy-done.10, ...), custom_call_target="tpu_custom_call" | custom-call | bytes 1340416 | tf_op jit(solution)/shard_map/convolve_normalize_pack/pallas_call | solution.py:41
  26.7 0.0 all-to-all-done.1
  26.7 3.2 %all-to-all-start = ((bf16[32,8,768]{2,1,0:T(8,128)(2,1)}), bf16[32,8,768]{2,1,0:T(8,128)(2,1)S(1)}, u32[]{:S(2)}, u32[]{:S(2)}) async-start(bf16[32,8,768]{2,1,0:T(8,128)(2,1)} %bitcast.57), calls=%async_computation | async-start | bytes 786432 | tf_op jit(solution)/shard_map/all_to_all | solution.py:381
  29.9 0.0 copy-done.17
  29.9 0.3 copy.14
  30.2 1.2 %pad_maximum_fusion.refs_2_ = f32[24,64,128]{2,1,0:T(8,128)} fusion(f32[24,64,64]{2,1,0:T(8,128)S(1)} %bitcast.49), kind=kLoop, calls=%fused_computation | loop fusion | flops 196608 | bytes 1179648 | tf_op jit(solution)/shard_map/concatenate | solution.py:457
  31.3 0.0 copy-done.16
  31.3 2.9 %cotangent_products.1 = (bf16[768,256]{1,0:T(8,128)(2,1)}, bf16[768,256]{1,0:T(8,128)(2,1)}) custom-call(bf16[256,768]{1,0:T(8,128)(2,1)} %bitcast.50, bf16[768,768]{1,0:T(8,128)(2,1)} %refs_2_.1), custom_call_target="tpu_custom_call" | custom-call | bytes 2359296 | tf_op jit(solution)/shard_map/cotangent_products/pallas_call | solution.py:41
  34.3 8.7 %all-to-all-done = bf16[32,8,768]{2,1,0:T(8,128)(2,1)S(1)} async-done(((bf16[32,8,768]{2,1,0:T(8,128)(2,1)}), bf16[32,8,768]{2,1,0:T(8,128)(2,1)S(1)}, u32[]{:S(2)}, u32[]{:S(2)}) %all-to-all-start) | async-done | bytes 393248 | tf_op jit(solution)/shard_map/all_to_all | solution.py:381
  43.0 0.7 copy-done.18
  43.7 0.0 copy-start.15
  43.8 9.0 %attention.1 = (bf16[256,768]{1,0:T(8,128)(2,1)}, bf16[768,256]{1,0:T(8,128)(2,1)}) custom-call(bf16[256,768]{1,0:T(8,128)(2,1)} %bitcast.58, bf16[768,2304]{1,0:T(8,128)(2,1)} %refs_1_.3, f32[24,64,128]{2,1,0:T(8,128)} %pad_maximum_fusion.refs_2_, bf16[768,256]{1,0:T(8,128)(2,1)} %get-tuple-element.36.refs_3_), custom_call_target="tpu_custom_call" | custom-call | flops 12000000000 | bytes 8000000 | tf_op jit(solution)/shard_map/attention/pallas_call | solution.py:487
  52.7 0.0 copy-start.1
  52.8 0.0 copy-start.2
  52.8 0.0 copy-start.5
  52.8 2.9 %all-to-all-start.2 = ((bf16[32,8,768]{2,1,0:T(8,128)(2,1)}), bf16[32,8,768]{2,1,0:T(8,128)(2,1)S(1)}, u32[]{:S(2)}, u32[]{:S(2)}) async-start(bf16[32,8,768]{2,1,0:T(8,128)(2,1)} %bitcast.56), calls=%async_computation.2 | async-start | bytes 786432 | tf_op jit(solution)/shard_map/all_to_all | solution.py:381
  55.7 1.0 %copy-done.7 = bf16[768,256]{1,0:T(8,128)(2,1)S(1)} copy-done((bf16[768,256]{1,0:T(8,128)(2,1)S(1)}, bf16[768,256]{1,0:T(8,128)(2,1)}, u32[]{:S(2)}) %copy-start.7) | copy-done | bytes 393240
  56.7 1.0 %copy-done.8 = bf16[768,256]{1,0:T(8,128)(2,1)S(1)} copy-done((bf16[768,256]{1,0:T(8,128)(2,1)S(1)}, bf16[768,256]{1,0:T(8,128)(2,1)}, u32[]{:S(2)}) %copy-start.8) | copy-done | bytes 393240
  57.7 2.1 %attended_products.1 = (bf16[256,768]{1,0:T(8,128)(2,1)S(1)}, bf16[2,8,48,384]{3,2,1,0:T(8,128)(2,1)S(1)}, bf16[2,8,48,384]{3,2,1,0:T(8,128)(2,1)}) custom-call(bf16[768,256]{1,0:T(8,128)(2,1)S(1)} %copy-done.7, bf16[768,256]{1,0:T(8,128)(2,1)S(1)} %copy-done.8, bf16[768,768]{1,0:T(8,128)(2,1)S(1)} %copy-done), custom_call_target="tpu_custom_call" | custom-call | bytes 3538944 | tf_op jit(solution)/shard_map/attended_products/pallas_call | solution.py:41
  59.8 0.7 copy-done.6
  60.6 0.0 collective-permute-start.7
  60.6 2.2 %collective-permute-done.7.met_ref = bf16[2,8,48,384]{3,2,1,0:T(8,128)(2,1)S(1)} collective-permute-done((bf16[2,8,48,384]{3,2,1,0:T(8,128)(2,1)}, bf16[2,8,48,384]{3,2,1,0:T(8,128)(2,1)S(1)}, u32[]{:S(2)}, u32[]{:S(2)}) %collective-permute-start.7) | collective-permute-done | bytes 589856 | tf_op jit(solution)/shard_map/ppermute | solution.py:407
  62.8 0.1 project_join.1
  62.9 1.5 %collective-permute-start.8 = (bf16[8,48,384]{2,1,0:T(8,128)(2,1)S(1)}, bf16[8,48,384]{2,1,0:T(8,128)(2,1)S(1)}, u32[]{:S(2)}, u32[]{:S(2)}) collective-permute-start(bf16[8,48,384]{2,1,0:T(8,128)(2,1)S(1)} %get-tuple-element.50), channel_id=1, source_target_pairs={{0,16},{16,0},{1,17},{17,1},{2,18},{18,2},{3,19},{19,3},{4,20},{20... | collective-permute-start | bytes 884744 | tf_op jit(solution)/shard_map/ppermute | solution.py:411
  64.5 4.2 %all-to-all-done.2 = bf16[32,8,768]{2,1,0:T(8,128)(2,1)S(1)} async-done(((bf16[32,8,768]{2,1,0:T(8,128)(2,1)}), bf16[32,8,768]{2,1,0:T(8,128)(2,1)S(1)}, u32[]{:S(2)}, u32[]{:S(2)}) %all-to-all-start.2) | async-done | bytes 393248 | tf_op jit(solution)/shard_map/all_to_all | solution.py:381
  68.7 0.0 copy-done.13
  68.7 0.0 copy-start.9
  68.7 1.9 %normalize_back.1 = (bf16[8,32,768]{2,1,0:T(8,128)(2,1)S(1)}, f32[16,768]{1,0:T(8,128)S(1)}, bf16[64,768]{1,0:T(8,128)(2,1)S(1)}, bf16[2,8,768]{2,1,0:T(8,128)(2,1)S(1)}) custom-call(s32[1,256]{1,0:T(1,128)S(1)} %bitcast.47, bf16[256,768]{1,0:T(8,128)(2,1)S(1)} %bitcast.43, bf16[256,768]{1,0:T(8,128)(2,1)S(1)} %copy-done.3, bf16[256,768]{1,0:T(8,128)(2,1)S(1)} %bitcast.41, ...), custom_call_target="tpu_custom_call" | custom-call | bytes 2271232 | tf_op jit(solution)/shard_map/normalize_back/pallas_call | solution.py:41
  70.6 1.1 %collective-permute-start.3 = (bf16[64,768]{1,0:T(8,128)(2,1)S(1)}, bf16[64,768]{1,0:T(8,128)(2,1)S(1)}, u32[]{:S(2)}, u32[]{:S(2)}) collective-permute-start(bf16[64,768]{1,0:T(8,128)(2,1)S(1)} %get-tuple-element.44), channel_id=1, source_target_pairs={{0,16},{16,0},{1,17},{17,1},{2,18},{18,2},{3,19},{19,3},{4,20},{20... | collective-permute-start | bytes 294920 | tf_op jit(solution)/shard_map/ppermute | solution.py:519
  71.7 2.6 %all-to-all-start.3 = ((bf16[32,8,768]{2,1,0:T(8,128)(2,1)}), bf16[32,8,768]{2,1,0:T(8,128)(2,1)S(1)}, u32[]{:S(2)}, u32[]{:S(2)}) async-start(bf16[32,8,768]{2,1,0:T(8,128)(2,1)} %bitcast.44), calls=%async_computation.3 | async-start | bytes 786432 | tf_op jit(solution)/shard_map/all_to_all | solution.py:381
  74.4 0.9 collective-permute-done.3
  75.4 0.2 concatenate.30
  75.5 0.1 collective-permute-start.4
  75.7 3.8 %collective-permute-start.6 = (bf16[10,768]{1,0:T(8,128)(2,1)S(1)}, bf16[10,768]{1,0:T(8,128)(2,1)S(1)}, u32[]{:S(2)}, u32[]{:S(2)}) collective-permute-start(bf16[10,768]{1,0:T(8,128)(2,1)S(1)} %pad_maximum_fusion.7), channel_id=1, source_target_pairs={{0,15},{1,2},{2,1},{3,4},{4,3},{5,6},{6,5},{7,8},{8,7},{9,10},{10,... | collective-permute-start | bytes 46088 | tf_op jit(solution)/shard_map/ppermute | solution.py:370
  79.5 0.0 collective-permute-done.8
  79.5 0.1 add_convert_fusion
  79.5 0.0 collective-permute-done.4
  79.6 0.1 collective-permute-start.5
  79.7 2.1 %collective-permute-start.9 = (bf16[4,48,384]{2,1,0:T(8,128)(2,1)S(1)}, bf16[4,48,384]{2,1,0:T(8,128)(2,1)S(1)}, u32[]{:S(2)}, u32[]{:S(2)}) collective-permute-start(bf16[4,48,384]{2,1,0:T(8,128)(2,1)S(1)} %dynamic-slice_bitcast_fusion), channel_id=1, source_target_pairs={{0,2},{1,3},{2,0},{3,1},{4,6},{5,7},{6,4},{7,5},{8,10},{9,11},{10,... | collective-permute-start | bytes 442376 | tf_op jit(solution)/shard_map/ppermute | solution.py:414
  81.8 2.3 %collective-permute-done.5 = f32[16,768]{1,0:T(8,128)S(1)} collective-permute-done((f32[16,768]{1,0:T(8,128)S(1)}, f32[16,768]{1,0:T(8,128)S(1)}, u32[]{:S(2)}, u32[]{:S(2)}) %collective-permute-start.5) | collective-permute-done | bytes 49184 | tf_op jit(solution)/shard_map/ppermute | solution.py:530
  84.1 2.4 %collective-permute-done.6.odd_ref = bf16[10,768]{1,0:T(8,128)(2,1)S(1)} collective-permute-done((bf16[10,768]{1,0:T(8,128)(2,1)S(1)}, bf16[10,768]{1,0:T(8,128)(2,1)S(1)}, u32[]{:S(2)}, u32[]{:S(2)}) %collective-permute-start.6) | collective-permute-done | bytes 15392 | tf_op jit(solution)/shard_map/ppermute | solution.py:370
  86.5 0.0 collective-permute-done.9
  86.6 2.1 %collective-permute-start.10 = (bf16[160,384]{1,0:T(8,128)(2,1)S(1)}, bf16[160,384]{1,0:T(8,128)(2,1)S(1)}, u32[]{:S(2)}, u32[]{:S(2)}) collective-permute-start(bf16[160,384]{1,0:T(8,128)(2,1)S(1)} %pad_maximum_fusion.1), channel_id=1, source_target_pairs={{0,4},{1,5},{2,6},{3,7},{4,0},{5,1},{6,2},{7,3},{8,12},{9,13},{10,... | collective-permute-start | bytes 368648 | tf_op jit(solution)/shard_map/ppermute | solution.py:542
  88.7 3.0 %collective-permute-done.10 = bf16[160,384]{1,0:T(8,128)(2,1)S(1)} collective-permute-done((bf16[160,384]{1,0:T(8,128)(2,1)S(1)}, bf16[160,384]{1,0:T(8,128)(2,1)S(1)}, u32[]{:S(2)}, u32[]{:S(2)}) %collective-permute-start.10) | collective-permute-done | bytes 122912 | tf_op jit(solution)/shard_map/ppermute | solution.py:542
  91.8 0.0 all-to-all-done.3
  91.8 3.0 %collective-permute-start.11 = (bf16[112,384]{1,0:T(8,128)(2,1)S(1)}, bf16[112,384]{1,0:T(8,128)(2,1)S(1)}, u32[]{:S(2)}, u32[]{:S(2)}) collective-permute-start(bf16[112,384]{1,0:T(8,128)(2,1)S(1)} %pad_maximum_fusion.2), channel_id=1, source_target_pairs={{0,8},{1,9},{2,10},{3,11},{4,12},{5,13},{6,14},{7,15},{8,0},{9,1},... | collective-permute-start | bytes 258056 | tf_op jit(solution)/shard_map/ppermute | solution.py:542
  94.9 1.7 %convolve_back.1 = bf16[8,32,768]{2,1,0:T(8,128)(2,1)} custom-call(bf16[8,32,768]{2,1,0:T(8,128)(2,1)S(1)} %get-tuple-element.53.field_ref, bf16[32,768]{1,0:T(8,128)(2,1)S(1)} %slice.120.before_ref.after_ref, bf16[32,768]{1,0:T(8,128)(2,1)S(1)} %slice.120.before_ref.after_ref, bf16[10,768]{1,0:T(8,128)(2,1)S(1)} %slice.121.even_ref, ...), custom_call_target="tpu_custom_call" | custom-call | bytes 943104 | tf_op jit(solution)/shard_map/convolve_back/pallas_call | solution.py:41
  96.6 1.0 %block_out.1 = bf16[256,768]{1,0:T(8,128)(2,1)} custom-call(s32[1,256]{1,0:T(1,128)S(1)} %bitcast.48, bf16[256,768]{1,0:T(8,128)(2,1)S(1)} %bitcast.42, bf16[256,768]{1,0:T(8,128)(2,1)S(1)} %copy-done.3), custom_call_target="tpu_custom_call" | custom-call | bytes 1180672 | tf_op jit(solution)/shard_map/block_out/pallas_call | solution.py:41
  97.6 0.0 collective-permute-done.11
  97.7 0.7 finish.1
  (58 shorter events, 0.5 us)
Async XLA Ops:
  0.6 29.3 %copy-start.17 = (f32[24,64,64]{2,1,0:T(8,128)S(1)}, f32[24,64,64]{2,1,0:T(8,128)}, u32[]{:S(2)}) copy-start(f32[24,64,64]{2,1,0:T(8,128)} %param.13) | copy-start | bytes 1179652
  2.9 8.6 %collective-permute-start = (bf16[32,768]{1,0:T(8,128)(2,1)}, bf16[32,768]{1,0:T(8,128)(2,1)S(1)}, u32[]{:S(2)}, u32[]{:S(2)}) collective-permute-start(bf16[32,768]{1,0:T(8,128)(2,1)} %get-tuple-element.32), channel_id=1, source_target_pairs={{0,16},{16,0},{1,17},{17,1},{2,18},{18,2},{3,19},{19,3},{4,20},{20... | collective-permute-start | bytes 147464 | tf_op jit(solution)/shard_map/ppermute | solution.py:472
  5.8 20.9 %all-to-all-start.1 = ((bf16[32,8,768]{2,1,0:T(8,128)(2,1)}), bf16[32,8,768]{2,1,0:T(8,128)(2,1)S(1)}, u32[]{:S(2)}, u32[]{:S(2)}) async-start(bf16[32,8,768]{2,1,0:T(8,128)(2,1)} %bitcast.55), calls=%async_computation.1 | async-start | bytes 786432 | tf_op jit(solution)/shard_map/all_to_all | solution.py:381
  11.5 11.3 %copy-start.4 = (bf16[32,768]{1,0:T(8,128)(2,1)}, bf16[32,768]{1,0:T(8,128)(2,1)S(1)}, u32[]{:S(2)}) copy-start(bf16[32,768]{1,0:T(8,128)(2,1)S(1)} %collective-permute-done.before_ref.after_ref) | copy-start | bytes 147460
  11.6 6.1 %collective-permute-start.1 = (bf16[10,768]{1,0:T(8,128)(2,1)S(1)}, bf16[10,768]{1,0:T(8,128)(2,1)S(1)}, u32[]{:S(2)}, u32[]{:S(2)}) collective-permute-start(bf16[10,768]{1,0:T(8,128)(2,1)S(1)} %pad_maximum_fusion.5), channel_id=1, source_target_pairs={{0,1},{1,0},{2,3},{3,2},{4,5},{5,4},{6,7},{7,6},{8,9},{9,8},{10,11... | collective-permute-start | bytes 46088 | tf_op jit(solution)/shard_map/ppermute | solution.py:368
  11.9 10.9 %collective-permute-start.2 = (bf16[10,768]{1,0:T(8,128)(2,1)S(1)}, bf16[10,768]{1,0:T(8,128)(2,1)S(1)}, u32[]{:S(2)}, u32[]{:S(2)}) collective-permute-start(bf16[10,768]{1,0:T(8,128)(2,1)S(1)} %pad_maximum_fusion.6), channel_id=1, source_target_pairs={{0,15},{1,2},{2,1},{3,4},{4,3},{5,6},{6,5},{7,8},{8,7},{9,10},{10,... | collective-permute-start | bytes 46088 | tf_op jit(solution)/shard_map/ppermute | solution.py:370
  17.7 5.1 %copy-start.10 = (bf16[10,768]{1,0:T(8,128)(2,1)}, bf16[10,768]{1,0:T(8,128)(2,1)S(1)}, u32[]{:S(2)}) copy-start(bf16[10,768]{1,0:T(8,128)(2,1)S(1)} %collective-permute-done.1.even_ref) | copy-start | bytes 46084
  22.8 0.6 copy-start.12
  26.7 4.6 %copy-start.16 = (bf16[32,8,768]{2,1,0:T(8,128)(2,1)}, bf16[32,8,768]{2,1,0:T(8,128)(2,1)S(1)}, u32[]{:S(2)}) copy-start(bf16[32,8,768]{2,1,0:T(8,128)(2,1)S(1)} %all-to-all-done.1) | copy-start | bytes 1179652
  26.7 16.3 %all-to-all-start = ((bf16[32,8,768]{2,1,0:T(8,128)(2,1)}), bf16[32,8,768]{2,1,0:T(8,128)(2,1)S(1)}, u32[]{:S(2)}, u32[]{:S(2)}) async-start(bf16[32,8,768]{2,1,0:T(8,128)(2,1)} %bitcast.57), calls=%async_computation | async-start | bytes 786432 | tf_op jit(solution)/shard_map/all_to_all | solution.py:381
  43.0 0.7 copy-start.18
  43.7 12.0 %copy-start = (bf16[768,768]{1,0:T(8,128)(2,1)S(1)}, bf16[768,768]{1,0:T(8,128)(2,1)}, u32[]{:S(2)}) copy-start(bf16[768,768]{1,0:T(8,128)(2,1)} %refs_2_.1) | copy-start | bytes 3538948
  43.7 24.9 %copy-start.11 = (bf16[10,768]{1,0:T(8,128)(2,1)S(1)}, bf16[10,768]{1,0:T(8,128)(2,1)}, u32[]{:S(2)}) copy-start(bf16[10,768]{1,0:T(8,128)(2,1)} %copy-done.10) | copy-start | bytes 46084
  43.7 24.9 %copy-start.13 = (bf16[10,768]{1,0:T(8,128)(2,1)S(1)}, bf16[10,768]{1,0:T(8,128)(2,1)}, u32[]{:S(2)}) copy-start(bf16[10,768]{1,0:T(8,128)(2,1)} %copy-done.12) | copy-start | bytes 46084
  43.7 24.9 %copy-start.14 = (f32[1,768]{1,0:T(1,128)S(1)}, f32[1,768]{1,0:T(1,128)}, u32[]{:S(2)}) copy-start(f32[1,768]{1,0:T(1,128)} %reshape.93.gain_ref) | copy-start | bytes 9220
  43.7 24.9 %copy-start.15 = (s32[1,1,256]{2,1,0:T(1,128)S(1)}, s32[1,1,256]{2,1,0:T(1,128)}, u32[]{:S(2)}) copy-start(s32[1,1,256]{2,1,0:T(1,128)} %param.14) | copy-start | bytes 3076
  52.7 15.9 %copy-start.1 = (bf16[8,32,768]{2,1,0:T(8,128)(2,1)S(1)}, bf16[8,32,768]{2,1,0:T(8,128)(2,1)}, u32[]{:S(2)}) copy-start(bf16[8,32,768]{2,1,0:T(8,128)(2,1)} %field_ref.5) | copy-start | bytes 1179652
  52.8 15.9 %copy-start.2 = (bf16[8,32,768]{2,1,0:T(8,128)(2,1)S(1)}, bf16[8,32,768]{2,1,0:T(8,128)(2,1)}, u32[]{:S(2)}) copy-start(bf16[8,32,768]{2,1,0:T(8,128)(2,1)} %param.15) | copy-start | bytes 1179652
  52.8 15.9 %copy-start.3 = (bf16[256,768]{1,0:T(8,128)(2,1)S(1)}, bf16[256,768]{1,0:T(8,128)(2,1)}, u32[]{:S(2)}) copy-start(bf16[256,768]{1,0:T(8,128)(2,1)} %get-tuple-element.42.h_ref) | copy-start | bytes 1179652
  52.8 15.9 %copy-start.5 = (bf16[32,768]{1,0:T(8,128)(2,1)S(1)}, bf16[32,768]{1,0:T(8,128)(2,1)}, u32[]{:S(2)}) copy-start(bf16[32,768]{1,0:T(8,128)(2,1)} %copy-done.4) | copy-start | bytes 147460
  52.8 15.9 %all-to-all-start.2 = ((bf16[32,8,768]{2,1,0:T(8,128)(2,1)}), bf16[32,8,768]{2,1,0:T(8,128)(2,1)S(1)}, u32[]{:S(2)}, u32[]{:S(2)}) async-start(bf16[32,8,768]{2,1,0:T(8,128)(2,1)} %bitcast.56), calls=%async_computation.2 | async-start | bytes 786432 | tf_op jit(solution)/shard_map/all_to_all | solution.py:381
  55.7 1.0 %copy-start.7 = (bf16[768,256]{1,0:T(8,128)(2,1)S(1)}, bf16[768,256]{1,0:T(8,128)(2,1)}, u32[]{:S(2)}) copy-start(bf16[768,256]{1,0:T(8,128)(2,1)} %get-tuple-element.38.refs_0_) | copy-start | bytes 1179652
  56.7 1.0 %copy-start.8 = (bf16[768,256]{1,0:T(8,128)(2,1)S(1)}, bf16[768,256]{1,0:T(8,128)(2,1)}, u32[]{:S(2)}) copy-start(bf16[768,256]{1,0:T(8,128)(2,1)} %get-tuple-element.39.refs_1_) | copy-start | bytes 1179652
  59.8 0.7 copy-start.6
  60.6 2.2 %collective-permute-start.7 = (bf16[2,8,48,384]{3,2,1,0:T(8,128)(2,1)}, bf16[2,8,48,384]{3,2,1,0:T(8,128)(2,1)S(1)}, u32[]{:S(2)}, u32[]{:S(2)}) collective-permute-start(bf16[2,8,48,384]{3,2,1,0:T(8,128)(2,1)} %get-tuple-element.48), channel_id=1, source_target_pairs={{0,1},{1,0},{2,3},{3,2},{4,5},{5,4},{6,7},{7,6},{8,9},{9,8},{10,11... | collective-permute-start | bytes 1769480 | tf_op jit(solution)/shard_map/ppermute | solution.py:407
  62.9 16.5 %collective-permute-start.8 = (bf16[8,48,384]{2,1,0:T(8,128)(2,1)S(1)}, bf16[8,48,384]{2,1,0:T(8,128)(2,1)S(1)}, u32[]{:S(2)}, u32[]{:S(2)}) collective-permute-start(bf16[8,48,384]{2,1,0:T(8,128)(2,1)S(1)} %get-tuple-element.50), channel_id=1, source_target_pairs={{0,16},{16,0},{1,17},{17,1},{2,18},{18,2},{3,19},{19,3},{4,20},{20... | collective-permute-start | bytes 884744 | tf_op jit(solution)/shard_map/ppermute | solution.py:411
  68.7 26.1 %copy-start.9 = (f32[3,3,768]{2,1,0:T(4,128)S(1)}, f32[3,3,768]{2,1,0:T(4,128)}, u32[]{:S(2)}) copy-start(f32[3,3,768]{2,1,0:T(4,128)} %taps_ref.3) | copy-start | bytes 82948
  70.6 4.7 %collective-permute-start.3 = (bf16[64,768]{1,0:T(8,128)(2,1)S(1)}, bf16[64,768]{1,0:T(8,128)(2,1)S(1)}, u32[]{:S(2)}, u32[]{:S(2)}) collective-permute-start(bf16[64,768]{1,0:T(8,128)(2,1)S(1)} %get-tuple-element.44), channel_id=1, source_target_pairs={{0,16},{16,0},{1,17},{17,1},{2,18},{18,2},{3,19},{19,3},{4,20},{20... | collective-permute-start | bytes 294920 | tf_op jit(solution)/shard_map/ppermute | solution.py:519
  71.7 20.0 %all-to-all-start.3 = ((bf16[32,8,768]{2,1,0:T(8,128)(2,1)}), bf16[32,8,768]{2,1,0:T(8,128)(2,1)S(1)}, u32[]{:S(2)}, u32[]{:S(2)}) async-start(bf16[32,8,768]{2,1,0:T(8,128)(2,1)} %bitcast.44), calls=%async_computation.3 | async-start | bytes 786432 | tf_op jit(solution)/shard_map/all_to_all | solution.py:381
  75.5 4.0 %collective-permute-start.4 = (bf16[42,768]{1,0:T(8,128)(2,1)S(1)}, bf16[42,768]{1,0:T(8,128)(2,1)S(1)}, u32[]{:S(2)}, u32[]{:S(2)}) collective-permute-start(bf16[42,768]{1,0:T(8,128)(2,1)S(1)} %concatenate.30), channel_id=1, source_target_pairs={{0,1},{1,0},{2,3},{3,2},{4,5},{5,4},{6,7},{7,6},{8,9},{9,8},{10,11... | collective-permute-start | bytes 193544 | tf_op jit(solution)/shard_map/ppermute | solution.py:368
  75.7 10.8 %collective-permute-start.6 = (bf16[10,768]{1,0:T(8,128)(2,1)S(1)}, bf16[10,768]{1,0:T(8,128)(2,1)S(1)}, u32[]{:S(2)}, u32[]{:S(2)}) collective-permute-start(bf16[10,768]{1,0:T(8,128)(2,1)S(1)} %pad_maximum_fusion.7), channel_id=1, source_target_pairs={{0,15},{1,2},{2,1},{3,4},{4,3},{5,6},{6,5},{7,8},{8,7},{9,10},{10,... | collective-permute-start | bytes 46088 | tf_op jit(solution)/shard_map/ppermute | solution.py:370
  79.6 4.5 %collective-permute-start.5 = (f32[16,768]{1,0:T(8,128)S(1)}, f32[16,768]{1,0:T(8,128)S(1)}, u32[]{:S(2)}, u32[]{:S(2)}) collective-permute-start(f32[16,768]{1,0:T(8,128)S(1)} %add_add_fusion), channel_id=1, source_target_pairs={{0,2},{1,3},{2,0},{3,1},{4,6},{5,7},{6,4},{7,5},{8,10},{9,11},{10,... | collective-permute-start | bytes 147464 | tf_op jit(solution)/shard_map/ppermute | solution.py:530
  79.7 6.8 %collective-permute-start.9 = (bf16[4,48,384]{2,1,0:T(8,128)(2,1)S(1)}, bf16[4,48,384]{2,1,0:T(8,128)(2,1)S(1)}, u32[]{:S(2)}, u32[]{:S(2)}) collective-permute-start(bf16[4,48,384]{2,1,0:T(8,128)(2,1)S(1)} %dynamic-slice_bitcast_fusion), channel_id=1, source_target_pairs={{0,2},{1,3},{2,0},{3,1},{4,6},{5,7},{6,4},{7,5},{8,10},{9,11},{10,... | collective-permute-start | bytes 442376 | tf_op jit(solution)/shard_map/ppermute | solution.py:414
  86.6 5.0 %collective-permute-start.10 = (bf16[160,384]{1,0:T(8,128)(2,1)S(1)}, bf16[160,384]{1,0:T(8,128)(2,1)S(1)}, u32[]{:S(2)}, u32[]{:S(2)}) collective-permute-start(bf16[160,384]{1,0:T(8,128)(2,1)S(1)} %pad_maximum_fusion.1), channel_id=1, source_target_pairs={{0,4},{1,5},{2,6},{3,7},{4,0},{5,1},{6,2},{7,3},{8,12},{9,13},{10,... | collective-permute-start | bytes 368648 | tf_op jit(solution)/shard_map/ppermute | solution.py:542
  91.8 5.8 %collective-permute-start.11 = (bf16[112,384]{1,0:T(8,128)(2,1)S(1)}, bf16[112,384]{1,0:T(8,128)(2,1)S(1)}, u32[]{:S(2)}, u32[]{:S(2)}) collective-permute-start(bf16[112,384]{1,0:T(8,128)(2,1)S(1)} %pad_maximum_fusion.2), channel_id=1, source_target_pairs={{0,8},{1,9},{2,10},{3,11},{4,12},{5,13},{6,14},{7,15},{8,0},{9,1},... | collective-permute-start | bytes 258056 | tf_op jit(solution)/shard_map/ppermute | solution.py:542

commit v6 on v5

--- a/solution.py
+++ b/solution.py
@@ -167,7 +167,7 @@
 def attention_kernel(
     slots, blocks, unroll,
     arrived_hbm, qkv_weight_hbm, bias_hbm, grad_att_hbm,
-    grad_hbm, att_hbm,
+    grad_hbm, att_hbm, att_sent_hbm,
     rows_buffer, qkv_weight, bias, grad_att, att_ref, qkv, grad_qkv, sems,
 ):
     cells, width = rows_buffer.shape
@@ -233,11 +233,12 @@
         heads(0, 0)
     else:
         lax.fori_loop(0, HEADS // unroll, heads, 0)
-    last = pltpu.make_async_copy(att_ref, att_hbm, sems.at[1])
-    last.start()
+    sent = att_sent_hbm.shape[0]
+    other = pl.multiple_of((1 - jnp.minimum(place()[0], 1)) * sent, 16)
+    leaving = fetch(sems, (att_ref.at[pl.ds(other, sent)], att_sent_hbm), (att_ref, att_hbm))
     grad = dot(qkv_weight[...], grad_qkv[...]).astype(bf16)
     rows_buffer[...] = dot(position_by_row(cells, slots, blocks, 0), grad, NT).astype(bf16)
-    for copy in [last, *fetch(sems, (rows_buffer, grad_hbm))]:
+    for copy in [*leaving, *fetch(sems.at[pl.ds(2, 1)], (rows_buffer, grad_hbm))]:
         copy.wait()
 
 
@@ -252,23 +253,19 @@
     mix(slots, blocks, out_weight_ref, att_ref, mixed_ref)
 
 
-def halves_kernel(
-    slots, blocks, cot_ref, att_ref, out_weight_ref, mixed_ref, kept_ref, sent_ref, part
-):
-    lats, chips, cols, rows = kept_ref.shape
-    core = place()[2]
-    for a in range(lats):
-        part[...] = dot(cot_ref[...], att_ref[a * rows : (a + 1) * rows], NT).astype(bf16)
-        for chip in range(chips):
-            kept_ref[a, chip] = part[pl.ds(pl.multiple_of((2 * chip + core) * cols, 16), cols)]
-            sent_ref[a, chip] = part[pl.ds(pl.multiple_of((2 * chip + 1 - core) * cols, 16), cols)]
+def mix_kernel(slots, blocks, att_ref, out_weight_ref, mixed_ref):
     mix(slots, blocks, out_weight_ref, att_ref, mixed_ref)
 
 
-def join_halves_kernel(kept_ref, met_ref, out_ref, sent_ref):
-    lat = jnp.minimum(place()[0], 1)
-    out_ref[...] = (kept_ref[lat].astype(f32) + met_ref[lat].astype(f32)).astype(bf16)
-    sent_ref[...] = (kept_ref[1 - lat].astype(f32) + met_ref[1 - lat].astype(f32)).astype(bf16)
+def halves_kernel(cot_ref, cot_met_ref, att_ref, att_met_ref, kept_ref, sent_ref, part):
+    chips, cols, rows = kept_ref.shape
+    lat, _, core = place()
+    mine = att_ref[pl.ds(pl.multiple_of(jnp.minimum(lat, 1) * rows, 16), rows)]
+    total = dot(cot_ref[...], mine, NT) + dot(cot_met_ref[...], att_met_ref[...], NT)
+    part[...] = total.astype(bf16)
+    for chip in range(chips):
+        kept_ref[chip] = part[pl.ds(pl.multiple_of((2 * chip + core) * cols, 16), cols)]
+        sent_ref[chip] = part[pl.ds(pl.multiple_of((2 * chip + 1 - core) * cols, 16), cols)]
 
 
 def leave_kernel(pattern_ref, mixed_ref, h_ref, out_ref):
@@ -381,12 +378,12 @@
     return lax.all_to_all(sent, AXES, split_axis=0, concat_axis=0, tiled=True).reshape(cells, width)
 
 
-def attended_products(slots, blocks, flags, cot_cols, att, out_weight):
+def attended_products(slots, blocks, cot_cols, cot_met, att, att_sent, out_weight):
     width, cells = att.shape
     lat_count, lon_count = lax.axis_size("lat"), lax.axis_size("lon")
     rows, cols = width // lat_count, width // lon_count
     mixed_shape = shape((cells, width), bf16)
-    if lat_count != 2 or lon_count % 4 or lon_count & (lon_count - 1) or rows % 128 or cols % 16:
+    if cot_met is None:
         mixed, parts = call(
             lambda *refs: products_kernel(slots, blocks, *refs),
             "attended_products", [mixed_shape, shape((width, width), bf16)],
@@ -396,19 +393,16 @@
         parts = parts.reshape(lat_count * lon_count, cols, rows)
         parts = lax.all_to_all(parts, AXES, split_axis=0, concat_axis=0, tiled=True)
         return mixed, jnp.sum(parts.astype(f32), axis=0)
-    halves = shape((lat_count, lon_count // 2, cols, rows), bf16)
-    quarters = shape((lon_count // 2, cols, rows), bf16)
-    mixed, kept, sent = call(
-        lambda *refs: halves_kernel(slots, blocks, *refs),
-        "attended_products", [mixed_shape, halves, halves],
-        [cot_cols, att, out_weight],
+    mixed = call(
+        lambda *refs: mix_kernel(slots, blocks, *refs), "mix", [mixed_shape], [att, out_weight]
+    )[0]
+    att_met = lax.ppermute(att_sent, "lat", swap_pairs(2, 1))
+    halves = shape((lon_count // 2, cols, rows), bf16)
+    kept, sent = call(
+        halves_kernel, "project_gradient", [halves, halves], [cot_cols, cot_met, att, att_met],
         [pltpu.VMEM((width, rows), bf16)],
     )
     met = lax.ppermute(sent, "lon", swap_pairs(lon_count, 1))
-    kept, sent = call(
-        join_halves_kernel, "project_join", [quarters, quarters], [kept, met]
-    )
-    met = lax.ppermute(sent, "lat", swap_pairs(2, 1))
     parts = (kept.astype(f32) + met.astype(f32)).astype(bf16)
     kept, sent = halved(parts, 2)
     return mixed, (kept, lax.ppermute(sent, "lon", swap_pairs(lon_count, 2)))
@@ -476,6 +470,10 @@
         "cotangent_products", [cols_shape, cols_shape], [cot_arrived, out_weight], mib=BIG,
     )
 
+    staged = lat_count == 2 and lon_count % 4 == 0 and lon_count & (lon_count - 1) == 0
+    staged = staged and (width // 2) % 128 == 0 and (width // lon_count) % 16 == 0
+    cot_met = lax.ppermute(cot_cols, "lat", swap_pairs(2, 1)) if staged else None
+
     beside = lat_rims(fields, met)
     beside = (*beside, *lon_rims(flags, beside, columns))
     h, packed = call(
@@ -484,12 +482,13 @@
         [pad, pltpu.VMEM((cells, width), bf16)], mib=BIG,
     )
     arrived = exchange(packed)
-    grad_grouped, att = pl.pallas_call(
+    half_shape = shape((width // 2, cells), bf16)
+    grad_grouped, att, att_sent = pl.pallas_call(
         lambda *refs: attention_kernel(slots, blocks, UNROLL, *refs),
         name="attention",
-        out_shape=[rows_shape, cols_shape],
+        out_shape=[rows_shape, cols_shape, half_shape],
         in_specs=[ANY] * 4,
-        out_specs=[ANY] * 2,
+        out_specs=[ANY] * 3,
         scratch_shapes=[
             pltpu.VMEM((cells, width), bf16), pltpu.VMEM(qkv_weight.shape, bf16),
             pltpu.VMEM(bias.shape, f32), pltpu.VMEM((width, cells), bf16),
@@ -502,7 +501,9 @@
         ),
     )(arrived, qkv_weight, bias, grad_att)
     grad_home = exchange(grad_grouped)
-    mixed, project = attended_products(slots, blocks, flags, cot_cols, att, out_weight)
+    mixed, project = attended_products(
+        slots, blocks, cot_cols, cot_met, att, att_sent, out_weight
+    )
     grad_home, mixed = lax.optimization_barrier((grad_home, mixed))
     mixed_home = exchange(mixed)
 
@@ -528,13 +529,12 @@
         beside = (*beside, even, odd)
         sums = sums + one_term(met)
         sums = sums + lax.ppermute(sums, "lon", swap_pairs(lon_count, 2))
-        sums, odd = lax.optimization_barrier((sums, odd))
-        beside = (*beside[:2], even, odd)
         kept, met = project
         bit = 4
         while bit < lon_count:
             if 2 * bit == lon_count:
-                sums, mixed_home = lax.optimization_barrier((sums, mixed_home))
+                sums, odd, mixed_home = lax.optimization_barrier((sums, odd, mixed_home))
+                beside = (*beside[:3], odd)
             project = (kept.astype(f32) + met.astype(f32)).astype(bf16)
             kept, sent = halved(project, bit)
             high_low = two_terms(sums).reshape(-1, sent.shape[-1])

time: 99 us -> 98.4 us (level)
  starting transfers between devices: 35.1 us -> 31.9 us
  Pallas kernels: 25 us -> 26.7 us
  waiting for transfers between devices: 28.8 us -> 27.3 us
  local copies, waits for them, and re-layouts: 6.72 us -> 8.18 us
    all_to_all x4, waiting for transfers between devices: 12.9 us -> 7.23 us  [exchange(): lax.all_to_all(sent, AXES, split_axis=0, concat_axis=0, tiled=True)]
    ppermute x2, starting transfers between devices: 5.05 us -> 2.1 us  [body(): lax.ppermute(jnp.concatenate([high_low, sent], axis=0), 'lon', swap_pairs...]
    ppermute x1 -> x2, waiting for transfers between devices: 0.01 us -> 2.68 us  [the longest x1 2.68 us: attended_products(): att_met = lax.ppermute(att_sent, 'lat', swap_pairs(2, 1))]
    ppermute x1, waiting for transfers between devices: 2.21 us -> 0.01 us  [attended_products(): met = lax.ppermute(sent, 'lon', swap_pairs(lon_count, 1))]
    ppermute x2, starting transfers between devices: 8.28 us -> 6.11 us  [lon_rims(): met_odd = lax.ppermute(column(1, jnp.logical_not(even)), 'lon', odd_pairs)]
    ppermute x2, waiting for transfers between devices: 2.97 us -> 4.81 us  [body(): lax.ppermute(jnp.concatenate([high_low, sent], axis=0), 'lon', swap_pairs...]
    pallas_call x9, Pallas kernels: 16.1 us -> 17.8 us  [call(): pl.pallas_call(kernel, name=name, grid=(1,), out_shape=list(out_shape), i...]
    ppermute x1, starting transfers between devices: 0.07 us -> 1.54 us  [body(): sums = sums + lax.ppermute(sums, 'lon', swap_pairs(lon_count, 2))]
  transfers between devices with their start and end apart: 16 -> 17, of which waited for: 8 -> 10; matrix products, arithmetic and copies ran while one was open for 4% -> 5% of each run, Pallas kernels for 13% -> 24%
where the time goes in v6:
time: 98.4 us; the launch traced here: 97.7 us
  starting transfers between devices  31.9 us (32%)
  waiting for transfers between devices  27.3 us (28%)
  Pallas kernels  26.7 us (27%)
  local copies, waits for them, and re-layouts  8.18 us (8%)
  other arithmetic  2.54 us (3%)
  between operations  1.07 us (1%)
    pallas_call x9, Pallas kernels, call(): pl.pallas_call(kernel, name=name, grid=(1,), out_shape=list(out_shape), i...  17.8 us
    all_to_all x4, starting transfers between devices, exchange(): lax.all_to_all(sent, AXES, split_axis=0, concat_axis=0, tiled=True)  13.8 us
    pallas_call x1, Pallas kernels, body(): pl.pallas_call(lambda *refs: attention_kernel(slots, blocks, UNROLL, *ref...  8.98 us
    all_to_all x4, waiting for transfers between devices, exchange(): lax.all_to_all(sent, AXES, split_axis=0, concat_axis=0, tiled=True)  7.23 us
    ppermute x2, waiting for transfers between devices, lon_rims(): met_odd = lax.ppermute(column(1, jnp.logical_not(even)), 'lon', odd_pairs)  6.83 us
    ppermute x2, starting transfers between devices, lon_rims(): met_odd = lax.ppermute(column(1, jnp.logical_not(even)), 'lon', odd_pairs)  6.11 us
    unnamed x43, local copies, waits for them, and re-layouts  5.88 us
    ppermute x2, waiting for transfers between devices, body(): lax.ppermute(jnp.concatenate([high_low, sent], axis=0), 'lon', swap_pairs...  4.81 us
  transfers between devices with their start and end apart: 17, of which 10 were waited for; matrix products, arithmetic and copies ran while one was open for 5% of the time, Pallas kernels for 24%

profile of v6, /device:TPU:0, one launch (start us, length us, event | category | flops | bytes accessed | tf_op | source)
XLA Modules:
  0.0 97.7 jit_solution(8369249577167063026)
XLA Ops:
  0.6 2.3 %start.1 = (bf16[256,768]{1,0:T(8,128)(2,1)}, bf16[32,768]{1,0:T(8,128)(2,1)}, bf16[2,8,768]{2,1,0:T(8,128)(2,1)}) custom-call(s32[1,256]{1,0:T(1,128)} %bitcast.44, bf16[256,768]{1,0:T(8,128)(2,1)} %bitcast.40, bf16[8,32,768]{2,1,0:T(8,128)(2,1)} %field_ref.5), custom_call_target="tpu_custom_call" | custom-call | bytes 1254400 | tf_op jit(solution)/shard_map/start/pallas_call | solution.py:41
  2.9 2.9 %collective-permute-start = (bf16[32,768]{1,0:T(8,128)(2,1)}, bf16[32,768]{1,0:T(8,128)(2,1)S(1)}, u32[]{:S(2)}, u32[]{:S(2)}) collective-permute-start(bf16[32,768]{1,0:T(8,128)(2,1)} %get-tuple-element.29), channel_id=1, source_target_pairs={{0,16},{16,0},{1,17},{17,1},{2,18},{18,2},{3,19},{19,3},{4,20},{20... | collective-permute-start | bytes 147464 | tf_op jit(solution)/shard_map/ppermute | solution.py:466
  5.8 4.9 %all-to-all-start.1 = ((bf16[32,8,768]{2,1,0:T(8,128)(2,1)}), bf16[32,8,768]{2,1,0:T(8,128)(2,1)S(1)}, u32[]{:S(2)}, u32[]{:S(2)}) async-start(bf16[32,8,768]{2,1,0:T(8,128)(2,1)} %bitcast.55), calls=%async_computation.1 | async-start | bytes 786432 | tf_op jit(solution)/shard_map/all_to_all | solution.py:378
  10.8 0.7 slice_bitcast_fusion.2
  11.5 0.0 collective-permute-done.before_ref.after_ref
  11.6 4.4 %collective-permute-start.2 = (bf16[10,768]{1,0:T(8,128)(2,1)S(1)}, bf16[10,768]{1,0:T(8,128)(2,1)S(1)}, u32[]{:S(2)}, u32[]{:S(2)}) collective-permute-start(bf16[10,768]{1,0:T(8,128)(2,1)S(1)} %pad_maximum_fusion.6), channel_id=1, source_target_pairs={{0,15},{1,2},{2,1},{3,4},{4,3},{5,6},{6,5},{7,8},{8,7},{9,10},{10,... | collective-permute-start | bytes 46088 | tf_op jit(solution)/shard_map/ppermute | solution.py:367
  16.0 0.1 collective-permute-start.1
  16.1 1.3 %reshape.93.gain_ref = f32[1,768]{1,0:T(1,128)} reshape(f32[768]{0:T(1024)} %param.10) | data formatting | bytes 6144 | tf_op jit(solution)/shard_map/reshape | solution.py:448
  17.3 5.5 %collective-permute-done.2.odd_ref = bf16[10,768]{1,0:T(8,128)(2,1)S(1)} collective-permute-done((bf16[10,768]{1,0:T(8,128)(2,1)S(1)}, bf16[10,768]{1,0:T(8,128)(2,1)S(1)}, u32[]{:S(2)}, u32[]{:S(2)}) %collective-permute-start.2) | collective-permute-done | bytes 15392 | tf_op jit(solution)/shard_map/ppermute | solution.py:367
  22.8 0.0 collective-permute-done.1.even_ref
  22.8 0.6 copy-done.12
  23.4 0.6 copy-done.14
  24.0 3.3 %convolve_normalize_pack.1 = (bf16[256,768]{1,0:T(8,128)(2,1)}, bf16[256,768]{1,0:T(8,128)(2,1)}) custom-call(s32[1,256]{1,0:T(1,128)} %bitcast.45, bf16[8,32,768]{2,1,0:T(8,128)(2,1)} %field_ref.5, bf16[32,768]{1,0:T(8,128)(2,1)} %copy-done.6, bf16[32,768]{1,0:T(8,128)(2,1)} %copy-done.6, bf16[10,768]{1,0:T(8,128)(2,1)} %copy-done.14, ...), custom_call_target="tpu_custom_call" | custom-call | bytes 1340416 | tf_op jit(solution)/shard_map/convolve_normalize_pack/pallas_call | solution.py:41
  27.3 0.0 all-to-all-done.1
  27.3 3.2 %all-to-all-start = ((bf16[32,8,768]{2,1,0:T(8,128)(2,1)}), bf16[32,8,768]{2,1,0:T(8,128)(2,1)S(1)}, u32[]{:S(2)}, u32[]{:S(2)}) async-start(bf16[32,8,768]{2,1,0:T(8,128)(2,1)} %bitcast.57), calls=%async_computation | async-start | bytes 786432 | tf_op jit(solution)/shard_map/all_to_all | solution.py:378
  30.5 0.3 copy.14
  30.8 1.2 %pad_maximum_fusion.refs_2_ = f32[24,64,128]{2,1,0:T(8,128)} fusion(f32[24,64,64]{2,1,0:T(8,128)S(1)} %bitcast.48), kind=kLoop, calls=%fused_computation | loop fusion | flops 196608 | bytes 1179648 | tf_op jit(solution)/shard_map/concatenate | solution.py:451
  31.9 3.0 %cotangent_products.1 = (bf16[768,256]{1,0:T(8,128)(2,1)}, bf16[768,256]{1,0:T(8,128)(2,1)}) custom-call(bf16[256,768]{1,0:T(8,128)(2,1)} %bitcast.49, bf16[768,768]{1,0:T(8,128)(2,1)} %refs_1_.5), custom_call_target="tpu_custom_call" | custom-call | bytes 2359296 | tf_op jit(solution)/shard_map/cotangent_products/pallas_call | solution.py:41
  34.9 1.8 %collective-permute-start.6 = (bf16[768,256]{1,0:T(8,128)(2,1)}, bf16[768,256]{1,0:T(8,128)(2,1)}, u32[]{:S(2)}, u32[]{:S(2)}) collective-permute-start(bf16[768,256]{1,0:T(8,128)(2,1)} %get-tuple-element.41.cot_ref), channel_id=1, source_target_pairs={{0,16},{16,0},{1,17},{17,1},{2,18},{18,2},{3,19},{19,3},{4,20},{20... | collective-permute-start | bytes 1179656 | tf_op jit(solution)/shard_map/ppermute | solution.py:475
  36.7 6.9 %all-to-all-done = bf16[32,8,768]{2,1,0:T(8,128)(2,1)S(1)} async-done(((bf16[32,8,768]{2,1,0:T(8,128)(2,1)}), bf16[32,8,768]{2,1,0:T(8,128)(2,1)S(1)}, u32[]{:S(2)}, u32[]{:S(2)}) %all-to-all-start) | async-done | bytes 393248 | tf_op jit(solution)/shard_map/all_to_all | solution.py:378
  43.6 0.7 copy-done.20
  44.3 0.0 copy-start.15
  44.3 0.0 copy-start.16
  44.4 0.0 copy-start.17
  44.4 9.0 %attention.1 = (bf16[256,768]{1,0:T(8,128)(2,1)}, bf16[768,256]{1,0:T(8,128)(2,1)}, bf16[384,256]{1,0:T(8,128)(2,1)}) custom-call(bf16[256,768]{1,0:T(8,128)(2,1)} %bitcast.56, bf16[768,2304]{1,0:T(8,128)(2,1)} %refs_1_.4, f32[24,64,128]{2,1,0:T(8,128)} %pad_maximum_fusion.refs_2_, bf16[768,256]{1,0:T(8,128)(2,1)} %get-tuple-element.33.refs_3_), custom_call_target="tpu_custom_call" | custom-call | flops 12000000000 | bytes 8000000 | tf_op jit(solution)/shard_map/attention/pallas_call | solution.py:486
  53.4 0.0 copy-start.1
  53.4 0.0 copy-start.2
  53.4 0.0 copy-start.3
  53.4 1.1 %collective-permute-start.7 = (bf16[384,256]{1,0:T(8,128)(2,1)}, bf16[384,256]{1,0:T(8,128)(2,1)S(1)}, u32[]{:S(2)}, u32[]{:S(2)}) collective-permute-start(bf16[384,256]{1,0:T(8,128)(2,1)} %get-tuple-element.42), channel_id=1, source_target_pairs={{0,16},{16,0},{1,17},{17,1},{2,18},{18,2},{3,19},{19,3},{4,20},{20... | collective-permute-start | bytes 589832 | tf_op jit(solution)/shard_map/ppermute | solution.py:399
  54.5 2.9 %all-to-all-start.2 = ((bf16[32,8,768]{2,1,0:T(8,128)(2,1)}), bf16[32,8,768]{2,1,0:T(8,128)(2,1)S(1)}, u32[]{:S(2)}, u32[]{:S(2)}) async-start(bf16[32,8,768]{2,1,0:T(8,128)(2,1)} %bitcast.54), calls=%async_computation.2 | async-start | bytes 786432 | tf_op jit(solution)/shard_map/all_to_all | solution.py:378
  57.4 2.7 %collective-permute-done.7.att_met_ref = bf16[384,256]{1,0:T(8,128)(2,1)S(1)} collective-permute-done((bf16[384,256]{1,0:T(8,128)(2,1)}, bf16[384,256]{1,0:T(8,128)(2,1)S(1)}, u32[]{:S(2)}, u32[]{:S(2)}) %collective-permute-start.7) | collective-permute-done | bytes 196640 | tf_op jit(solution)/shard_map/ppermute | solution.py:399
  60.1 0.7 copy-done.9
  60.8 0.0 collective-permute-done.6.cot_met_ref
  60.8 1.0 %copy-done.4 = bf16[768,256]{1,0:T(8,128)(2,1)S(1)} copy-done((bf16[768,256]{1,0:T(8,128)(2,1)S(1)}, bf16[768,256]{1,0:T(8,128)(2,1)}, u32[]{:S(2)}) %copy-start.4) | copy-done | bytes 393240
  61.8 0.9 copy-done.10
  62.7 2.4 %project_gradient.1 = (bf16[8,48,384]{2,1,0:T(8,128)(2,1)S(1)}, bf16[8,48,384]{2,1,0:T(8,128)(2,1)}) custom-call(bf16[768,256]{1,0:T(8,128)(2,1)S(1)} %copy-done.8, bf16[768,256]{1,0:T(8,128)(2,1)} %collective-permute-done.6.cot_met_ref, bf16[768,256]{1,0:T(8,128)(2,1)S(1)} %copy-done.4, bf16[384,256]{1,0:T(8,128)(2,1)S(1)} %copy-done.10), custom_call_target="tpu_custom_call" | custom-call | bytes 1966080 | tf_op jit(solution)/shard_map/project_gradient/pallas_call | solution.py:41
  65.2 0.0 collective-permute-start.8
  65.2 1.0 %copy-done.5 = bf16[768,256]{1,0:T(8,128)(2,1)S(1)} copy-done((bf16[768,256]{1,0:T(8,128)(2,1)S(1)}, bf16[768,256]{1,0:T(8,128)(2,1)}, u32[]{:S(2)}) %copy-start.5) | copy-done | bytes 393240
  66.2 1.5 %mix.1 = bf16[256,768]{1,0:T(8,128)(2,1)} custom-call(bf16[768,256]{1,0:T(8,128)(2,1)S(1)} %copy-done.5, bf16[768,768]{1,0:T(8,128)(2,1)S(1)} %copy-done), custom_call_target="tpu_custom_call" | custom-call | bytes 1966080 | tf_op jit(solution)/shard_map/mix/pallas_call | solution.py:41
  67.7 1.0 %add_convert_fusion = bf16[8,48,384]{2,1,0:T(8,128)(2,1)S(1)} fusion(bf16[8,48,384]{2,1,0:T(8,128)(2,1)} %collective-permute-done.8, bf16[8,48,384]{2,1,0:T(8,128)(2,1)S(1)} %get-tuple-element.43), kind=kLoop, calls=%fused_computation.1 | loop fusion | flops 589824 | bytes 884736 | tf_op jit(solution)/shard_map/convert_element_type | solution.py:406
  68.7 0.0 copy-start.11
  68.8 1.3 %collective-permute-start.9 = (bf16[4,48,384]{2,1,0:T(8,128)(2,1)S(1)}, bf16[4,48,384]{2,1,0:T(8,128)(2,1)S(1)}, u32[]{:S(2)}, u32[]{:S(2)}) collective-permute-start(bf16[4,48,384]{2,1,0:T(8,128)(2,1)S(1)} %dynamic-slice_bitcast_fusion), channel_id=1, source_target_pairs={{0,2},{1,3},{2,0},{3,1},{4,6},{5,7},{6,4},{7,5},{8,10},{9,11},{10,... | collective-permute-start | bytes 442376 | tf_op jit(solution)/shard_map/ppermute | solution.py:408
  70.0 0.3 all-to-all-done.2
  70.4 1.9 %normalize_back.1 = (bf16[8,32,768]{2,1,0:T(8,128)(2,1)S(1)}, f32[16,768]{1,0:T(8,128)S(1)}, bf16[64,768]{1,0:T(8,128)(2,1)S(1)}, bf16[2,8,768]{2,1,0:T(8,128)(2,1)S(1)}) custom-call(s32[1,256]{1,0:T(1,128)S(1)} %bitcast.46, bf16[256,768]{1,0:T(8,128)(2,1)S(1)} %bitcast.42, bf16[256,768]{1,0:T(8,128)(2,1)S(1)} %copy-done.3, bf16[256,768]{1,0:T(8,128)(2,1)S(1)} %bitcast.41, ...), custom_call_target="tpu_custom_call" | custom-call | bytes 2271232 | tf_op jit(solution)/shard_map/normalize_back/pallas_call | solution.py:41
  72.3 1.1 %collective-permute-start.3 = (bf16[64,768]{1,0:T(8,128)(2,1)S(1)}, bf16[64,768]{1,0:T(8,128)(2,1)S(1)}, u32[]{:S(2)}, u32[]{:S(2)}) collective-permute-start(bf16[64,768]{1,0:T(8,128)(2,1)S(1)} %get-tuple-element.39), channel_id=1, source_target_pairs={{0,16},{16,0},{1,17},{17,1},{2,18},{18,2},{3,19},{19,3},{4,20},{20... | collective-permute-start | bytes 294920 | tf_op jit(solution)/shard_map/ppermute | solution.py:520
  73.4 2.8 %all-to-all-start.3 = ((bf16[32,8,768]{2,1,0:T(8,128)(2,1)}), bf16[32,8,768]{2,1,0:T(8,128)(2,1)S(1)}, u32[]{:S(2)}, u32[]{:S(2)}) async-start(bf16[32,8,768]{2,1,0:T(8,128)(2,1)} %bitcast.18), calls=%async_computation.3 | async-start | bytes 786432 | tf_op jit(solution)/shard_map/all_to_all | solution.py:378
  76.2 0.8 collective-permute-done.3
  77.1 0.2 concatenate.30
  77.2 0.1 collective-permute-start.4
  77.3 0.0 collective-permute-done.9
  77.3 0.1 fusion
  77.4 1.2 %collective-permute-done.4 = bf16[42,768]{1,0:T(8,128)(2,1)S(1)} collective-permute-done((bf16[42,768]{1,0:T(8,128)(2,1)S(1)}, bf16[42,768]{1,0:T(8,128)(2,1)S(1)}, u32[]{:S(2)}, u32[]{:S(2)}) %collective-permute-start.4) | collective-permute-done | bytes 64544 | tf_op jit(solution)/shard_map/ppermute | solution.py:365
  78.6 1.5 %collective-permute-start.5 = (f32[16,768]{1,0:T(8,128)S(1)}, f32[16,768]{1,0:T(8,128)S(1)}, u32[]{:S(2)}, u32[]{:S(2)}) collective-permute-start(f32[16,768]{1,0:T(8,128)S(1)} %add_add_fusion), channel_id=1, source_target_pairs={{0,2},{1,3},{2,0},{3,1},{4,6},{5,7},{6,4},{7,5},{8,10},{9,11},{10,... | collective-permute-start | bytes 147464 | tf_op jit(solution)/shard_map/ppermute | solution.py:531
  80.2 3.7 %collective-permute-done.5 = f32[16,768]{1,0:T(8,128)S(1)} collective-permute-done((f32[16,768]{1,0:T(8,128)S(1)}, f32[16,768]{1,0:T(8,128)S(1)}, u32[]{:S(2)}, u32[]{:S(2)}) %collective-permute-start.5) | collective-permute-done | bytes 49184 | tf_op jit(solution)/shard_map/ppermute | solution.py:531
  83.9 1.3 %collective-permute-start.10 = (bf16[160,384]{1,0:T(8,128)(2,1)S(1)}, bf16[160,384]{1,0:T(8,128)(2,1)S(1)}, u32[]{:S(2)}, u32[]{:S(2)}) collective-permute-start(bf16[160,384]{1,0:T(8,128)(2,1)S(1)} %pad_maximum_fusion.1), channel_id=1, source_target_pairs={{0,4},{1,5},{2,6},{3,7},{4,0},{5,1},{6,2},{7,3},{8,12},{9,13},{10,... | collective-permute-start | bytes 368648 | tf_op jit(solution)/shard_map/ppermute | solution.py:542
  85.3 1.7 %collective-permute-start.11 = (bf16[10,768]{1,0:T(8,128)(2,1)S(1)}, bf16[10,768]{1,0:T(8,128)(2,1)S(1)}, u32[]{:S(2)}, u32[]{:S(2)}) collective-permute-start(bf16[10,768]{1,0:T(8,128)(2,1)S(1)} %pad_maximum_fusion.7), channel_id=1, source_target_pairs={{0,15},{1,2},{2,1},{3,4},{4,3},{5,6},{6,5},{7,8},{8,7},{9,10},{10,... | collective-permute-start | bytes 46088 | tf_op jit(solution)/shard_map/ppermute | solution.py:367
  87.1 2.9 %collective-permute-done.10 = bf16[160,384]{1,0:T(8,128)(2,1)S(1)} collective-permute-done((bf16[160,384]{1,0:T(8,128)(2,1)S(1)}, bf16[160,384]{1,0:T(8,128)(2,1)S(1)}, u32[]{:S(2)}, u32[]{:S(2)}) %collective-permute-start.10) | collective-permute-done | bytes 122912 | tf_op jit(solution)/shard_map/ppermute | solution.py:542
  90.0 1.4 %collective-permute-done.11.odd_ref = bf16[10,768]{1,0:T(8,128)(2,1)S(1)} collective-permute-done((bf16[10,768]{1,0:T(8,128)(2,1)S(1)}, bf16[10,768]{1,0:T(8,128)(2,1)S(1)}, u32[]{:S(2)}, u32[]{:S(2)}) %collective-permute-start.11) | collective-permute-done | bytes 15392 | tf_op jit(solution)/shard_map/ppermute | solution.py:367
  91.4 0.0 all-to-all-done.3
  91.5 0.8 collective-permute-start.12
  92.3 1.0 %block_out.1 = bf16[256,768]{1,0:T(8,128)(2,1)} custom-call(s32[1,256]{1,0:T(1,128)S(1)} %bitcast.47, bf16[256,768]{1,0:T(8,128)(2,1)S(1)} %bitcast.43, bf16[256,768]{1,0:T(8,128)(2,1)S(1)} %copy-done.3), custom_call_target="tpu_custom_call" | custom-call | bytes 1180672 | tf_op jit(solution)/shard_map/block_out/pallas_call | solution.py:41
  93.3 1.7 %convolve_back.1 = bf16[8,32,768]{2,1,0:T(8,128)(2,1)} custom-call(bf16[8,32,768]{2,1,0:T(8,128)(2,1)S(1)} %get-tuple-element.47.field_ref, bf16[32,768]{1,0:T(8,128)(2,1)S(1)} %slice.120.before_ref.after_ref, bf16[32,768]{1,0:T(8,128)(2,1)S(1)} %slice.120.before_ref.after_ref, bf16[10,768]{1,0:T(8,128)(2,1)S(1)} %slice.121.even_ref, ...), custom_call_target="tpu_custom_call" | custom-call | bytes 943104 | tf_op jit(solution)/shard_map/convolve_back/pallas_call | solution.py:41
  95.0 1.9 %collective-permute-done.12 = bf16[112,384]{1,0:T(8,128)(2,1)S(1)} collective-permute-done((bf16[112,384]{1,0:T(8,128)(2,1)S(1)}, bf16[112,384]{1,0:T(8,128)(2,1)S(1)}, u32[]{:S(2)}, u32[]{:S(2)}) %collective-permute-start.12) | collective-permute-done | bytes 86048 | tf_op jit(solution)/shard_map/ppermute | solution.py:542
  97.0 0.7 finish.1
  (63 shorter events, 0.5 us)
Async XLA Ops:
  0.6 29.8 %copy-start.19 = (f32[24,64,64]{2,1,0:T(8,128)S(1)}, f32[24,64,64]{2,1,0:T(8,128)}, u32[]{:S(2)}) copy-start(f32[24,64,64]{2,1,0:T(8,128)} %param.13) | copy-start | bytes 1179652
  2.9 8.6 %collective-permute-start = (bf16[32,768]{1,0:T(8,128)(2,1)}, bf16[32,768]{1,0:T(8,128)(2,1)S(1)}, u32[]{:S(2)}, u32[]{:S(2)}) collective-permute-start(bf16[32,768]{1,0:T(8,128)(2,1)} %get-tuple-element.29), channel_id=1, source_target_pairs={{0,16},{16,0},{1,17},{17,1},{2,18},{18,2},{3,19},{19,3},{4,20},{20... | collective-permute-start | bytes 147464 | tf_op jit(solution)/shard_map/ppermute | solution.py:466
  5.8 21.5 %all-to-all-start.1 = ((bf16[32,8,768]{2,1,0:T(8,128)(2,1)}), bf16[32,8,768]{2,1,0:T(8,128)(2,1)S(1)}, u32[]{:S(2)}, u32[]{:S(2)}) async-start(bf16[32,8,768]{2,1,0:T(8,128)(2,1)} %bitcast.55), calls=%async_computation.1 | async-start | bytes 786432 | tf_op jit(solution)/shard_map/all_to_all | solution.py:378
  11.5 11.3 %copy-start.6 = (bf16[32,768]{1,0:T(8,128)(2,1)}, bf16[32,768]{1,0:T(8,128)(2,1)S(1)}, u32[]{:S(2)}) copy-start(bf16[32,768]{1,0:T(8,128)(2,1)S(1)} %collective-permute-done.before_ref.after_ref) | copy-start | bytes 147460
  11.6 11.2 %collective-permute-start.2 = (bf16[10,768]{1,0:T(8,128)(2,1)S(1)}, bf16[10,768]{1,0:T(8,128)(2,1)S(1)}, u32[]{:S(2)}, u32[]{:S(2)}) collective-permute-start(bf16[10,768]{1,0:T(8,128)(2,1)S(1)} %pad_maximum_fusion.6), channel_id=1, source_target_pairs={{0,15},{1,2},{2,1},{3,4},{4,3},{5,6},{6,5},{7,8},{8,7},{9,10},{10,... | collective-permute-start | bytes 46088 | tf_op jit(solution)/shard_map/ppermute | solution.py:367
  16.0 6.8 %collective-permute-start.1 = (bf16[10,768]{1,0:T(8,128)(2,1)S(1)}, bf16[10,768]{1,0:T(8,128)(2,1)S(1)}, u32[]{:S(2)}, u32[]{:S(2)}) collective-permute-start(bf16[10,768]{1,0:T(8,128)(2,1)S(1)} %pad_maximum_fusion.5), channel_id=1, source_target_pairs={{0,1},{1,0},{2,3},{3,2},{4,5},{5,4},{6,7},{7,6},{8,9},{9,8},{10,11... | collective-permute-start | bytes 46088 | tf_op jit(solution)/shard_map/ppermute | solution.py:365
  22.8 0.6 copy-start.12
  23.4 0.6 copy-start.14
  27.3 4.6 %copy-start.18 = (bf16[32,8,768]{2,1,0:T(8,128)(2,1)}, bf16[32,8,768]{2,1,0:T(8,128)(2,1)S(1)}, u32[]{:S(2)}) copy-start(bf16[32,8,768]{2,1,0:T(8,128)(2,1)S(1)} %all-to-all-done.1) | copy-start | bytes 1179652
  27.3 16.3 %all-to-all-start = ((bf16[32,8,768]{2,1,0:T(8,128)(2,1)}), bf16[32,8,768]{2,1,0:T(8,128)(2,1)S(1)}, u32[]{:S(2)}, u32[]{:S(2)}) async-start(bf16[32,8,768]{2,1,0:T(8,128)(2,1)} %bitcast.57), calls=%async_computation | async-start | bytes 786432 | tf_op jit(solution)/shard_map/all_to_all | solution.py:378
  34.9 25.9 %collective-permute-start.6 = (bf16[768,256]{1,0:T(8,128)(2,1)}, bf16[768,256]{1,0:T(8,128)(2,1)}, u32[]{:S(2)}, u32[]{:S(2)}) collective-permute-start(bf16[768,256]{1,0:T(8,128)(2,1)} %get-tuple-element.41.cot_ref), channel_id=1, source_target_pairs={{0,16},{16,0},{1,17},{17,1},{2,18},{18,2},{3,19},{19,3},{4,20},{20... | collective-permute-start | bytes 1179656 | tf_op jit(solution)/shard_map/ppermute | solution.py:475
  43.6 0.7 copy-start.20
  44.3 16.5 %copy-start.8 = (bf16[768,256]{1,0:T(8,128)(2,1)S(1)}, bf16[768,256]{1,0:T(8,128)(2,1)}, u32[]{:S(2)}) copy-start(bf16[768,256]{1,0:T(8,128)(2,1)} %get-tuple-element.41.cot_ref) | copy-start | bytes 1179652
  44.3 20.8 %copy-start = (bf16[768,768]{1,0:T(8,128)(2,1)S(1)}, bf16[768,768]{1,0:T(8,128)(2,1)}, u32[]{:S(2)}) copy-start(bf16[768,768]{1,0:T(8,128)(2,1)} %refs_1_.5) | copy-start | bytes 3538948
  44.3 26.0 %copy-start.7 = (bf16[32,768]{1,0:T(8,128)(2,1)S(1)}, bf16[32,768]{1,0:T(8,128)(2,1)}, u32[]{:S(2)}) copy-start(bf16[32,768]{1,0:T(8,128)(2,1)} %copy-done.6) | copy-start | bytes 147460
  44.3 26.0 %copy-start.13 = (bf16[10,768]{1,0:T(8,128)(2,1)S(1)}, bf16[10,768]{1,0:T(8,128)(2,1)}, u32[]{:S(2)}) copy-start(bf16[10,768]{1,0:T(8,128)(2,1)} %copy-done.12) | copy-start | bytes 46084
  44.3 26.0 %copy-start.15 = (bf16[10,768]{1,0:T(8,128)(2,1)S(1)}, bf16[10,768]{1,0:T(8,128)(2,1)}, u32[]{:S(2)}) copy-start(bf16[10,768]{1,0:T(8,128)(2,1)} %copy-done.14) | copy-start | bytes 46084
  44.3 26.0 %copy-start.16 = (f32[1,768]{1,0:T(1,128)S(1)}, f32[1,768]{1,0:T(1,128)}, u32[]{:S(2)}) copy-start(f32[1,768]{1,0:T(1,128)} %reshape.93.gain_ref) | copy-start | bytes 9220
  44.4 26.0 %copy-start.17 = (s32[1,1,256]{2,1,0:T(1,128)S(1)}, s32[1,1,256]{2,1,0:T(1,128)}, u32[]{:S(2)}) copy-start(s32[1,1,256]{2,1,0:T(1,128)} %param.14) | copy-start | bytes 3076
  53.4 17.0 %copy-start.1 = (bf16[8,32,768]{2,1,0:T(8,128)(2,1)S(1)}, bf16[8,32,768]{2,1,0:T(8,128)(2,1)}, u32[]{:S(2)}) copy-start(bf16[8,32,768]{2,1,0:T(8,128)(2,1)} %field_ref.5) | copy-start | bytes 1179652
  53.4 17.0 %copy-start.2 = (bf16[8,32,768]{2,1,0:T(8,128)(2,1)S(1)}, bf16[8,32,768]{2,1,0:T(8,128)(2,1)}, u32[]{:S(2)}) copy-start(bf16[8,32,768]{2,1,0:T(8,128)(2,1)} %param.15) | copy-start | bytes 1179652
  53.4 17.0 %copy-start.3 = (bf16[256,768]{1,0:T(8,128)(2,1)S(1)}, bf16[256,768]{1,0:T(8,128)(2,1)}, u32[]{:S(2)}) copy-start(bf16[256,768]{1,0:T(8,128)(2,1)} %get-tuple-element.37.h_ref) | copy-start | bytes 1179652
  53.4 6.7 %collective-permute-start.7 = (bf16[384,256]{1,0:T(8,128)(2,1)}, bf16[384,256]{1,0:T(8,128)(2,1)S(1)}, u32[]{:S(2)}, u32[]{:S(2)}) collective-permute-start(bf16[384,256]{1,0:T(8,128)(2,1)} %get-tuple-element.42), channel_id=1, source_target_pairs={{0,16},{16,0},{1,17},{17,1},{2,18},{18,2},{3,19},{19,3},{4,20},{20... | collective-permute-start | bytes 589832 | tf_op jit(solution)/shard_map/ppermute | solution.py:399
  54.5 15.9 %all-to-all-start.2 = ((bf16[32,8,768]{2,1,0:T(8,128)(2,1)}), bf16[32,8,768]{2,1,0:T(8,128)(2,1)S(1)}, u32[]{:S(2)}, u32[]{:S(2)}) async-start(bf16[32,8,768]{2,1,0:T(8,128)(2,1)} %bitcast.54), calls=%async_computation.2 | async-start | bytes 786432 | tf_op jit(solution)/shard_map/all_to_all | solution.py:378
  60.1 0.7 copy-start.9
  60.8 1.0 %copy-start.4 = (bf16[768,256]{1,0:T(8,128)(2,1)S(1)}, bf16[768,256]{1,0:T(8,128)(2,1)}, u32[]{:S(2)}) copy-start(bf16[768,256]{1,0:T(8,128)(2,1)} %get-tuple-element.35.refs_0_.att_ref) | copy-start | bytes 1179652
  61.8 0.9 copy-start.10
  65.2 2.5 %collective-permute-start.8 = (bf16[8,48,384]{2,1,0:T(8,128)(2,1)}, bf16[8,48,384]{2,1,0:T(8,128)(2,1)}, u32[]{:S(2)}, u32[]{:S(2)}) collective-permute-start(bf16[8,48,384]{2,1,0:T(8,128)(2,1)} %get-tuple-element.44), channel_id=1, source_target_pairs={{0,1},{1,0},{2,3},{3,2},{4,5},{5,4},{6,7},{7,6},{8,9},{9,8},{10,11... | collective-permute-start | bytes 884744 | tf_op jit(solution)/shard_map/ppermute | solution.py:405
  65.2 1.0 %copy-start.5 = (bf16[768,256]{1,0:T(8,128)(2,1)S(1)}, bf16[768,256]{1,0:T(8,128)(2,1)}, u32[]{:S(2)}) copy-start(bf16[768,256]{1,0:T(8,128)(2,1)} %get-tuple-element.35.refs_0_.att_ref) | copy-start | bytes 1179652
  68.7 24.5 %copy-start.11 = (f32[3,3,768]{2,1,0:T(4,128)S(1)}, f32[3,3,768]{2,1,0:T(4,128)}, u32[]{:S(2)}) copy-start(f32[3,3,768]{2,1,0:T(4,128)} %taps_ref.3) | copy-start | bytes 82948
  68.8 8.6 %collective-permute-start.9 = (bf16[4,48,384]{2,1,0:T(8,128)(2,1)S(1)}, bf16[4,48,384]{2,1,0:T(8,128)(2,1)S(1)}, u32[]{:S(2)}, u32[]{:S(2)}) collective-permute-start(bf16[4,48,384]{2,1,0:T(8,128)(2,1)S(1)} %dynamic-slice_bitcast_fusion), channel_id=1, source_target_pairs={{0,2},{1,3},{2,0},{3,1},{4,6},{5,7},{6,4},{7,5},{8,10},{9,11},{10,... | collective-permute-start | bytes 442376 | tf_op jit(solution)/shard_map/ppermute | solution.py:408
  72.3 4.7 %collective-permute-start.3 = (bf16[64,768]{1,0:T(8,128)(2,1)S(1)}, bf16[64,768]{1,0:T(8,128)(2,1)S(1)}, u32[]{:S(2)}, u32[]{:S(2)}) collective-permute-start(bf16[64,768]{1,0:T(8,128)(2,1)S(1)} %get-tuple-element.39), channel_id=1, source_target_pairs={{0,16},{16,0},{1,17},{17,1},{2,18},{18,2},{3,19},{19,3},{4,20},{20... | collective-permute-start | bytes 294920 | tf_op jit(solution)/shard_map/ppermute | solution.py:520
  73.4 18.0 %all-to-all-start.3 = ((bf16[32,8,768]{2,1,0:T(8,128)(2,1)}), bf16[32,8,768]{2,1,0:T(8,128)(2,1)S(1)}, u32[]{:S(2)}, u32[]{:S(2)}) async-start(bf16[32,8,768]{2,1,0:T(8,128)(2,1)} %bitcast.18), calls=%async_computation.3 | async-start | bytes 786432 | tf_op jit(solution)/shard_map/all_to_all | solution.py:378
  77.2 1.3 %collective-permute-start.4 = (bf16[42,768]{1,0:T(8,128)(2,1)S(1)}, bf16[42,768]{1,0:T(8,128)(2,1)S(1)}, u32[]{:S(2)}, u32[]{:S(2)}) collective-permute-start(bf16[42,768]{1,0:T(8,128)(2,1)S(1)} %concatenate.30), channel_id=1, source_target_pairs={{0,1},{1,0},{2,3},{3,2},{4,5},{5,4},{6,7},{7,6},{8,9},{9,8},{10,11... | collective-permute-start | bytes 193544 | tf_op jit(solution)/shard_map/ppermute | solution.py:365
  78.6 5.3 %collective-permute-start.5 = (f32[16,768]{1,0:T(8,128)S(1)}, f32[16,768]{1,0:T(8,128)S(1)}, u32[]{:S(2)}, u32[]{:S(2)}) collective-permute-start(f32[16,768]{1,0:T(8,128)S(1)} %add_add_fusion), channel_id=1, source_target_pairs={{0,2},{1,3},{2,0},{3,1},{4,6},{5,7},{6,4},{7,5},{8,10},{9,11},{10,... | collective-permute-start | bytes 147464 | tf_op jit(solution)/shard_map/ppermute | solution.py:531
  83.9 6.0 %collective-permute-start.10 = (bf16[160,384]{1,0:T(8,128)(2,1)S(1)}, bf16[160,384]{1,0:T(8,128)(2,1)S(1)}, u32[]{:S(2)}, u32[]{:S(2)}) collective-permute-start(bf16[160,384]{1,0:T(8,128)(2,1)S(1)} %pad_maximum_fusion.1), channel_id=1, source_target_pairs={{0,4},{1,5},{2,6},{3,7},{4,0},{5,1},{6,2},{7,3},{8,12},{9,13},{10,... | collective-permute-start | bytes 368648 | tf_op jit(solution)/shard_map/ppermute | solution.py:542
  85.3 6.1 %collective-permute-start.11 = (bf16[10,768]{1,0:T(8,128)(2,1)S(1)}, bf16[10,768]{1,0:T(8,128)(2,1)S(1)}, u32[]{:S(2)}, u32[]{:S(2)}) collective-permute-start(bf16[10,768]{1,0:T(8,128)(2,1)S(1)} %pad_maximum_fusion.7), channel_id=1, source_target_pairs={{0,15},{1,2},{2,1},{3,4},{4,3},{5,6},{6,5},{7,8},{8,7},{9,10},{10,... | collective-permute-start | bytes 46088 | tf_op jit(solution)/shard_map/ppermute | solution.py:367
  91.5 5.4 %collective-permute-start.12 = (bf16[112,384]{1,0:T(8,128)(2,1)S(1)}, bf16[112,384]{1,0:T(8,128)(2,1)S(1)}, u32[]{:S(2)}, u32[]{:S(2)}) collective-permute-start(bf16[112,384]{1,0:T(8,128)(2,1)S(1)} %pad_maximum_fusion.2), channel_id=1, source_target_pairs={{0,8},{1,9},{2,10},{3,11},{4,12},{5,13},{6,14},{7,15},{8,0},{9,1},... | collective-permute-start | bytes 258056 | tf_op jit(solution)/shard_map/ppermute | solution.py:542

commit v7 on v6

--- a/solution.py
+++ b/solution.py
@@ -529,6 +529,7 @@
         beside = (*beside, even, odd)
         sums = sums + one_term(met)
         sums = sums + lax.ppermute(sums, "lon", swap_pairs(lon_count, 2))
+        sums = sums[:10]
         kept, met = project
         bit = 4
         while bit < lon_count:

time: 98.4 us -> 97.6 us (level)
  transfers between devices with their start and end apart: 17 -> 17, of which waited for: 10 -> 10; matrix products, arithmetic and copies ran while one was open for 5% -> 5% of each run, Pallas kernels for 24% -> 25%
where the time goes in v7:
time: 97.6 us; the launch traced here: 96.8 us
  starting transfers between devices  32.4 us (33%)
  Pallas kernels  26.7 us (27%)
  waiting for transfers between devices  26.5 us (27%)
  local copies, waits for them, and re-layouts  7.58 us (8%)
  other arithmetic  2.56 us (3%)
  between operations  1.06 us (1%)
    pallas_call x9, Pallas kernels, call(): pl.pallas_call(kernel, name=name, grid=(1,), out_shape=list(out_shape), i...  17.8 us
    all_to_all x4, starting transfers between devices, exchange(): lax.all_to_all(sent, AXES, split_axis=0, concat_axis=0, tiled=True)  13.8 us
    pallas_call x1, Pallas kernels, body(): pl.pallas_call(lambda *refs: attention_kernel(slots, blocks, UNROLL, *ref...  8.97 us
    all_to_all x4, waiting for transfers between devices, exchange(): lax.all_to_all(sent, AXES, split_axis=0, concat_axis=0, tiled=True)  7.22 us
    ppermute x2, waiting for transfers between devices, lon_rims(): met_odd = lax.ppermute(column(1, jnp.logical_not(even)), 'lon', odd_pairs)  6.83 us
    ppermute x2, starting transfers between devices, lon_rims(): met_odd = lax.ppermute(column(1, jnp.logical_not(even)), 'lon', odd_pairs)  6.18 us
    unnamed x43, local copies, waits for them, and re-layouts  5.28 us
    ppermute x2, waiting for transfers between devices, body(): lax.ppermute(jnp.concatenate([high_low, sent], axis=0), 'lon', swap_pairs...  4.16 us
  transfers between devices with their start and end apart: 17, of which 10 were waited for; matrix products, arithmetic and copies ran while one was open for 5% of the time, Pallas kernels for 25%

profile of v7, /device:TPU:0, one launch (start us, length us, event | category | flops | bytes accessed | tf_op | source)
XLA Modules:
  0.0 96.8 jit_solution(5187848539880244152)
XLA Ops:
  0.6 2.3 %start.1 = (bf16[256,768]{1,0:T(8,128)(2,1)}, bf16[32,768]{1,0:T(8,128)(2,1)}, bf16[2,8,768]{2,1,0:T(8,128)(2,1)}) custom-call(s32[1,256]{1,0:T(1,128)} %bitcast.44, bf16[256,768]{1,0:T(8,128)(2,1)} %bitcast.40, bf16[8,32,768]{2,1,0:T(8,128)(2,1)} %field_ref.5), custom_call_target="tpu_custom_call" | custom-call | bytes 1254400 | tf_op jit(solution)/shard_map/start/pallas_call | solution.py:41
  2.9 2.9 %collective-permute-start = (bf16[32,768]{1,0:T(8,128)(2,1)}, bf16[32,768]{1,0:T(8,128)(2,1)S(1)}, u32[]{:S(2)}, u32[]{:S(2)}) collective-permute-start(bf16[32,768]{1,0:T(8,128)(2,1)} %get-tuple-element.29), channel_id=1, source_target_pairs={{0,16},{16,0},{1,17},{17,1},{2,18},{18,2},{3,19},{19,3},{4,20},{20... | collective-permute-start | bytes 147464 | tf_op jit(solution)/shard_map/ppermute | solution.py:466
  5.8 4.9 %all-to-all-start.1 = ((bf16[32,8,768]{2,1,0:T(8,128)(2,1)}), bf16[32,8,768]{2,1,0:T(8,128)(2,1)S(1)}, u32[]{:S(2)}, u32[]{:S(2)}) async-start(bf16[32,8,768]{2,1,0:T(8,128)(2,1)} %bitcast.55), calls=%async_computation.1 | async-start | bytes 786432 | tf_op jit(solution)/shard_map/all_to_all | solution.py:378
  10.8 0.7 slice_bitcast_fusion.2
  11.5 0.0 collective-permute-done.before_ref.after_ref
  11.6 0.3 collective-permute-start.1
  11.9 4.5 %collective-permute-start.2 = (bf16[10,768]{1,0:T(8,128)(2,1)S(1)}, bf16[10,768]{1,0:T(8,128)(2,1)S(1)}, u32[]{:S(2)}, u32[]{:S(2)}) collective-permute-start(bf16[10,768]{1,0:T(8,128)(2,1)S(1)} %pad_maximum_fusion.6), channel_id=1, source_target_pairs={{0,15},{1,2},{2,1},{3,4},{4,3},{5,6},{6,5},{7,8},{8,7},{9,10},{10,... | collective-permute-start | bytes 46088 | tf_op jit(solution)/shard_map/ppermute | solution.py:367
  16.4 1.3 %reshape.93.gain_ref = f32[1,768]{1,0:T(1,128)} reshape(f32[768]{0:T(1024)} %param.10) | data formatting | bytes 6144 | tf_op jit(solution)/shard_map/reshape | solution.py:448
  17.7 0.0 collective-permute-done.1.even_ref
  17.7 5.1 %collective-permute-done.2.odd_ref = bf16[10,768]{1,0:T(8,128)(2,1)S(1)} collective-permute-done((bf16[10,768]{1,0:T(8,128)(2,1)S(1)}, bf16[10,768]{1,0:T(8,128)(2,1)S(1)}, u32[]{:S(2)}, u32[]{:S(2)}) %collective-permute-start.2) | collective-permute-done | bytes 15392 | tf_op jit(solution)/shard_map/ppermute | solution.py:367
  22.8 0.6 copy-done.14
  23.4 3.3 %convolve_normalize_pack.1 = (bf16[256,768]{1,0:T(8,128)(2,1)}, bf16[256,768]{1,0:T(8,128)(2,1)}) custom-call(s32[1,256]{1,0:T(1,128)} %bitcast.45, bf16[8,32,768]{2,1,0:T(8,128)(2,1)} %field_ref.5, bf16[32,768]{1,0:T(8,128)(2,1)} %copy-done.6, bf16[32,768]{1,0:T(8,128)(2,1)} %copy-done.6, bf16[10,768]{1,0:T(8,128)(2,1)} %copy-done.12, ...), custom_call_target="tpu_custom_call" | custom-call | bytes 1340416 | tf_op jit(solution)/shard_map/convolve_normalize_pack/pallas_call | solution.py:41
  26.7 0.0 all-to-all-done.1
  26.7 3.2 %all-to-all-start = ((bf16[32,8,768]{2,1,0:T(8,128)(2,1)}), bf16[32,8,768]{2,1,0:T(8,128)(2,1)S(1)}, u32[]{:S(2)}, u32[]{:S(2)}) async-start(bf16[32,8,768]{2,1,0:T(8,128)(2,1)} %bitcast.57), calls=%async_computation | async-start | bytes 786432 | tf_op jit(solution)/shard_map/all_to_all | solution.py:378
  29.9 0.0 copy-done.19
  29.9 0.3 copy.14
  30.2 1.2 %pad_maximum_fusion.refs_2_ = f32[24,64,128]{2,1,0:T(8,128)} fusion(f32[24,64,64]{2,1,0:T(8,128)S(1)} %bitcast.48), kind=kLoop, calls=%fused_computation | loop fusion | flops 196608 | bytes 1179648 | tf_op jit(solution)/shard_map/concatenate | solution.py:451
  31.3 3.0 %cotangent_products.1 = (bf16[768,256]{1,0:T(8,128)(2,1)}, bf16[768,256]{1,0:T(8,128)(2,1)}) custom-call(bf16[256,768]{1,0:T(8,128)(2,1)} %bitcast.49, bf16[768,768]{1,0:T(8,128)(2,1)} %refs_1_.5), custom_call_target="tpu_custom_call" | custom-call | bytes 2359296 | tf_op jit(solution)/shard_map/cotangent_products/pallas_call | solution.py:41
  34.3 1.8 %collective-permute-start.6 = (bf16[768,256]{1,0:T(8,128)(2,1)}, bf16[768,256]{1,0:T(8,128)(2,1)}, u32[]{:S(2)}, u32[]{:S(2)}) collective-permute-start(bf16[768,256]{1,0:T(8,128)(2,1)} %get-tuple-element.41.cot_ref), channel_id=1, source_target_pairs={{0,16},{16,0},{1,17},{17,1},{2,18},{18,2},{3,19},{19,3},{4,20},{20... | collective-permute-start | bytes 1179656 | tf_op jit(solution)/shard_map/ppermute | solution.py:475
  36.1 6.9 %all-to-all-done = bf16[32,8,768]{2,1,0:T(8,128)(2,1)S(1)} async-done(((bf16[32,8,768]{2,1,0:T(8,128)(2,1)}), bf16[32,8,768]{2,1,0:T(8,128)(2,1)S(1)}, u32[]{:S(2)}, u32[]{:S(2)}) %all-to-all-start) | async-done | bytes 393248 | tf_op jit(solution)/shard_map/all_to_all | solution.py:378
  43.0 0.7 copy-done.20
  43.7 0.0 copy-start.16
  43.8 0.0 copy-start.17
  43.8 9.0 %attention.1 = (bf16[256,768]{1,0:T(8,128)(2,1)}, bf16[768,256]{1,0:T(8,128)(2,1)}, bf16[384,256]{1,0:T(8,128)(2,1)}) custom-call(bf16[256,768]{1,0:T(8,128)(2,1)} %bitcast.56, bf16[768,2304]{1,0:T(8,128)(2,1)} %refs_1_.4, f32[24,64,128]{2,1,0:T(8,128)} %pad_maximum_fusion.refs_2_, bf16[768,256]{1,0:T(8,128)(2,1)} %get-tuple-element.33.refs_3_), custom_call_target="tpu_custom_call" | custom-call | flops 12000000000 | bytes 8000000 | tf_op jit(solution)/shard_map/attention/pallas_call | solution.py:486
  52.8 0.0 copy-start.1
  52.8 0.0 copy-start.2
  52.8 0.0 copy-start.3
  52.8 1.1 %collective-permute-start.7 = (bf16[384,256]{1,0:T(8,128)(2,1)}, bf16[384,256]{1,0:T(8,128)(2,1)S(1)}, u32[]{:S(2)}, u32[]{:S(2)}) collective-permute-start(bf16[384,256]{1,0:T(8,128)(2,1)} %get-tuple-element.42), channel_id=1, source_target_pairs={{0,16},{16,0},{1,17},{17,1},{2,18},{18,2},{3,19},{19,3},{4,20},{20... | collective-permute-start | bytes 589832 | tf_op jit(solution)/shard_map/ppermute | solution.py:399
  53.9 2.9 %all-to-all-start.2 = ((bf16[32,8,768]{2,1,0:T(8,128)(2,1)}), bf16[32,8,768]{2,1,0:T(8,128)(2,1)S(1)}, u32[]{:S(2)}, u32[]{:S(2)}) async-start(bf16[32,8,768]{2,1,0:T(8,128)(2,1)} %bitcast.54), calls=%async_computation.2 | async-start | bytes 786432 | tf_op jit(solution)/shard_map/all_to_all | solution.py:378
  56.8 2.7 %collective-permute-done.7.att_met_ref = bf16[384,256]{1,0:T(8,128)(2,1)S(1)} collective-permute-done((bf16[384,256]{1,0:T(8,128)(2,1)}, bf16[384,256]{1,0:T(8,128)(2,1)S(1)}, u32[]{:S(2)}, u32[]{:S(2)}) %collective-permute-start.7) | collective-permute-done | bytes 196640 | tf_op jit(solution)/shard_map/ppermute | solution.py:399
  59.5 0.7 copy-done.9
  60.2 0.0 collective-permute-done.6.cot_met_ref
  60.2 1.0 %copy-done.4 = bf16[768,256]{1,0:T(8,128)(2,1)S(1)} copy-done((bf16[768,256]{1,0:T(8,128)(2,1)S(1)}, bf16[768,256]{1,0:T(8,128)(2,1)}, u32[]{:S(2)}) %copy-start.4) | copy-done | bytes 393240
  61.2 0.9 copy-done.10
  62.1 2.4 %project_gradient.1 = (bf16[8,48,384]{2,1,0:T(8,128)(2,1)S(1)}, bf16[8,48,384]{2,1,0:T(8,128)(2,1)}) custom-call(bf16[768,256]{1,0:T(8,128)(2,1)S(1)} %copy-done.8, bf16[768,256]{1,0:T(8,128)(2,1)} %collective-permute-done.6.cot_met_ref, bf16[768,256]{1,0:T(8,128)(2,1)S(1)} %copy-done.4, bf16[384,256]{1,0:T(8,128)(2,1)S(1)} %copy-done.10), custom_call_target="tpu_custom_call" | custom-call | bytes 1966080 | tf_op jit(solution)/shard_map/project_gradient/pallas_call | solution.py:41
  64.6 0.0 collective-permute-start.8
  64.6 1.0 %copy-done.5 = bf16[768,256]{1,0:T(8,128)(2,1)S(1)} copy-done((bf16[768,256]{1,0:T(8,128)(2,1)S(1)}, bf16[768,256]{1,0:T(8,128)(2,1)}, u32[]{:S(2)}) %copy-start.5) | copy-done | bytes 393240
  65.6 1.5 %mix.1 = bf16[256,768]{1,0:T(8,128)(2,1)} custom-call(bf16[768,256]{1,0:T(8,128)(2,1)S(1)} %copy-done.5, bf16[768,768]{1,0:T(8,128)(2,1)S(1)} %copy-done), custom_call_target="tpu_custom_call" | custom-call | bytes 1966080 | tf_op jit(solution)/shard_map/mix/pallas_call | solution.py:41
  67.1 0.0 collective-permute-done.8
  67.1 1.0 %add_convert_fusion = bf16[8,48,384]{2,1,0:T(8,128)(2,1)S(1)} fusion(bf16[8,48,384]{2,1,0:T(8,128)(2,1)} %collective-permute-done.8, bf16[8,48,384]{2,1,0:T(8,128)(2,1)S(1)} %get-tuple-element.43), kind=kLoop, calls=%fused_computation.1 | loop fusion | flops 589824 | bytes 884736 | tf_op jit(solution)/shard_map/convert_element_type | solution.py:406
  68.1 0.0 copy-start.11
  68.2 1.3 %collective-permute-start.9 = (bf16[4,48,384]{2,1,0:T(8,128)(2,1)S(1)}, bf16[4,48,384]{2,1,0:T(8,128)(2,1)S(1)}, u32[]{:S(2)}, u32[]{:S(2)}) collective-permute-start(bf16[4,48,384]{2,1,0:T(8,128)(2,1)S(1)} %dynamic-slice_bitcast_fusion), channel_id=1, source_target_pairs={{0,2},{1,3},{2,0},{3,1},{4,6},{5,7},{6,4},{7,5},{8,10},{9,11},{10,... | collective-permute-start | bytes 442376 | tf_op jit(solution)/shard_map/ppermute | solution.py:408
  69.5 0.3 all-to-all-done.2
  69.8 1.9 %normalize_back.1 = (bf16[8,32,768]{2,1,0:T(8,128)(2,1)S(1)}, f32[16,768]{1,0:T(8,128)S(1)}, bf16[64,768]{1,0:T(8,128)(2,1)S(1)}, bf16[2,8,768]{2,1,0:T(8,128)(2,1)S(1)}) custom-call(s32[1,256]{1,0:T(1,128)S(1)} %bitcast.46, bf16[256,768]{1,0:T(8,128)(2,1)S(1)} %bitcast.42, bf16[256,768]{1,0:T(8,128)(2,1)S(1)} %copy-done.3, bf16[256,768]{1,0:T(8,128)(2,1)S(1)} %bitcast.41, ...), custom_call_target="tpu_custom_call" | custom-call | bytes 2271232 | tf_op jit(solution)/shard_map/normalize_back/pallas_call | solution.py:41
  71.7 1.1 %collective-permute-start.3 = (bf16[64,768]{1,0:T(8,128)(2,1)S(1)}, bf16[64,768]{1,0:T(8,128)(2,1)S(1)}, u32[]{:S(2)}, u32[]{:S(2)}) collective-permute-start(bf16[64,768]{1,0:T(8,128)(2,1)S(1)} %get-tuple-element.39), channel_id=1, source_target_pairs={{0,16},{16,0},{1,17},{17,1},{2,18},{18,2},{3,19},{19,3},{4,20},{20... | collective-permute-start | bytes 294920 | tf_op jit(solution)/shard_map/ppermute | solution.py:520
  72.8 2.8 %all-to-all-start.3 = ((bf16[32,8,768]{2,1,0:T(8,128)(2,1)}), bf16[32,8,768]{2,1,0:T(8,128)(2,1)S(1)}, u32[]{:S(2)}, u32[]{:S(2)}) async-start(bf16[32,8,768]{2,1,0:T(8,128)(2,1)} %bitcast.18), calls=%async_computation.3 | async-start | bytes 786432 | tf_op jit(solution)/shard_map/all_to_all | solution.py:378
  75.6 0.0 collective-permute-done.9
  75.6 0.1 fusion
  75.7 0.8 collective-permute-done.3
  76.5 0.2 concatenate.30
  76.7 0.1 collective-permute-start.4
  76.8 1.2 %collective-permute-done.4 = bf16[42,768]{1,0:T(8,128)(2,1)S(1)} collective-permute-done((bf16[42,768]{1,0:T(8,128)(2,1)S(1)}, bf16[42,768]{1,0:T(8,128)(2,1)S(1)}, u32[]{:S(2)}, u32[]{:S(2)}) %collective-permute-start.4) | collective-permute-done | bytes 64544 | tf_op jit(solution)/shard_map/ppermute | solution.py:365
  78.0 1.6 %collective-permute-start.5 = (f32[16,768]{1,0:T(8,128)S(1)}, f32[16,768]{1,0:T(8,128)S(1)}, u32[]{:S(2)}, u32[]{:S(2)}) collective-permute-start(f32[16,768]{1,0:T(8,128)S(1)} %add_add_fusion), channel_id=1, source_target_pairs={{0,2},{1,3},{2,0},{3,1},{4,6},{5,7},{6,4},{7,5},{8,10},{9,11},{10,... | collective-permute-start | bytes 147464 | tf_op jit(solution)/shard_map/ppermute | solution.py:531
  79.6 3.6 %collective-permute-done.5 = f32[16,768]{1,0:T(8,128)S(1)} collective-permute-done((f32[16,768]{1,0:T(8,128)S(1)}, f32[16,768]{1,0:T(8,128)S(1)}, u32[]{:S(2)}, u32[]{:S(2)}) %collective-permute-start.5) | collective-permute-done | bytes 49184 | tf_op jit(solution)/shard_map/ppermute | solution.py:531
  83.3 1.4 %collective-permute-start.10 = (bf16[136,384]{1,0:T(8,128)(2,1)S(1)}, bf16[136,384]{1,0:T(8,128)(2,1)S(1)}, u32[]{:S(2)}, u32[]{:S(2)}) collective-permute-start(bf16[136,384]{1,0:T(8,128)(2,1)S(1)} %pad_maximum_fusion.1), channel_id=1, source_target_pairs={{0,4},{1,5},{2,6},{3,7},{4,0},{5,1},{6,2},{7,3},{8,12},{9,13},{10,... | collective-permute-start | bytes 313352 | tf_op jit(solution)/shard_map/ppermute | solution.py:543
  84.8 1.7 %collective-permute-start.11 = (bf16[10,768]{1,0:T(8,128)(2,1)S(1)}, bf16[10,768]{1,0:T(8,128)(2,1)S(1)}, u32[]{:S(2)}, u32[]{:S(2)}) collective-permute-start(bf16[10,768]{1,0:T(8,128)(2,1)S(1)} %pad_maximum_fusion.7), channel_id=1, source_target_pairs={{0,15},{1,2},{2,1},{3,4},{4,3},{5,6},{6,5},{7,8},{8,7},{9,10},{10,... | collective-permute-start | bytes 46088 | tf_op jit(solution)/shard_map/ppermute | solution.py:367
  86.5 2.5 %collective-permute-done.10 = bf16[136,384]{1,0:T(8,128)(2,1)S(1)} collective-permute-done((bf16[136,384]{1,0:T(8,128)(2,1)S(1)}, bf16[136,384]{1,0:T(8,128)(2,1)S(1)}, u32[]{:S(2)}, u32[]{:S(2)}) %collective-permute-start.10) | collective-permute-done | bytes 104480 | tf_op jit(solution)/shard_map/ppermute | solution.py:543
  89.0 1.7 %collective-permute-done.11.odd_ref = bf16[10,768]{1,0:T(8,128)(2,1)S(1)} collective-permute-done((bf16[10,768]{1,0:T(8,128)(2,1)S(1)}, bf16[10,768]{1,0:T(8,128)(2,1)S(1)}, u32[]{:S(2)}, u32[]{:S(2)}) %collective-permute-start.11) | collective-permute-done | bytes 15392 | tf_op jit(solution)/shard_map/ppermute | solution.py:367
  90.8 0.0 all-to-all-done.3
  90.8 0.8 collective-permute-start.12
  91.7 1.0 %block_out.1 = bf16[256,768]{1,0:T(8,128)(2,1)} custom-call(s32[1,256]{1,0:T(1,128)S(1)} %bitcast.47, bf16[256,768]{1,0:T(8,128)(2,1)S(1)} %bitcast.43, bf16[256,768]{1,0:T(8,128)(2,1)S(1)} %copy-done.3), custom_call_target="tpu_custom_call" | custom-call | bytes 1180672 | tf_op jit(solution)/shard_map/block_out/pallas_call | solution.py:41
  92.7 1.7 %convolve_back.1 = bf16[8,32,768]{2,1,0:T(8,128)(2,1)} custom-call(bf16[8,32,768]{2,1,0:T(8,128)(2,1)S(1)} %get-tuple-element.47.field_ref, bf16[32,768]{1,0:T(8,128)(2,1)S(1)} %slice.126.before_ref.after_ref, bf16[32,768]{1,0:T(8,128)(2,1)S(1)} %slice.126.before_ref.after_ref, bf16[10,768]{1,0:T(8,128)(2,1)S(1)} %slice.127.even_ref, ...), custom_call_target="tpu_custom_call" | custom-call | bytes 943104 | tf_op jit(solution)/shard_map/convolve_back/pallas_call | solution.py:41
  94.4 1.7 %collective-permute-done.12 = bf16[88,384]{1,0:T(8,128)(2,1)S(1)} collective-permute-done((bf16[88,384]{1,0:T(8,128)(2,1)S(1)}, bf16[88,384]{1,0:T(8,128)(2,1)S(1)}, u32[]{:S(2)}, u32[]{:S(2)}) %collective-permute-start.12) | collective-permute-done | bytes 67616 | tf_op jit(solution)/shard_map/ppermute | solution.py:543
  96.2 0.7 finish.1
  (63 shorter events, 0.5 us)
Async XLA Ops:
  0.6 29.2 %copy-start.19 = (f32[24,64,64]{2,1,0:T(8,128)S(1)}, f32[24,64,64]{2,1,0:T(8,128)}, u32[]{:S(2)}) copy-start(f32[24,64,64]{2,1,0:T(8,128)} %param.13) | copy-start | bytes 1179652
  2.9 8.6 %collective-permute-start = (bf16[32,768]{1,0:T(8,128)(2,1)}, bf16[32,768]{1,0:T(8,128)(2,1)S(1)}, u32[]{:S(2)}, u32[]{:S(2)}) collective-permute-start(bf16[32,768]{1,0:T(8,128)(2,1)} %get-tuple-element.29), channel_id=1, source_target_pairs={{0,16},{16,0},{1,17},{17,1},{2,18},{18,2},{3,19},{19,3},{4,20},{20... | collective-permute-start | bytes 147464 | tf_op jit(solution)/shard_map/ppermute | solution.py:466
  5.8 20.8 %all-to-all-start.1 = ((bf16[32,8,768]{2,1,0:T(8,128)(2,1)}), bf16[32,8,768]{2,1,0:T(8,128)(2,1)S(1)}, u32[]{:S(2)}, u32[]{:S(2)}) async-start(bf16[32,8,768]{2,1,0:T(8,128)(2,1)} %bitcast.55), calls=%async_computation.1 | async-start | bytes 786432 | tf_op jit(solution)/shard_map/all_to_all | solution.py:378
  11.5 11.3 %copy-start.6 = (bf16[32,768]{1,0:T(8,128)(2,1)}, bf16[32,768]{1,0:T(8,128)(2,1)S(1)}, u32[]{:S(2)}) copy-start(bf16[32,768]{1,0:T(8,128)(2,1)S(1)} %collective-permute-done.before_ref.after_ref) | copy-start | bytes 147460
  11.6 6.1 %collective-permute-start.1 = (bf16[10,768]{1,0:T(8,128)(2,1)S(1)}, bf16[10,768]{1,0:T(8,128)(2,1)S(1)}, u32[]{:S(2)}, u32[]{:S(2)}) collective-permute-start(bf16[10,768]{1,0:T(8,128)(2,1)S(1)} %pad_maximum_fusion.5), channel_id=1, source_target_pairs={{0,1},{1,0},{2,3},{3,2},{4,5},{5,4},{6,7},{7,6},{8,9},{9,8},{10,11... | collective-permute-start | bytes 46088 | tf_op jit(solution)/shard_map/ppermute | solution.py:365
  11.9 10.9 %collective-permute-start.2 = (bf16[10,768]{1,0:T(8,128)(2,1)S(1)}, bf16[10,768]{1,0:T(8,128)(2,1)S(1)}, u32[]{:S(2)}, u32[]{:S(2)}) collective-permute-start(bf16[10,768]{1,0:T(8,128)(2,1)S(1)} %pad_maximum_fusion.6), channel_id=1, source_target_pairs={{0,15},{1,2},{2,1},{3,4},{4,3},{5,6},{6,5},{7,8},{8,7},{9,10},{10,... | collective-permute-start | bytes 46088 | tf_op jit(solution)/shard_map/ppermute | solution.py:367
  17.7 5.1 %copy-start.12 = (bf16[10,768]{1,0:T(8,128)(2,1)}, bf16[10,768]{1,0:T(8,128)(2,1)S(1)}, u32[]{:S(2)}) copy-start(bf16[10,768]{1,0:T(8,128)(2,1)S(1)} %collective-permute-done.1.even_ref) | copy-start | bytes 46084
  22.8 0.6 copy-start.14
  26.7 4.6 %copy-start.18 = (bf16[32,8,768]{2,1,0:T(8,128)(2,1)}, bf16[32,8,768]{2,1,0:T(8,128)(2,1)S(1)}, u32[]{:S(2)}) copy-start(bf16[32,8,768]{2,1,0:T(8,128)(2,1)S(1)} %all-to-all-done.1) | copy-start | bytes 1179652
  26.7 16.3 %all-to-all-start = ((bf16[32,8,768]{2,1,0:T(8,128)(2,1)}), bf16[32,8,768]{2,1,0:T(8,128)(2,1)S(1)}, u32[]{:S(2)}, u32[]{:S(2)}) async-start(bf16[32,8,768]{2,1,0:T(8,128)(2,1)} %bitcast.57), calls=%async_computation | async-start | bytes 786432 | tf_op jit(solution)/shard_map/all_to_all | solution.py:378
  34.3 25.9 %collective-permute-start.6 = (bf16[768,256]{1,0:T(8,128)(2,1)}, bf16[768,256]{1,0:T(8,128)(2,1)}, u32[]{:S(2)}, u32[]{:S(2)}) collective-permute-start(bf16[768,256]{1,0:T(8,128)(2,1)} %get-tuple-element.41.cot_ref), channel_id=1, source_target_pairs={{0,16},{16,0},{1,17},{17,1},{2,18},{18,2},{3,19},{19,3},{4,20},{20... | collective-permute-start | bytes 1179656 | tf_op jit(solution)/shard_map/ppermute | solution.py:475
  43.0 0.7 copy-start.20
  43.7 16.5 %copy-start.8 = (bf16[768,256]{1,0:T(8,128)(2,1)S(1)}, bf16[768,256]{1,0:T(8,128)(2,1)}, u32[]{:S(2)}) copy-start(bf16[768,256]{1,0:T(8,128)(2,1)} %get-tuple-element.41.cot_ref) | copy-start | bytes 1179652
  43.7 20.8 %copy-start = (bf16[768,768]{1,0:T(8,128)(2,1)S(1)}, bf16[768,768]{1,0:T(8,128)(2,1)}, u32[]{:S(2)}) copy-start(bf16[768,768]{1,0:T(8,128)(2,1)} %refs_1_.5) | copy-start | bytes 3538948
  43.7 26.0 %copy-start.7 = (bf16[32,768]{1,0:T(8,128)(2,1)S(1)}, bf16[32,768]{1,0:T(8,128)(2,1)}, u32[]{:S(2)}) copy-start(bf16[32,768]{1,0:T(8,128)(2,1)} %copy-done.6) | copy-start | bytes 147460
  43.7 26.0 %copy-start.13 = (bf16[10,768]{1,0:T(8,128)(2,1)S(1)}, bf16[10,768]{1,0:T(8,128)(2,1)}, u32[]{:S(2)}) copy-start(bf16[10,768]{1,0:T(8,128)(2,1)} %copy-done.12) | copy-start | bytes 46084
  43.7 26.0 %copy-start.15 = (bf16[10,768]{1,0:T(8,128)(2,1)S(1)}, bf16[10,768]{1,0:T(8,128)(2,1)}, u32[]{:S(2)}) copy-start(bf16[10,768]{1,0:T(8,128)(2,1)} %copy-done.14) | copy-start | bytes 46084
  43.7 26.0 %copy-start.16 = (f32[1,768]{1,0:T(1,128)S(1)}, f32[1,768]{1,0:T(1,128)}, u32[]{:S(2)}) copy-start(f32[1,768]{1,0:T(1,128)} %reshape.93.gain_ref) | copy-start | bytes 9220
  43.8 26.0 %copy-start.17 = (s32[1,1,256]{2,1,0:T(1,128)S(1)}, s32[1,1,256]{2,1,0:T(1,128)}, u32[]{:S(2)}) copy-start(s32[1,1,256]{2,1,0:T(1,128)} %param.14) | copy-start | bytes 3076
  52.8 17.0 %copy-start.1 = (bf16[8,32,768]{2,1,0:T(8,128)(2,1)S(1)}, bf16[8,32,768]{2,1,0:T(8,128)(2,1)}, u32[]{:S(2)}) copy-start(bf16[8,32,768]{2,1,0:T(8,128)(2,1)} %field_ref.5) | copy-start | bytes 1179652
  52.8 17.0 %copy-start.2 = (bf16[8,32,768]{2,1,0:T(8,128)(2,1)S(1)}, bf16[8,32,768]{2,1,0:T(8,128)(2,1)}, u32[]{:S(2)}) copy-start(bf16[8,32,768]{2,1,0:T(8,128)(2,1)} %param.15) | copy-start | bytes 1179652
  52.8 17.0 %copy-start.3 = (bf16[256,768]{1,0:T(8,128)(2,1)S(1)}, bf16[256,768]{1,0:T(8,128)(2,1)}, u32[]{:S(2)}) copy-start(bf16[256,768]{1,0:T(8,128)(2,1)} %get-tuple-element.37.h_ref) | copy-start | bytes 1179652
  52.8 6.7 %collective-permute-start.7 = (bf16[384,256]{1,0:T(8,128)(2,1)}, bf16[384,256]{1,0:T(8,128)(2,1)S(1)}, u32[]{:S(2)}, u32[]{:S(2)}) collective-permute-start(bf16[384,256]{1,0:T(8,128)(2,1)} %get-tuple-element.42), channel_id=1, source_target_pairs={{0,16},{16,0},{1,17},{17,1},{2,18},{18,2},{3,19},{19,3},{4,20},{20... | collective-permute-start | bytes 589832 | tf_op jit(solution)/shard_map/ppermute | solution.py:399
  53.9 15.9 %all-to-all-start.2 = ((bf16[32,8,768]{2,1,0:T(8,128)(2,1)}), bf16[32,8,768]{2,1,0:T(8,128)(2,1)S(1)}, u32[]{:S(2)}, u32[]{:S(2)}) async-start(bf16[32,8,768]{2,1,0:T(8,128)(2,1)} %bitcast.54), calls=%async_computation.2 | async-start | bytes 786432 | tf_op jit(solution)/shard_map/all_to_all | solution.py:378
  59.5 0.7 copy-start.9
  60.2 1.0 %copy-start.4 = (bf16[768,256]{1,0:T(8,128)(2,1)S(1)}, bf16[768,256]{1,0:T(8,128)(2,1)}, u32[]{:S(2)}) copy-start(bf16[768,256]{1,0:T(8,128)(2,1)} %get-tuple-element.35.refs_0_.att_ref) | copy-start | bytes 1179652
  61.2 0.9 copy-start.10
  64.6 2.5 %collective-permute-start.8 = (bf16[8,48,384]{2,1,0:T(8,128)(2,1)}, bf16[8,48,384]{2,1,0:T(8,128)(2,1)}, u32[]{:S(2)}, u32[]{:S(2)}) collective-permute-start(bf16[8,48,384]{2,1,0:T(8,128)(2,1)} %get-tuple-element.44), channel_id=1, source_target_pairs={{0,1},{1,0},{2,3},{3,2},{4,5},{5,4},{6,7},{7,6},{8,9},{9,8},{10,11... | collective-permute-start | bytes 884744 | tf_op jit(solution)/shard_map/ppermute | solution.py:405
  64.6 1.0 %copy-start.5 = (bf16[768,256]{1,0:T(8,128)(2,1)S(1)}, bf16[768,256]{1,0:T(8,128)(2,1)}, u32[]{:S(2)}) copy-start(bf16[768,256]{1,0:T(8,128)(2,1)} %get-tuple-element.35.refs_0_.att_ref) | copy-start | bytes 1179652
  68.1 24.6 %copy-start.11 = (f32[3,3,768]{2,1,0:T(4,128)S(1)}, f32[3,3,768]{2,1,0:T(4,128)}, u32[]{:S(2)}) copy-start(f32[3,3,768]{2,1,0:T(4,128)} %taps_ref.3) | copy-start | bytes 82948
  68.2 7.4 %collective-permute-start.9 = (bf16[4,48,384]{2,1,0:T(8,128)(2,1)S(1)}, bf16[4,48,384]{2,1,0:T(8,128)(2,1)S(1)}, u32[]{:S(2)}, u32[]{:S(2)}) collective-permute-start(bf16[4,48,384]{2,1,0:T(8,128)(2,1)S(1)} %dynamic-slice_bitcast_fusion), channel_id=1, source_target_pairs={{0,2},{1,3},{2,0},{3,1},{4,6},{5,7},{6,4},{7,5},{8,10},{9,11},{10,... | collective-permute-start | bytes 442376 | tf_op jit(solution)/shard_map/ppermute | solution.py:408
  71.7 4.7 %collective-permute-start.3 = (bf16[64,768]{1,0:T(8,128)(2,1)S(1)}, bf16[64,768]{1,0:T(8,128)(2,1)S(1)}, u32[]{:S(2)}, u32[]{:S(2)}) collective-permute-start(bf16[64,768]{1,0:T(8,128)(2,1)S(1)} %get-tuple-element.39), channel_id=1, source_target_pairs={{0,16},{16,0},{1,17},{17,1},{2,18},{18,2},{3,19},{19,3},{4,20},{20... | collective-permute-start | bytes 294920 | tf_op jit(solution)/shard_map/ppermute | solution.py:520
  72.8 18.0 %all-to-all-start.3 = ((bf16[32,8,768]{2,1,0:T(8,128)(2,1)}), bf16[32,8,768]{2,1,0:T(8,128)(2,1)S(1)}, u32[]{:S(2)}, u32[]{:S(2)}) async-start(bf16[32,8,768]{2,1,0:T(8,128)(2,1)} %bitcast.18), calls=%async_computation.3 | async-start | bytes 786432 | tf_op jit(solution)/shard_map/all_to_all | solution.py:378
  76.7 1.3 %collective-permute-start.4 = (bf16[42,768]{1,0:T(8,128)(2,1)S(1)}, bf16[42,768]{1,0:T(8,128)(2,1)S(1)}, u32[]{:S(2)}, u32[]{:S(2)}) collective-permute-start(bf16[42,768]{1,0:T(8,128)(2,1)S(1)} %concatenate.30), channel_id=1, source_target_pairs={{0,1},{1,0},{2,3},{3,2},{4,5},{5,4},{6,7},{7,6},{8,9},{9,8},{10,11... | collective-permute-start | bytes 193544 | tf_op jit(solution)/shard_map/ppermute | solution.py:365
  78.0 5.3 %collective-permute-start.5 = (f32[16,768]{1,0:T(8,128)S(1)}, f32[16,768]{1,0:T(8,128)S(1)}, u32[]{:S(2)}, u32[]{:S(2)}) collective-permute-start(f32[16,768]{1,0:T(8,128)S(1)} %add_add_fusion), channel_id=1, source_target_pairs={{0,2},{1,3},{2,0},{3,1},{4,6},{5,7},{6,4},{7,5},{8,10},{9,11},{10,... | collective-permute-start | bytes 147464 | tf_op jit(solution)/shard_map/ppermute | solution.py:531
  83.3 5.6 %collective-permute-start.10 = (bf16[136,384]{1,0:T(8,128)(2,1)S(1)}, bf16[136,384]{1,0:T(8,128)(2,1)S(1)}, u32[]{:S(2)}, u32[]{:S(2)}) collective-permute-start(bf16[136,384]{1,0:T(8,128)(2,1)S(1)} %pad_maximum_fusion.1), channel_id=1, source_target_pairs={{0,4},{1,5},{2,6},{3,7},{4,0},{5,1},{6,2},{7,3},{8,12},{9,13},{10,... | collective-permute-start | bytes 313352 | tf_op jit(solution)/shard_map/ppermute | solution.py:543
  84.8 6.0 %collective-permute-start.11 = (bf16[10,768]{1,0:T(8,128)(2,1)S(1)}, bf16[10,768]{1,0:T(8,128)(2,1)S(1)}, u32[]{:S(2)}, u32[]{:S(2)}) collective-permute-start(bf16[10,768]{1,0:T(8,128)(2,1)S(1)} %pad_maximum_fusion.7), channel_id=1, source_target_pairs={{0,15},{1,2},{2,1},{3,4},{4,3},{5,6},{6,5},{7,8},{8,7},{9,10},{10,... | collective-permute-start | bytes 46088 | tf_op jit(solution)/shard_map/ppermute | solution.py:367
  90.8 5.3 %collective-permute-start.12 = (bf16[88,384]{1,0:T(8,128)(2,1)S(1)}, bf16[88,384]{1,0:T(8,128)(2,1)S(1)}, u32[]{:S(2)}, u32[]{:S(2)}) collective-permute-start(bf16[88,384]{1,0:T(8,128)(2,1)S(1)} %pad_maximum_fusion.2), channel_id=1, source_target_pairs={{0,8},{1,9},{2,10},{3,11},{4,12},{5,13},{6,14},{7,15},{8,0},{9,1},... | collective-permute-start | bytes 202760 | tf_op jit(solution)/shard_map/ppermute | solution.py:543
